TPU v7x, 512 devices: a whole 4x4x16 slice. The times are simulated.
512 devices in a mesh: pb: 16 (over x, z_hi, core), dev: 32 (over y, z_lo).
Axes of the slice: x: 4, y: 4, z: 16 (z_hi: 2, z_lo: 8; z = z_hi * 8 + z_lo), core: 2. Of those that a mesh axis runs over, the one named last changes fastest.
Arguments:
- queries: bfloat16 [16384, 128], P(('dev', 'pb')), may hold values from -0.75 to 0.75
- documents: bfloat16 [131072, 128], P(('pb', 'dev')), may hold values from -0.75 to 0.75
- lengths: int32 [1024], P(('pb', 'dev')), may hold values from 1 to 128
- normalizers: float32 [1024, 16384], P('pb', 'dev'), may hold values from 4.5 to 7.5
- probs: float32 [512, 1024], P('dev', 'pb'), may hold values from 0.01 to 0.2
- positives: int32 [512], P('dev'), may hold values from 0 to 1023
Outputs:
- query_grad: float32 [16384, 128], P(('dev', 'pb'))
- doc_grad: float32 [131072, 128], P(('pb', 'dev'))
Inputs may be any that keep to these rules, and one draw needn't show every extreme that they name: `lengths`: slots of a document at positions of its length or beyond are padding. `positives`: index of the query's paired document among all 1024.
All inputs are finite; a program needn't handle non-finite values.
Results may differ from a plain program's by a relative error of at most 0.00082.
Values may be sent and summed in bfloat16 or wider, within the bound.
No kernel may reach another device: no remote copies, remote signals or barrier semaphores. Data moves between devices by JAX's collectives and lax.ppermute only.
A program may use at most 64 MiB of HBM per device.

v0:
```python
import jax
import jax.numpy as jnp
from jax import lax
from jax.sharding import Mesh
from jax.sharding import PartitionSpec as P

PB = ("pb_0", "pb_1", "pb_2")
DEV_PB = ("dev", "pb_0", "pb_1", "pb_2")
PB_DEV = ("pb_0", "pb_1", "pb_2", "dev")


sharpness = 10.0


def from_everyone(x, axis):
    copies = jnp.broadcast_to(x, (lax.axis_size(axis), *x.shape))
    return lax.all_to_all(copies, axis, split_axis=0, concat_axis=0, tiled=True)


def in_order(tiles, dim):
    lengths = list(tiles.shape[1:])
    lengths[dim] *= tiles.shape[0]
    return jnp.moveaxis(tiles, 0, dim).reshape(lengths)


def gathered_copies(x, axis, dim):
    tiles = from_everyone(x, axis)
    return in_order(tiles, dim)


def cut_along(x, dim, devices):
    before, after = (x.shape[:dim], x.shape[dim + 1 :])
    return jnp.moveaxis(x.reshape(*before, devices, -1, *after), dim, 0)


def summed_rows(x, chips, core, dim):
    sizes = (lax.axis_size(chips), lax.axis_size(core))
    tiles = cut_along(x, dim, sizes[0] * sizes[1])
    inside = tiles.shape[1:]
    tiles = tiles.reshape(*sizes, *inside).swapaxes(0, 1).reshape(-1, *inside)
    tiles = lax.psum_scatter(tiles, core, scatter_dimension=0, tiled=True)
    return lax.psum_scatter(tiles, chips, scatter_dimension=0, tiled=True)[0]


def interact(query_rows, z_rows, p_cols, positive_ids, doc_rows, doc_lengths, first_doc):
    query_total = query_rows.shape[0]
    query_count = p_cols.shape[0]
    query_length = query_total // query_count
    doc_count = doc_lengths.shape[0]
    doc_length = doc_rows.shape[0] // doc_count
    scores = lax.dot_general(
        query_rows, doc_rows, (((1,), (1,)), ((), ())), preferred_element_type=jnp.float32
    )
    scores = scores.reshape(query_count, query_length, doc_count, doc_length)
    doc_ids = first_doc + jnp.arange(doc_count, dtype=jnp.int32)
    signal = p_cols - (positive_ids[:, None] == doc_ids[None, :]).astype(jnp.float32)
    present = (jnp.arange(doc_length, dtype=jnp.int32)[None, :] < doc_lengths[:, None]).astype(
        jnp.float32
    )
    z_cols = jnp.transpose(z_rows.reshape(doc_count, query_count, query_length), (1, 2, 0))
    shifted = sharpness * scores - z_cols[:, :, :, None]
    shifted = jnp.minimum(shifted, 0.0)
    weight = jnp.exp(shifted) * present[None, None] * signal[:, None, :, None]
    weight = weight.reshape(query_total, doc_count * doc_length).astype(jnp.bfloat16)
    query_part = jnp.dot(weight, doc_rows, preferred_element_type=jnp.float32)
    doc_part = lax.dot_general(
        weight, query_rows, (((0,), (0,)), ((), ())), preferred_element_type=jnp.float32
    )
    return (query_part, doc_part)


def columns(source_table, start_col, span_count):
    return lax.dynamic_slice_in_dim(source_table, start_col, span_count, 1)


def table_rows(source_table, start_row, span_count):
    return lax.dynamic_slice_in_dim(source_table, start_row, span_count, 0)


def per_device(queries, documents, lengths, normalizers, probs, positives):
    cycle_length = lax.axis_size("dev")
    row_index = lax.axis_index(PB)
    doc_count = lengths.shape[0]
    gathered = gathered_copies(queries, PB, 0)
    query_zero = jnp.zeros((gathered.shape[0], documents.shape[1]), jnp.float32)

    def visit_block(anchor, doc_rows, doc_lengths, offset):
        span_count = doc_lengths.shape[0]
        first_doc = (row_index * cycle_length + anchor) * doc_count + offset
        return interact(
            gathered,
            table_rows(normalizers, anchor * doc_count + offset, span_count),
            columns(probs, anchor * doc_count + offset, span_count),
            positives,
            doc_rows,
            doc_lengths,
            first_doc,
        )

    all_rows, all_lengths = (
        gathered_copies(documents, "dev", 0),
        gathered_copies(lengths, "dev", 0),
    )
    block_rows = all_rows.reshape(cycle_length, documents.shape[0], documents.shape[1])
    block_lengths = all_lengths.reshape(cycle_length, doc_count)

    def visit_each(query_sums, inputs):
        anchor, doc_rows, doc_lengths = inputs
        query_part, doc_part = visit_block(anchor, doc_rows, doc_lengths, 0)
        return (query_sums + query_part, doc_part)

    anchors = jnp.arange(cycle_length, dtype=jnp.int32)
    query_sums, doc_parts = lax.scan(visit_each, query_zero, (anchors, block_rows, block_lengths))
    returned = lax.all_to_all(doc_parts, "dev", split_axis=0, concat_axis=0, tiled=True)
    doc_grad = jnp.sum(returned, axis=0)
    query_grad = summed_rows(query_sums, ("pb_0", "pb_1"), "pb_2", 0)
    return (query_grad, doc_grad)


def solution(mesh):
    split = Mesh(mesh.devices.reshape(4, 2, 2, mesh.shape["dev"]), ("pb_0", "pb_1", "pb_2", "dev"))
    return jax.shard_map(
        per_device,
        mesh=split,
        in_specs=(
            P(DEV_PB, None),
            P(PB_DEV, None),
            P(PB_DEV),
            P(PB, "dev"),
            P("dev", PB),
            P("dev"),
        ),
        out_specs=(P(DEV_PB, None), P(PB_DEV, None)),
        check_vma=False,
    )
```

profile of v0, /device:TPU:40, one launch (start us, length us, event | category | flops | bytes accessed | tf_op | source)
XLA Modules:
  0.0 611.1 jit_solution(10489021004140020646)
XLA Ops:
  7.9 25.6 %all_to_all.24 = s32[32,1,2]{2,1,0:T(1,128)S(1)} all-to-all(s32[32,1,2]{2,1,0:T(1,128)S(1)} %broadcast_in_dim.32), channel_id=1, replica_groups=mesh['pb_0'=4,'pb_1'=2,'pb_2'=2,'dev'=32] {'dev'}, dimensions={0} | all-to-all | bytes 512 | tf_op jit(solution)/shard_map/all_to_all | solution.py:17
  34.2 29.4 %all_to_all.25 = bf16[16,32,128]{2,1,0:T(8,128)(2,1)S(1)} all-to-all(bf16[16,32,128]{2,1,0:T(8,128)(2,1)S(1)} %broadcast_in_dim.31), channel_id=1, replica_groups=mesh['pb_0'=4,'pb_1'=2,'pb_2'=2,'dev'=32] {'pb_0','pb_1','pb_2'}, dimensions={0} | all-to-all | bytes 262144 | tf_op jit(solution)/shard_map/all_to_all | solution.py:17
  63.6 2.6 broadcast_in_dim.30
  66.2 5.0 all-to-all-start
  71.3 96.4 %all-to-all-done = bf16[32,256,128]{2,1,0:T(8,128)(2,1)} async-done(((bf16[32,256,128]{2,1,0:T(8,128)(2,1)}), bf16[32,256,128]{2,1,0:T(8,128)(2,1)}, u32[]{:S(2)}, u32[]{:S(2)}) %all-to-all-start) | async-done | bytes 2097184 | tf_op jit(solution)/shard_map/all_to_all | solution.py:17
  167.7 237.6 %while.15 = (s32[]{:T(128)}, f32[512,128]{1,0:T(8,128)S(1)}, f32[32,256,128]{2,1,0:T(8,128)}, bf16[32,256,128]{2,1,0:T(8,128)(2,1)}, bf16[512,128]{1,0:T(8,128)(...) while((s32[]{:T(128)}, f32[512,128]{1,0:T(8,128)S(1)}, ...), condition=%wide.region_1.2_spmd.clone, body=%wide.region_0.1_spmd.clone.sunk | while | flops 101581416 | bytes 8151797 | solution.py:113
  173.1 1.2 convolution_add_fusion.2
  180.5 1.2 convolution_add_fusion.2
  186.7 1.1 fusion.35
  187.9 1.2 convolution_add_fusion.2
  194.2 1.1 fusion.35
  195.3 1.2 convolution_add_fusion.2
  202.7 1.2 convolution_add_fusion.2
  209.0 1.1 fusion.35
  210.1 1.2 convolution_add_fusion.2
  216.4 1.1 fusion.35
  217.6 1.2 convolution_add_fusion.2
  225.0 1.2 convolution_add_fusion.2
  232.5 1.2 convolution_add_fusion.2
  238.7 1.1 fusion.35
  239.9 1.2 convolution_add_fusion.2
  247.3 1.2 convolution_add_fusion.2
  253.6 1.1 fusion.35
  254.7 1.2 convolution_add_fusion.2
  261.0 1.1 fusion.35
  262.1 1.2 convolution_add_fusion.2
  268.4 1.1 fusion.35
  269.6 1.2 convolution_add_fusion.2
  275.8 1.1 fusion.35
  277.0 1.2 convolution_add_fusion.2
  283.3 1.1 fusion.35
  284.4 1.2 convolution_add_fusion.2
  290.7 1.1 fusion.35
  291.9 1.2 convolution_add_fusion.2
  298.1 1.1 fusion.35
  299.3 1.2 convolution_add_fusion.2
  305.5 1.1 fusion.35
  306.7 1.2 convolution_add_fusion.2
  313.0 1.1 fusion.35
  314.1 1.2 convolution_add_fusion.2
  321.5 1.2 convolution_add_fusion.2
  329.0 1.2 convolution_add_fusion.2
  336.4 1.2 convolution_add_fusion.2
  342.7 1.1 fusion.35
  343.8 1.2 convolution_add_fusion.2
  350.1 1.1 fusion.35
  351.2 1.2 convolution_add_fusion.2
  357.5 1.1 fusion.35
  358.6 1.2 convolution_add_fusion.2
  364.9 1.1 fusion.35
  366.1 1.2 convolution_add_fusion.2
  372.3 1.1 fusion.35
  373.5 1.2 convolution_add_fusion.2
  379.8 1.1 fusion.35
  380.9 1.2 convolution_add_fusion.2
  387.2 1.1 fusion.35
  388.3 1.2 convolution_add_fusion.2
  394.6 1.1 fusion.35
  395.8 1.2 convolution_add_fusion.2
  403.2 1.2 convolution_add_fusion.2
  405.3 6.3 %all-to-all-start.3 = ((f32[32,256,128]{2,1,0:T(8,128)}), f32[32,256,128]{2,1,0:T(8,128)}, u32[]{:S(2)}, u32[]{:S(2)}) async-start(f32[32,256,128]{2,1,0:T(8,128)} %get-tuple-element.131), calls=%async_computation.5 | async-start | bytes 8388608 | tf_op jit(solution)/shard_map/all_to_all | solution.py:114
  412.5 17.7 %reduce-scatter.3.cloned.1.call-done = f32[8,32,128]{2,1,0:T(8,128)} async-done(((f32[16,32,128]{2,1,0:T(8,128)}), f32[8,32,128]{2,1,0:T(8,128)}) %reduce-scatter.3.cloned.1.call-update) | async-done | bytes 131088 | tf_op jit(solution)/shard_map/reduce_scatter | solution.py:41
  430.2 171.0 %all-to-all-done.3 = f32[32,256,128]{2,1,0:T(8,128)} async-done(((f32[32,256,128]{2,1,0:T(8,128)}), f32[32,256,128]{2,1,0:T(8,128)}, u32[]{:S(2)}, u32[]{:S(2)}) %all-to-all-start.3) | async-done | bytes 4194336 | tf_op jit(solution)/shard_map/all_to_all | solution.py:114
  601.2 3.0 reduce_sum.9
  (505 shorter events, 134.6 us)
Async XLA Ops:
  7.2 160.5 %copy-start.1 = (s32[16]{0:T(128)S(1)}, s32[16]{0:T(128)}, u32[]{:S(2)}) copy-start(s32[16]{0:T(128)} %param.13) | copy-start | bytes 196
  7.2 160.5 %copy-start = (f32[16,64]{1,0:T(8,128)S(1)}, f32[16,64]{1,0:T(8,128)}, u32[]{:S(2)}) copy-start(f32[16,64]{1,0:T(8,128)} %param.12) | copy-start | bytes 12292
  66.2 101.4 %all-to-all-start = ((bf16[32,256,128]{2,1,0:T(8,128)(2,1)}), bf16[32,256,128]{2,1,0:T(8,128)(2,1)}, u32[]{:S(2)}, u32[]{:S(2)}) async-start(bf16[32,256,128]{2,1,0:T(8,128)(2,1)} %broadcast_in_dim.30), calls=%async_computation | async-start | bytes 4194304 | tf_op jit(solution)/shard_map/all_to_all | solution.py:17
  405.3 195.9 %all-to-all-start.3 = ((f32[32,256,128]{2,1,0:T(8,128)}), f32[32,256,128]{2,1,0:T(8,128)}, u32[]{:S(2)}, u32[]{:S(2)}) async-start(f32[32,256,128]{2,1,0:T(8,128)} %get-tuple-element.131), calls=%async_computation.5 | async-start | bytes 8388608 | tf_op jit(solution)/shard_map/all_to_all | solution.py:114
  411.6 18.5 %reduce-scatter.3.cloned.1.call-start = ((), (), s32[]{:S(2)}) async-start(), calls=%async_computation.6 | async-start | bytes 393216 | tf_op jit(solution)/shard_map/reduce_scatter | solution.py:41
  412.4 191.8 %reduce-scatter.5.cloned.1.call-start = ((), (), s32[]{:S(2)}) async-start(), calls=%async_computation.7 | async-start | bytes 147456 | tf_op jit(solution)/shard_map/reduce_scatter | solution.py:42
Sparse Core Ops, SparseCore 0:
  415.2 14.8 reduce-scatter.2
  435.8 156.5 reduce-scatter.4
where the time goes:
time: 617 us; the launch traced here: 611 us
  waiting for transfers between devices  285 us (46%)
  matrix products  102 us (17%)
  local copies, waits for them, and re-layouts  94.8 us (15%)
  blocking collectives  55 us (9%)
  loops' own time  43 us (7%)
  between operations  14.1 us (2%)
  starting transfers between devices  11.4 us (2%)
    all_to_all x1, waiting for transfers between devices, per_device(): lax.all_to_all(doc_parts, 'dev', split_axis=0, concat_axis=0, tiled=True)  171 us
    all_to_all x1, waiting for transfers between devices, from_everyone(): return lax.all_to_all(copies, axis, split_axis=0, concat_axis=0, tiled=True)  96.4 us
    all_to_all x2, blocking collectives, from_everyone(): return lax.all_to_all(copies, axis, split_axis=0, concat_axis=0, tiled=True)  55 us
    another operation x1, loops' own time, per_device(): lax.scan(visit_each, query_zero, (anchors, block_rows, block_lengths))  43 us
    dot_general x32, matrix products, interact(): query_part = jnp.dot(weight, doc_rows, preferred_element_type=jnp.float32)  37.1 us
    dot_general x32, matrix products, interact(): lax.dot_general(query_rows, doc_rows, (((1,), (1,)), ((), ())), preferred...  36.4 us
    dot_general x32, matrix products, interact(): lax.dot_general(weight, query_rows, (((0,), (0,)), ((), ())), preferred_e...  28.2 us
    dynamic_slice x64, local copies, waits for them, and re-layouts, table_rows(): return lax.dynamic_slice_in_dim(source_table, start_row, span_count, 0)  27.8 us
  transfers between devices with their start and end apart: 4, of which 3 were waited for; matrix products, arithmetic and copies ran while one was open for 1% of the time, Pallas kernels for 0%

commit v1 on v0

v1 whole, which is shorter than its diff:
```python
import jax
import jax.numpy as jnp
from jax import lax
from jax.experimental import pallas as pl
from jax.experimental.pallas import tpu as pltpu
from jax.sharding import Mesh
from jax.sharding import PartitionSpec as P

DOC_AXES = ("x", "zh", "c")
QUERY_AXES = ("y", "zl")
RING = ("zh", "zl")

SHARPNESS = 10.0
LOG2E = 1.4426950408889634
f32, bf16 = jnp.float32, jnp.bfloat16


def tile_body(q_ref, d_ref, n_ref, qg_ref, dg_ref, w_ref):
    step = pl.program_id(0)
    docs, length = n_ref.shape[1], d_ref.shape[0] // n_ref.shape[1]
    nx, nc, nzh, _, rows, width = q_ref.shape
    tokens = nx * nc * nzh * rows
    queries = tokens // rows
    q = jnp.swapaxes(q_ref[...].reshape(nx, nc, nzh, rows, width), 1, 2).reshape(tokens, width)
    z = n_ref[0, :, :tokens] * LOG2E
    one_each = n_ref[0, :, tokens : tokens + queries]
    place = lax.broadcasted_iota(jnp.int32, (queries, tokens), 1) // rows
    spread = (place == lax.broadcasted_iota(jnp.int32, (queries, tokens), 0)).astype(f32)
    signal = jnp.dot(one_each, spread, preferred_element_type=f32, precision=lax.Precision.HIGHEST)
    for k in range(docs):
        d = d_ref[k * length : (k + 1) * length, :]
        s = lax.dot_general(d, q, (((1,), (1,)), ((), ())), preferred_element_type=f32)
        t = jnp.minimum(s * (SHARPNESS * LOG2E) - z[k : k + 1, :], 0.0)
        w_ref[k * length : (k + 1) * length, :] = (jnp.exp2(t) * signal[k : k + 1, :]).astype(bf16)
    w = w_ref[...]
    qg = lax.dot_general(w, d_ref[...], (((0,), (0,)), ((), ())), preferred_element_type=f32)
    qg = jnp.transpose(qg.reshape(nx, nzh, nc, rows, width), (2, 0, 1, 3, 4))
    qg_ref[...] = qg.reshape(qg_ref.shape)
    dg = jnp.dot(w, q, preferred_element_type=f32)

    @pl.when(step == 0)
    def _():
        dg_ref[...] = dg

    @pl.when(step > 0)
    def _():
        dg_ref[...] += dg


def tile_gradients(q, d, n):
    nx, nc, nzh, nzl, rows, width = q.shape
    slots = d.shape[0]
    tokens = nx * nc * nzh * rows
    return pl.pallas_call(
        tile_body,
        grid=(nzl,),
        in_specs=[
            pl.BlockSpec((nx, nc, nzh, 1, rows, width), lambda i: (0, 0, 0, i, 0, 0)),
            pl.BlockSpec((slots, width), lambda i: (0, 0)),
            pl.BlockSpec((1, *n.shape[1:]), lambda i: (i, 0, 0)),
        ],
        out_specs=[
            pl.BlockSpec((nc, nx, nzh, 1, rows, width), lambda i: (0, 0, 0, i, 0, 0)),
            pl.BlockSpec((slots, width), lambda i: (0, 0)),
        ],
        out_shape=[
            jax.ShapeDtypeStruct((nc, nx, nzh, nzl, rows, width), f32),
            jax.ShapeDtypeStruct((slots, width), f32),
        ],
        scratch_shapes=[pltpu.VMEM((slots, tokens), bf16)],
        name="pair_tile",
        compiler_params=pltpu.CompilerParams(vmem_limit_bytes=48 * 1024 * 1024),
        cost_estimate=pl.CostEstimate(
            flops=6 * nzl * tokens * slots * width,
            bytes_accessed=8 * nzl * tokens * width,
            transcendentals=nzl * tokens * slots,
        ),
    )(q, d, n)


def per_device(queries, documents, lengths, normalizers, probs, positives):
    ny, nzl = lax.axis_size("y"), lax.axis_size("zl")
    nx, nzh, nc = (lax.axis_size(a) for a in DOC_AXES)
    nz = nzh * nzl
    rows, width = queries.shape
    local_docs = lengths.shape[0]
    length = documents.shape[0] // local_docs
    row_docs = normalizers.shape[0]
    row_queries, row_tokens = probs.shape[0], normalizers.shape[1]

    q = lax.all_to_all(
        jnp.broadcast_to(queries, (nz, rows, width)), RING, split_axis=0, concat_axis=0, tiled=True
    )
    q = lax.all_gather(q, ("x", "c"))
    q = q.reshape(nx, nc, nzh, nzl, rows, width)

    live = (jnp.arange(length, dtype=jnp.int32)[None, :] < lengths[:, None]).reshape(-1, 1)
    d = lax.all_gather(jnp.where(live, documents, 0).astype(bf16), "y", tiled=True)

    first_doc = lax.axis_index(DOC_AXES) * row_docs
    doc_ids = first_doc + jnp.arange(row_docs, dtype=jnp.int32)
    signal = probs - (positives[:, None] == doc_ids[None, :]).astype(f32)
    pad = (-row_queries) % 128
    table = jnp.concatenate(
        [normalizers, signal.T, jnp.zeros((row_docs, pad), f32)], axis=1
    )
    table = table.reshape(ny, nzl, local_docs, row_tokens + row_queries + pad)
    table = jnp.swapaxes(table, 0, 1).reshape(nzl, ny * local_docs, -1)
    table = lax.all_to_all(table, "zl", split_axis=0, concat_axis=0, tiled=True)

    qg, dg = tile_gradients(q, d, table)

    doc_grad = lax.psum_scatter(dg, "y", scatter_dimension=0, tiled=True)
    doc_grad = jnp.where(live, doc_grad, 0.0)

    me = lax.axis_index("c")
    mine = lax.dynamic_index_in_dim(qg, me, 0, keepdims=False)
    other = lax.dynamic_index_in_dim(qg, 1 - me, 0, keepdims=False)
    mine = mine + lax.ppermute(other, "c", [(0, 1), (1, 0)])
    mine = mine.reshape(nx, nz * rows, width)
    mine = jnp.sum(lax.all_to_all(mine, "x", split_axis=0, concat_axis=0, tiled=True), axis=0)
    mine = mine.reshape(nz, rows, width)
    query_grad = jnp.sum(lax.all_to_all(mine, RING, split_axis=0, concat_axis=0, tiled=True), axis=0)
    return query_grad, doc_grad


def solution(mesh):
    split = Mesh(mesh.devices.reshape(4, 2, 2, 4, 8), ("x", "zh", "c", "y", "zl"))
    return jax.shard_map(
        per_device,
        mesh=split,
        in_specs=(
            P((*QUERY_AXES, *DOC_AXES), None),
            P((*DOC_AXES, *QUERY_AXES), None),
            P((*DOC_AXES, *QUERY_AXES)),
            P(DOC_AXES, QUERY_AXES),
            P(QUERY_AXES, DOC_AXES),
            P(QUERY_AXES),
        ),
        out_specs=(P((*QUERY_AXES, *DOC_AXES), None), P((*DOC_AXES, *QUERY_AXES), None)),
        check_vma=False,
    )
```

time: 617 us -> 139 us (0.23)
  the two profiles are of different devices: /device:TPU:40 before, /device:TPU:8 now
where the time goes in v1:
time: 139 us
  blocking collectives  42.3 us (30%)
  waiting for transfers between devices  39.7 us (29%)
  starting transfers between devices  21.8 us (16%)
  between operations  14.1 us (10%)
  Pallas kernels  10.3 us (7%)
  other arithmetic  7.32 us (5%)
  local copies, waits for them, and re-layouts  3.07 us (2%)
    all_to_all x1, blocking collectives, per_device(): lax.all_to_all(jnp.broadcast_to(queries, (nz, rows, width)), RING, split_...  29.8 us
    all_to_all x1, waiting for transfers between devices, per_device(): lax.all_to_all(mine, 'x', split_axis=0, concat_axis=0, tiled=True)  15 us
    all_gather x1, blocking collectives, per_device(): lax.all_gather(jnp.where(live, documents, 0).astype(bf16), 'y', tiled=True)  12.5 us
    all_to_all x1, starting transfers between devices, per_device(): lax.all_to_all(mine, RING, split_axis=0, concat_axis=0, tiled=True)  12.3 us
    all_to_all x1, waiting for transfers between devices, per_device(): lax.all_to_all(mine, RING, split_axis=0, concat_axis=0, tiled=True)  12.2 us
    pallas_call x1, Pallas kernels, tile_gradients(): pl.pallas_call(tile_body, grid=(nzl,), in_specs=[pl.BlockSpec((nx, nc, nz...  10.3 us
    all_gather x1, waiting for transfers between devices, per_device(): q = lax.all_gather(q, ('x', 'c'))  5.01 us
    reduce_scatter x1, waiting for transfers between devices, per_device(): doc_grad = lax.psum_scatter(dg, 'y', scatter_dimension=0, tiled=True)  4.31 us
  transfers between devices with their start and end apart: 6, of which 5 were waited for; matrix products, arithmetic and copies ran while one was open for 4% of the time, Pallas kernels for 0%

profile of v1, /device:TPU:8, one launch (start us, length us, event | category | flops | bytes accessed | tf_op | source)
XLA Modules:
  0.0 138.7 jit_solution(5256964358461784981)
XLA Ops:
  7.2 0.0 copy-start.2
  7.2 0.0 copy-start.1
  7.2 0.0 all-gather.3.cloned.1.call-start
  7.2 0.7 broadcast_in_dim.32
  7.9 29.8 %all_to_all.20 = bf16[16,32,128]{2,1,0:T(8,128)(2,1)} all-to-all(bf16[16,32,128]{2,1,0:T(8,128)(2,1)S(1)} %broadcast_in_dim.32), channel_id=1, replica_groups=mesh['x'=4,'zh'=2,'c'=2,'y'=4,'zl'=8] {'zh','zl'}, dimensions={0} | all-to-all | bytes 262144 | tf_op jit(solution)/shard_map/all_to_all | solution.py:91
  37.7 0.0 all-gather.3.cloned.1.call-update
  37.8 0.8 subtract_bitcast_fusion
  38.6 0.1 copy.12
  38.7 0.1 pad.2.clone
  38.7 0.9 maximum_maximum_fusion
  39.7 0.1 reshape.41
  39.8 0.8 reshape.42
  40.6 3.7 %all-to-all-start.1 = ((f32[8,8,640]{2,1,0:T(8,128)}), f32[8,8,640]{2,1,0:T(8,128)S(1)}, u32[]{:S(2)}, u32[]{:S(2)}) async-start(f32[8,8,640]{2,1,0:T(8,128)} %reshape.42), calls=%async_computation.1 | async-start | bytes 327680 | tf_op jit(solution)/shard_map/all_to_all | solution.py:109
  44.3 0.0 copy-done.2
  44.3 0.1 compare_bitcast_fusion
  44.4 0.0 copy-done.1
  44.4 0.1 broadcast_select_fusion.1
  44.5 12.5 %all_gather.11.d_ref = bf16[1024,128]{1,0:T(8,128)(2,1)S(1)} all-gather(bf16[256,128]{1,0:T(8,128)(2,1)S(1)} %broadcast_select_fusion.1), channel_id=1, replica_groups=mesh['x'=4,'zh'=2,'c'=2,'y'=4,'zl'=8] {'y'}, dimensions={0}, use_global_device_ids=true | all-gather | bytes 327680 | tf_op jit(solution)/shard_map/all_gather | solution.py:98
  57.0 0.0 all-to-all-done.1.n_ref
  57.0 5.0 %all-gather.3.cloned.1.call-done = bf16[128,32,128]{2,1,0:T(8,128)(2,1)} async-done(((bf16[16,32,128]{2,1,0:T(8,128)(2,1)}), bf16[128,32,128]{2,1,0:T(8,128)(2,1)}) %all-gather.3.cloned.1.call-update) | async-done | bytes 1048592 | tf_op jit(solution)/shard_map/all_gather | solution.py:94
  62.0 0.0 copy-start
  62.0 1.2 copy-done
  63.2 10.3 %pair_tile.1 = (f32[2,4,2,8,32,128]{5,4,3,2,1,0:T(8,128)S(1)}, f32[1024,128]{1,0:T(8,128)}) custom-call(bf16[4,2,2,8,32,128]{5,4,3,2,1,0:T(8,128)(2,1)S(1)} %bitcast.14, bf16[1024,128]{1,0:T(8,128)(2,1)S(1)} %all_gather.11.d_ref, f32[8,8,640]{2,1,0:T(8,128)S(1)} %all-to-all-done.1.n_ref), custom_call_target="tpu_custom_call" | custom-call | flops 3221225472 | bytes 4194304 | tf_op jit(solution)/shard_map/pair_tile/pallas_call | solution.py:54
  73.6 0.1 dynamic-slice_bitcast_fusion
  73.6 2.2 %collective-permute-start = (f32[4,2,8,32,128]{4,3,2,1,0:T(8,128)S(1)}, f32[4,2,8,32,128]{4,3,2,1,0:T(8,128)}, u32[]{:S(2)}, u32[]{:S(2)}) collective-permute-start(f32[4,2,8,32,128]{4,3,2,1,0:T(8,128)S(1)} %dynamic-slice_bitcast_fusion), channel_id=1, source_target_pairs={{0,32},{32,0},{1,33},{33,1},{2,34},{34,2},{3,35},{35,3},{4,36},{36... | collective-permute-start | bytes 3145736 | tf_op jit(solution)/shard_map/ppermute | solution.py:119
  75.8 2.5 %collective-permute-done = f32[4,2,8,32,128]{4,3,2,1,0:T(8,128)} collective-permute-done((f32[4,2,8,32,128]{4,3,2,1,0:T(8,128)S(1)}, f32[4,2,8,32,128]{4,3,2,1,0:T(8,128)}, u32[]{:S(2)}, u32[]{:S(2)}) %collective-permute-start) | collective-permute-done | bytes 1048608 | tf_op jit(solution)/shard_map/ppermute | solution.py:119
  78.3 2.4 %bitcast_add_fusion = f32[4,2,8,32,128]{4,3,2,1,0:T(8,128)} fusion(f32[4,2,8,32,128]{4,3,2,1,0:T(8,128)} %collective-permute-done, f32[2,4,2,8,32,128]{5,4,3,2,1,0:T(8,128)S(1)} %get-tuple-element.4, s32[]{:T(128)S(6)} %select_n.16), kind=kLoop, calls=%fused_computation | loop fusion | flops 262144 | bytes 3145732 | tf_op jit(solution)/shard_map/add | solution.py:119
  80.7 3.5 %all-to-all-start.2 = ((f32[4,512,128]{2,1,0:T(8,128)}), f32[4,512,128]{2,1,0:T(8,128)S(1)}, u32[]{:S(2)}, u32[]{:S(2)}) async-start(f32[4,512,128]{2,1,0:T(8,128)} %bitcast.6), calls=%async_computation.2 | async-start | bytes 2097152 | tf_op jit(solution)/shard_map/all_to_all | solution.py:121
  84.2 0.0 reduce-scatter.2.cloned.1.call-start
  84.3 0.7 reduce-scatter.2.cloned.1.call-update
  85.0 15.0 %all-to-all-done.2 = f32[4,512,128]{2,1,0:T(8,128)S(1)} async-done(((f32[4,512,128]{2,1,0:T(8,128)}), f32[4,512,128]{2,1,0:T(8,128)S(1)}, u32[]{:S(2)}, u32[]{:S(2)}) %all-to-all-start.2) | async-done | bytes 1048608 | tf_op jit(solution)/shard_map/all_to_all | solution.py:121
  100.0 0.8 reduce_sum.18
  100.8 12.3 %all-to-all-start.3 = ((f32[16,32,128]{2,1,0:T(8,128)}), f32[16,32,128]{2,1,0:T(8,128)S(1)}, u32[]{:S(2)}, u32[]{:S(2)}) async-start(f32[16,32,128]{2,1,0:T(8,128)} %bitcast.7), calls=%async_computation.3 | async-start | bytes 524288 | tf_op jit(solution)/shard_map/all_to_all | solution.py:123
  113.1 4.3 %reduce-scatter.2.cloned.1.call-done = f32[256,128]{1,0:T(8,128)} async-done(((f32[1024,128]{1,0:T(8,128)}), f32[256,128]{1,0:T(8,128)}) %reduce-scatter.2.cloned.1.call-update) | async-done | bytes 131088 | tf_op jit(solution)/shard_map/reduce_scatter | solution.py:113
  117.4 1.7 %broadcast_select_fusion = f32[256,128]{1,0:T(8,128)} fusion(f32[256,128]{1,0:T(8,128)} %reduce-scatter.2.cloned.1.call-done, pred[256]{0:T(512)(128)(4,1)S(1)} %compare_bitcast_fusion), kind=kLoop, calls=%fused_computation.4 | loop fusion | flops 32768 | bytes 262400 | tf_op jit(solution)/shard_map/jit(_where)/select_n | solution.py:114
  119.0 12.2 %all-to-all-done.3 = f32[16,32,128]{2,1,0:T(8,128)S(1)} async-done(((f32[16,32,128]{2,1,0:T(8,128)}), f32[16,32,128]{2,1,0:T(8,128)S(1)}, u32[]{:S(2)}, u32[]{:S(2)}) %all-to-all-start.3) | async-done | bytes 262176 | tf_op jit(solution)/shard_map/all_to_all | solution.py:123
  131.2 0.6 reduce_sum.19
  (3 shorter events, 0.0 us)
Async XLA Ops:
  7.2 37.1 %copy-start.2 = (s32[2]{0:T(128)S(1)}, s32[2]{0:T(128)}, u32[]{:S(2)}) copy-start(s32[2]{0:T(128)} %param.8) | copy-start | bytes 28
  7.2 37.2 %copy-start.1 = (bf16[256,128]{1,0:T(8,128)(2,1)S(1)}, bf16[256,128]{1,0:T(8,128)(2,1)}, u32[]{:S(2)}) copy-start(bf16[256,128]{1,0:T(8,128)(2,1)} %param.7) | copy-start | bytes 196612
  7.2 54.8 %all-gather.3.cloned.1.call-start = ((), (), s32[]{:S(2)}) async-start(), calls=%async_computation.6 | async-start | bytes 1179648 | tf_op jit(solution)/shard_map/all_gather | solution.py:94
  40.6 16.4 %all-to-all-start.1 = ((f32[8,8,640]{2,1,0:T(8,128)}), f32[8,8,640]{2,1,0:T(8,128)S(1)}, u32[]{:S(2)}, u32[]{:S(2)}) async-start(f32[8,8,640]{2,1,0:T(8,128)} %reshape.42), calls=%async_computation.1 | async-start | bytes 327680 | tf_op jit(solution)/shard_map/all_to_all | solution.py:109
  62.0 1.2 copy-start
  73.6 4.7 %collective-permute-start = (f32[4,2,8,32,128]{4,3,2,1,0:T(8,128)S(1)}, f32[4,2,8,32,128]{4,3,2,1,0:T(8,128)}, u32[]{:S(2)}, u32[]{:S(2)}) collective-permute-start(f32[4,2,8,32,128]{4,3,2,1,0:T(8,128)S(1)} %dynamic-slice_bitcast_fusion), channel_id=1, source_target_pairs={{0,32},{32,0},{1,33},{33,1},{2,34},{34,2},{3,35},{35,3},{4,36},{36... | collective-permute-start | bytes 3145736 | tf_op jit(solution)/shard_map/ppermute | solution.py:119
  80.7 19.3 %all-to-all-start.2 = ((f32[4,512,128]{2,1,0:T(8,128)}), f32[4,512,128]{2,1,0:T(8,128)S(1)}, u32[]{:S(2)}, u32[]{:S(2)}) async-start(f32[4,512,128]{2,1,0:T(8,128)} %bitcast.6), calls=%async_computation.2 | async-start | bytes 2097152 | tf_op jit(solution)/shard_map/all_to_all | solution.py:121
  84.2 33.1 %reduce-scatter.2.cloned.1.call-start = ((), (), s32[]{:S(2)}) async-start(), calls=%async_computation.5 | async-start | bytes 655360 | tf_op jit(solution)/shard_map/reduce_scatter | solution.py:113
  100.8 30.4 %all-to-all-start.3 = ((f32[16,32,128]{2,1,0:T(8,128)}), f32[16,32,128]{2,1,0:T(8,128)S(1)}, u32[]{:S(2)}, u32[]{:S(2)}) async-start(f32[16,32,128]{2,1,0:T(8,128)} %bitcast.7), calls=%async_computation.3 | async-start | bytes 524288 | tf_op jit(solution)/shard_map/all_to_all | solution.py:123
Sparse Core Ops, SparseCore 0:
  37.9 24.0 all-gather.2
  87.9 29.4 reduce-scatter.1

commit v2 on v1

--- a/solution.py
+++ b/solution.py
@@ -9,19 +9,24 @@
 DOC_AXES = ("x", "zh", "c")
 QUERY_AXES = ("y", "zl")
 RING = ("zh", "zl")
+PLANE = ("x", "c")
 
 SHARPNESS = 10.0
 LOG2E = 1.4426950408889634
-f32, bf16 = jnp.float32, jnp.bfloat16
+TOP = 14.0
+f32, f16, bf16 = jnp.float32, jnp.float16, jnp.bfloat16
 
 
-def tile_body(q_ref, d_ref, n_ref, qg_ref, dg_ref, w_ref):
+def tile_body(*refs):
+    *q_refs, d_ref, n_ref, qg_ref, dg_ref, top_ref, w_ref = refs
     step = pl.program_id(0)
     docs, length = n_ref.shape[1], d_ref.shape[0] // n_ref.shape[1]
-    nx, nc, nzh, _, rows, width = q_ref.shape
+    nx, nc, _, rows, width = q_refs[0].shape
+    nzh = len(q_refs)
     tokens = nx * nc * nzh * rows
     queries = tokens // rows
-    q = jnp.swapaxes(q_ref[...].reshape(nx, nc, nzh, rows, width), 1, 2).reshape(tokens, width)
+    q = jnp.stack([r[...].reshape(nx, nc, rows, width) for r in q_refs], axis=1)
+    q = q.reshape(tokens, width)
     z = n_ref[0, :, :tokens] * LOG2E
     one_each = n_ref[0, :, tokens : tokens + queries]
     place = lax.broadcasted_iota(jnp.int32, (queries, tokens), 1) // rows
@@ -34,38 +39,49 @@
         w_ref[k * length : (k + 1) * length, :] = (jnp.exp2(t) * signal[k : k + 1, :]).astype(bf16)
     w = w_ref[...]
     qg = lax.dot_general(w, d_ref[...], (((0,), (0,)), ((), ())), preferred_element_type=f32)
-    qg = jnp.transpose(qg.reshape(nx, nzh, nc, rows, width), (2, 0, 1, 3, 4))
+    here = jnp.max(jnp.abs(qg).reshape(-1, 8, width), axis=0)
+    qg = jnp.swapaxes(qg.reshape(nx, nzh, nc, rows, width), 1, 2)
     qg_ref[...] = qg.reshape(qg_ref.shape)
     dg = jnp.dot(w, q, preferred_element_type=f32)
 
     @pl.when(step == 0)
     def _():
         dg_ref[...] = dg
+        top_ref[...] = here
 
     @pl.when(step > 0)
     def _():
         dg_ref[...] += dg
+        top_ref[...] = jnp.maximum(top_ref[...], here)
+
+    @pl.when(step == pl.num_programs(0) - 1)
+    def _():
+        largest = jnp.maximum(jnp.max(top_ref[...], keepdims=True), 1e-30)
+        top_ref[...] = jnp.broadcast_to(jnp.ceil(jnp.log2(largest)), top_ref.shape)
 
 
-def tile_gradients(q, d, n):
-    nx, nc, nzh, nzl, rows, width = q.shape
+def tile_gradients(parts, d, n):
+    nx, nc, nzl, rows, width = parts[0].shape
+    nzh = len(parts)
     slots = d.shape[0]
     tokens = nx * nc * nzh * rows
     return pl.pallas_call(
         tile_body,
         grid=(nzl,),
         in_specs=[
-            pl.BlockSpec((nx, nc, nzh, 1, rows, width), lambda i: (0, 0, 0, i, 0, 0)),
+            *[pl.BlockSpec((nx, nc, 1, rows, width), lambda i: (0, 0, i, 0, 0))] * nzh,
             pl.BlockSpec((slots, width), lambda i: (0, 0)),
             pl.BlockSpec((1, *n.shape[1:]), lambda i: (i, 0, 0)),
         ],
         out_specs=[
-            pl.BlockSpec((nc, nx, nzh, 1, rows, width), lambda i: (0, 0, 0, i, 0, 0)),
+            pl.BlockSpec((nx, nc, nzh, 1, rows, width), lambda i: (0, 0, 0, i, 0, 0)),
             pl.BlockSpec((slots, width), lambda i: (0, 0)),
+            pl.BlockSpec((8, width), lambda i: (0, 0)),
         ],
         out_shape=[
-            jax.ShapeDtypeStruct((nc, nx, nzh, nzl, rows, width), f32),
+            jax.ShapeDtypeStruct((nx, nc, nzh, nzl, rows, width), f32),
             jax.ShapeDtypeStruct((slots, width), f32),
+            jax.ShapeDtypeStruct((8, width), f32),
         ],
         scratch_shapes=[pltpu.VMEM((slots, tokens), bf16)],
         name="pair_tile",
@@ -75,7 +91,22 @@
             bytes_accessed=8 * nzl * tokens * width,
             transcendentals=nzl * tokens * slots,
         ),
-    )(q, d, n)
+    )(*parts, d, n)
+
+
+def from_everyone(x, axes):
+    copies = jnp.broadcast_to(x, (lax.axis_size(axes), *x.shape))
+    return lax.all_to_all(copies, axes, split_axis=0, concat_axis=0, tiled=True)
+
+
+def summed_pieces(pieces, top, axes):
+    count, _, width = pieces.shape
+    sent = (pieces * jnp.exp2(TOP - top)).astype(f16)
+    sent = jnp.concatenate([sent, jnp.full((count, 8, width), top, f32).astype(f16)], axis=1)
+    got = lax.all_to_all(sent, axes, split_axis=0, concat_axis=0, tiled=True).astype(f32)
+    tops = got[:, -8, 0]
+    total = jnp.sum(got[:, :-8] * jnp.exp2(tops - TOP)[:, None, None], axis=0)
+    return total, jnp.max(tops)
 
 
 def per_device(queries, documents, lengths, normalizers, probs, positives):
@@ -88,12 +119,7 @@
     row_docs = normalizers.shape[0]
     row_queries, row_tokens = probs.shape[0], normalizers.shape[1]
 
-    q = lax.all_to_all(
-        jnp.broadcast_to(queries, (nz, rows, width)), RING, split_axis=0, concat_axis=0, tiled=True
-    )
-    q = lax.all_gather(q, ("x", "c"))
-    q = q.reshape(nx, nc, nzh, nzl, rows, width)
-
+    q = from_everyone(queries, RING)
     live = (jnp.arange(length, dtype=jnp.int32)[None, :] < lengths[:, None]).reshape(-1, 1)
     d = lax.all_gather(jnp.where(live, documents, 0).astype(bf16), "y", tiled=True)
 
@@ -108,19 +134,18 @@
     table = jnp.swapaxes(table, 0, 1).reshape(nzl, ny * local_docs, -1)
     table = lax.all_to_all(table, "zl", split_axis=0, concat_axis=0, tiled=True)
 
-    qg, dg = tile_gradients(q, d, table)
+    parts = [
+        lax.all_gather(half, PLANE).reshape(nx, nc, nzl, rows, width)
+        for half in q.reshape(nzh, nzl, rows, width)
+    ]
+    qg, dg, top = tile_gradients(parts, d, table)
 
     doc_grad = lax.psum_scatter(dg, "y", scatter_dimension=0, tiled=True)
     doc_grad = jnp.where(live, doc_grad, 0.0)
 
-    me = lax.axis_index("c")
-    mine = lax.dynamic_index_in_dim(qg, me, 0, keepdims=False)
-    other = lax.dynamic_index_in_dim(qg, 1 - me, 0, keepdims=False)
-    mine = mine + lax.ppermute(other, "c", [(0, 1), (1, 0)])
-    mine = mine.reshape(nx, nz * rows, width)
-    mine = jnp.sum(lax.all_to_all(mine, "x", split_axis=0, concat_axis=0, tiled=True), axis=0)
-    mine = mine.reshape(nz, rows, width)
-    query_grad = jnp.sum(lax.all_to_all(mine, RING, split_axis=0, concat_axis=0, tiled=True), axis=0)
+    mine, top = summed_pieces(qg.reshape(nx * nc, nz * rows, width), top[0, 0], PLANE)
+    spare = (nx * nc - 1).bit_length()
+    query_grad, _ = summed_pieces(mine.reshape(nz, rows, width), top + spare, RING)
     return query_grad, doc_grad
 
 

time: 139 us -> 147 us (1.058)
  starting transfers between devices: 21.8 us -> 38.9 us
  waiting for transfers between devices: 39.7 us -> 29.9 us
  blocking collectives: 42.3 us -> 39.2 us
  between operations: 14.1 us -> 16.2 us
  local copies, waits for them, and re-layouts: 3.07 us -> 4.82 us
    all_to_all x1 -> x0, blocking collectives: 29.8 us -> none  [per_device(): lax.all_to_all(jnp.broadcast_to(queries, (nz, rows, width)), RING, split_...]
    all_gather x0 -> x2, blocking collectives: none -> 26.6 us  [per_device(): lax.all_gather(half, PLANE).reshape(nx, nc, nzl, rows, width)]
    all_to_all x2 -> x3, starting transfers between devices: 15.8 us -> 28.9 us  [the longest x1 15.2 us: from_everyone(): return lax.all_to_all(copies, axes, split_axis=0, concat_axis=0, tiled=True)]
    all_to_all x1, starting transfers between devices: 3.73 us -> 9.94 us  [per_device(): table = lax.all_to_all(table, 'zl', split_axis=0, concat_axis=0, tiled=True)]
    all_gather x1 -> x0, waiting for transfers between devices: 5.01 us -> none  [per_device(): q = lax.all_gather(q, ('x', 'c'))]
    ppermute x1 -> x0, waiting for transfers between devices: 2.51 us -> none  [per_device(): mine = mine + lax.ppermute(other, 'c', [(0, 1), (1, 0)])]
    add x1 -> x0, other arithmetic: 2.4 us -> none  [per_device(): mine = mine + lax.ppermute(other, 'c', [(0, 1), (1, 0)])]
    reduce_scatter x1, waiting for transfers between devices: 4.31 us -> 2.03 us  [per_device(): doc_grad = lax.psum_scatter(dg, 'y', scatter_dimension=0, tiled=True)]
  transfers between devices with their start and end apart: 6 -> 5, of which waited for: 5 -> 3; matrix products, arithmetic and copies ran while one was open for 4% -> 5% of each run, Pallas kernels for 0% -> 0%
where the time goes in v2:
time: 147 us
  blocking collectives  39.2 us (27%)
  starting transfers between devices  38.9 us (26%)
  waiting for transfers between devices  29.9 us (20%)
  between operations  16.2 us (11%)
  Pallas kernels  10.5 us (7%)
  other arithmetic  7.23 us (5%)
  local copies, waits for them, and re-layouts  4.82 us (3%)
    all_to_all x2, waiting for transfers between devices, summed_pieces(): lax.all_to_all(sent, axes, split_axis=0, concat_axis=0, tiled=True)  27.1 us
    all_gather x2, blocking collectives, per_device(): lax.all_gather(half, PLANE).reshape(nx, nc, nzl, rows, width)  26.6 us
    all_to_all x1, starting transfers between devices, from_everyone(): return lax.all_to_all(copies, axes, split_axis=0, concat_axis=0, tiled=True)  15.2 us
    all_to_all x2, starting transfers between devices, summed_pieces(): lax.all_to_all(sent, axes, split_axis=0, concat_axis=0, tiled=True)  13.7 us
    all_gather x1, blocking collectives, per_device(): lax.all_gather(jnp.where(live, documents, 0).astype(bf16), 'y', tiled=True)  12.6 us
    pallas_call x1, Pallas kernels, tile_gradients(): pl.pallas_call(tile_body, grid=(nzl,), in_specs=[*[pl.BlockSpec((nx, nc,...  10.5 us
    all_to_all x1, starting transfers between devices, per_device(): table = lax.all_to_all(table, 'zl', split_axis=0, concat_axis=0, tiled=True)  9.94 us
  transfers between devices with their start and end apart: 5, of which 3 were waited for; matrix products, arithmetic and copies ran while one was open for 5% of the time, Pallas kernels for 0%

profile of v2, /device:TPU:8, one launch (start us, length us, event | category | flops | bytes accessed | tf_op | source)
XLA Modules:
  0.0 146.7 jit_solution(11900622947180315307)
XLA Ops:
  7.2 1.4 broadcast_in_dim.36
  8.5 15.2 %all-to-all-start = ((bf16[16,32,128]{2,1,0:T(8,128)(2,1)}), bf16[16,32,128]{2,1,0:T(8,128)(2,1)S(1)}, u32[]{:S(2)}, u32[]{:S(2)}) async-start(bf16[16,32,128]{2,1,0:T(8,128)(2,1)} %broadcast_in_dim.36), calls=%async_computation | async-start | bytes 262144 | tf_op jit(solution)/shard_map/all_to_all | solution.py:99
  23.8 0.8 subtract_bitcast_fusion
  24.5 0.1 copy.19
  24.6 0.1 pad.4.clone
  24.7 0.9 maximum_maximum_fusion
  25.6 0.1 reshape.56
  25.7 0.8 reshape.57
  26.5 0.7 compare_bitcast_fusion
  27.2 0.9 broadcast_select_fusion.1
  28.2 12.6 %all_gather.11.refs_2_ = bf16[1024,128]{1,0:T(8,128)(2,1)S(1)} all-gather(bf16[256,128]{1,0:T(8,128)(2,1)S(1)} %broadcast_select_fusion.1), channel_id=1, replica_groups=mesh['x'=4,'zh'=2,'c'=2,'y'=4,'zl'=8] {'y'}, dimensions={0}, use_global_device_ids=true | all-gather | bytes 327680 | tf_op jit(solution)/shard_map/all_gather | solution.py:124
  40.8 0.0 all-to-all-done
  40.8 9.9 %all-to-all-start.1 = ((f32[8,8,640]{2,1,0:T(8,128)}), f32[8,8,640]{2,1,0:T(8,128)S(1)}, u32[]{:S(2)}, u32[]{:S(2)}) async-start(f32[8,8,640]{2,1,0:T(8,128)} %reshape.57), calls=%async_computation.1 | async-start | bytes 327680 | tf_op jit(solution)/shard_map/all_to_all | solution.py:135
  50.8 13.5 %all-gather.1 = bf16[64,32,128]{2,1,0:T(8,128)(2,1)S(1)} all-gather(bf16[8,32,128]{2,1,0:T(8,128)(2,1)S(1)} %get-tuple-element.10), channel_id=3, replica_groups=mesh['x'=4,'zh'=2,'c'=2,'y'=4,'zl'=8] {'x','c'}, dimensions={0}, use_global_device_ids=true | all-gather | bytes 589824 | tf_op jit(solution)/shard_map/all_gather | solution.py:138
  64.2 13.1 %all-gather = bf16[64,32,128]{2,1,0:T(8,128)(2,1)S(1)} all-gather(bf16[8,32,128]{2,1,0:T(8,128)(2,1)S(1)} %get-tuple-element.11), channel_id=2, replica_groups=mesh['x'=4,'zh'=2,'c'=2,'y'=4,'zl'=8] {'x','c'}, dimensions={0}, use_global_device_ids=true | all-gather | bytes 589824 | tf_op jit(solution)/shard_map/all_gather | solution.py:138
  77.3 0.0 all-to-all-done.1.refs_3_
  77.3 10.5 %pair_tile.1 = (f32[4,2,2,8,32,128]{5,4,3,2,1,0:T(8,128)S(1)}, f32[1024,128]{1,0:T(8,128)}, f32[8,128]{1,0:T(8,128)S(1)}) custom-call(bf16[4,2,8,32,128]{4,3,2,1,0:T(8,128)(2,1)S(1)} %bitcast.14, bf16[4,2,8,32,128]{4,3,2,1,0:T(8,128)(2,1)S(1)} %bitcast.13, bf16[1024,128]{1,0:T(8,128)(2,1)S(1)} %all_gather.11.refs_2_, f32[8,8,640]{2,1,0:T(8,128)S(1)} %all-to-all-done.1.refs_3_), custom_call_target="tpu_custom_call" | custom-call | flops 3221225472 | bytes 4194304 | tf_op jit(solution)/shard_map/pair_tile/pallas_call | solution.py:68
  87.9 0.5 slice.17
  89.7 0.3 multiply_convert_fusion
  90.0 1.2 concatenate.10
  91.2 3.7 %all-to-all-start.2 = ((f16[8,520,128]{2,1,0:T(8,128)(2,1)}), f16[8,520,128]{2,1,0:T(8,128)(2,1)S(1)}, u32[]{:S(2)}, u32[]{:S(2)}) async-start(f16[8,520,128]{2,1,0:T(8,128)(2,1)} %concatenate.10), calls=%async_computation.2 | async-start | bytes 2129920 | tf_op jit(solution)/shard_map/all_to_all | solution.py:106
  94.9 0.0 reduce-scatter.2.cloned.1.call-start
  94.9 0.7 reduce-scatter.2.cloned.1.call-update
  95.6 15.4 %all-to-all-done.2 = f16[8,520,128]{2,1,0:T(8,128)(2,1)S(1)} async-done(((f16[8,520,128]{2,1,0:T(8,128)(2,1)}), f16[8,520,128]{2,1,0:T(8,128)(2,1)S(1)}, u32[]{:S(2)}, u32[]{:S(2)}) %all-to-all-start.2) | async-done | bytes 1064992 | tf_op jit(solution)/shard_map/all_to_all | solution.py:106
  111.0 0.1 convert_element_type.39
  111.2 0.6 slice_reduce_fusion
  112.5 0.2 fusion
  112.7 0.7 concatenate.11
  113.4 10.0 %all-to-all-start.3 = ((f16[16,40,128]{2,1,0:T(8,128)(2,1)}), f16[16,40,128]{2,1,0:T(8,128)(2,1)S(1)}, u32[]{:S(2)}, u32[]{:S(2)}) async-start(f16[16,40,128]{2,1,0:T(8,128)(2,1)} %concatenate.11), calls=%async_computation.3 | async-start | bytes 327680 | tf_op jit(solution)/shard_map/all_to_all | solution.py:106
  123.5 2.0 %reduce-scatter.2.cloned.1.call-done = f32[256,128]{1,0:T(8,128)} async-done(((f32[1024,128]{1,0:T(8,128)}), f32[256,128]{1,0:T(8,128)}) %reduce-scatter.2.cloned.1.call-update) | async-done | bytes 131088 | tf_op jit(solution)/shard_map/reduce_scatter | solution.py:143
  125.5 1.7 %broadcast_select_fusion = f32[256,128]{1,0:T(8,128)} fusion(f32[256,128]{1,0:T(8,128)} %reduce-scatter.2.cloned.1.call-done, pred[256]{0:T(512)(128)(4,1)S(1)} %compare_bitcast_fusion), kind=kLoop, calls=%fused_computation.8 | loop fusion | flops 32768 | bytes 262400 | tf_op jit(solution)/shard_map/jit(_where)/select_n | solution.py:144
  127.2 11.7 %all-to-all-done.3 = f16[16,40,128]{2,1,0:T(8,128)(2,1)S(1)} async-done(((f16[16,40,128]{2,1,0:T(8,128)(2,1)}), f16[16,40,128]{2,1,0:T(8,128)(2,1)S(1)}, u32[]{:S(2)}, u32[]{:S(2)}) %all-to-all-start.3) | async-done | bytes 163872 | tf_op jit(solution)/shard_map/all_to_all | solution.py:106
  138.9 0.2 fusion.4
  139.1 0.7 fusion.1
  (6 shorter events, 0.1 us)
Async XLA Ops:
  8.5 32.3 %all-to-all-start = ((bf16[16,32,128]{2,1,0:T(8,128)(2,1)}), bf16[16,32,128]{2,1,0:T(8,128)(2,1)S(1)}, u32[]{:S(2)}, u32[]{:S(2)}) async-start(bf16[16,32,128]{2,1,0:T(8,128)(2,1)} %broadcast_in_dim.36), calls=%async_computation | async-start | bytes 262144 | tf_op jit(solution)/shard_map/all_to_all | solution.py:99
  40.8 36.5 %all-to-all-start.1 = ((f32[8,8,640]{2,1,0:T(8,128)}), f32[8,8,640]{2,1,0:T(8,128)S(1)}, u32[]{:S(2)}, u32[]{:S(2)}) async-start(f32[8,8,640]{2,1,0:T(8,128)} %reshape.57), calls=%async_computation.1 | async-start | bytes 327680 | tf_op jit(solution)/shard_map/all_to_all | solution.py:135
  91.2 19.8 %all-to-all-start.2 = ((f16[8,520,128]{2,1,0:T(8,128)(2,1)}), f16[8,520,128]{2,1,0:T(8,128)(2,1)S(1)}, u32[]{:S(2)}, u32[]{:S(2)}) async-start(f16[8,520,128]{2,1,0:T(8,128)(2,1)} %concatenate.10), calls=%async_computation.2 | async-start | bytes 2129920 | tf_op jit(solution)/shard_map/all_to_all | solution.py:106
  94.9 30.6 %reduce-scatter.2.cloned.1.call-start = ((), (), s32[]{:S(2)}) async-start(), calls=%async_computation.5 | async-start | bytes 655360 | tf_op jit(solution)/shard_map/reduce_scatter | solution.py:143
  113.4 25.4 %all-to-all-start.3 = ((f16[16,40,128]{2,1,0:T(8,128)(2,1)}), f16[16,40,128]{2,1,0:T(8,128)(2,1)S(1)}, u32[]{:S(2)}, u32[]{:S(2)}) async-start(f16[16,40,128]{2,1,0:T(8,128)(2,1)} %concatenate.11), calls=%async_computation.3 | async-start | bytes 327680 | tf_op jit(solution)/shard_map/all_to_all | solution.py:106
Sparse Core Ops, SparseCore 0:
  98.5 26.9 reduce-scatter.1

commit v3 on v1

v3 whole, which is shorter than its diff:
```python
import jax
import jax.numpy as jnp
from jax import lax
from jax.experimental import pallas as pl
from jax.experimental.pallas import tpu as pltpu
from jax.sharding import Mesh
from jax.sharding import PartitionSpec as P

DOC_AXES = ("x", "zh", "c")
QUERY_AXES = ("y", "zl")
RING = ("zh", "zl")

SHARPNESS = 10.0
LOG2E = 1.4426950408889634
TOP = 14.0
EXPONENT_ROWS = 8
f32, f16, bf16 = jnp.float32, jnp.float16, jnp.bfloat16
HIGHEST = lax.Precision.HIGHEST


def pick(flag, one, two):
    return jnp.where(flag, one, two)


def table_body(nx, nzh, nc, ny, nzl, positives_ref, lengths_ref, z_ref, probs_ref, docs_ref, mine_ref, other_ref, d_ref, t_ref):
    row_docs, row_tokens = z_ref.shape
    row_queries = probs_ref.shape[0]
    rows = row_tokens // row_queries
    local_docs = row_docs // (ny * nzl)
    groups = row_queries // nc
    half = groups * rows
    me = lax.axis_index("c")
    first_doc = ((lax.axis_index("x") * nzh + lax.axis_index("zh")) * nc + me) * row_docs
    doc = first_doc + lax.broadcasted_iota(jnp.int32, probs_ref.shape, 1)
    query = lax.broadcasted_iota(jnp.int32, probs_ref.shape, 0)
    hit = jnp.zeros(probs_ref.shape, jnp.bool_)
    for i in range(row_queries):
        hit = hit | ((query == i) & (doc == positives_ref[i]))
    signal = probs_ref[...] - hit.astype(f32)

    z = z_ref[...] * LOG2E
    by_core = []
    for c in range(nc):
        columns = [z[:, (g * nc + c) * rows : (g * nc + c + 1) * rows] for g in range(groups)]
        one = (
            lax.broadcasted_iota(jnp.int32, (row_queries, 128), 0)
            == lax.broadcasted_iota(jnp.int32, (row_queries, 128), 1) * nc + c
        )
        turned = lax.dot_general(
            signal, one.astype(f32), (((0,), (0,)), ((), ())), preferred_element_type=f32, precision=HIGHEST
        )
        by_core.append((jnp.concatenate(columns, axis=1), turned))
    for out_ref, core in ((mine_ref, me), (other_ref, 1 - me)):
        for k in range(half // 128):
            t_ref[k] = pick(core == 0, *[b[0][:, k * 128 : (k + 1) * 128] for b in by_core])
        t_ref[half // 128] = pick(core == 0, by_core[0][1], by_core[1][1])
        tail = jnp.zeros((row_docs // local_docs, 128), f32)
        for e in range(local_docs):
            lines = [
                t_ref.at[k][pl.ds(e, row_docs // local_docs, stride=local_docs), :]
                for k in range(t_ref.shape[0])
            ]
            for k in range(half // 128):
                for y in range(ny):
                    out_ref[:, y, e * half + k * 128 : e * half + (k + 1) * 128] = lines[k][y * nzl : (y + 1) * nzl]
            part = lines[-1]
            tail = tail + (pltpu.roll(part, e * groups, 1) if e else part)
        for y in range(ny):
            out_ref[:, y, local_docs * half :] = tail[y * nzl : (y + 1) * nzl]

    length = docs_ref.shape[0] // local_docs
    for e in range(local_docs):
        block = docs_ref[e * length : (e + 1) * length, :].astype(f32)
        live = lax.broadcasted_iota(jnp.int32, block.shape, 0) < lengths_ref[e]
        d_ref[e * length : (e + 1) * length, :] = jnp.where(live, block, 0.0).astype(bf16)


def make_table(sizes, positives, lengths, normalizers, probs, documents):
    _, _, nc, ny, nzl = sizes
    row_docs, row_tokens = normalizers.shape
    half = row_tokens // nc
    local_docs = lengths.shape[0]
    shape = (nzl, ny, local_docs * half + 128)
    smem, vmem = pl.BlockSpec(memory_space=pltpu.SMEM), pl.BlockSpec(memory_space=pltpu.VMEM)
    return pl.pallas_call(
        lambda *refs: table_body(*sizes, *refs),
        in_specs=[smem, smem, vmem, vmem, vmem],
        out_specs=[vmem, vmem, vmem],
        out_shape=[
            jax.ShapeDtypeStruct(shape, f32),
            jax.ShapeDtypeStruct(shape, f32),
            jax.ShapeDtypeStruct(documents.shape, bf16),
        ],
        scratch_shapes=[pltpu.VMEM((half // 128 + 1, row_docs, 128), f32)],
        name="pair_table",
    )(positives, lengths, normalizers, probs, documents)


def tile_body(q_ref, d_ref, n_ref, qg_ref, mine_ref, other_ref, top_ref, dr_ref, w_ref):
    step = pl.program_id(0)
    ny, nc, local_slots, width = d_ref.shape
    pair, lines, _ = n_ref.shape
    nx, nzh, _, rows, _ = q_ref.shape
    groups = nx * nzh
    half = groups * rows
    tokens = pair * half
    local_docs = (n_ref.shape[2] - 128) // half
    length = local_slots // local_docs
    me = lax.axis_index("c")

    @pl.when(step == 0)
    def _():
        for r in range(nc):
            for y in range(ny):
                at = (r * ny + y) * local_slots
                dr_ref[at : at + local_slots, :] = d_ref[y, pick(r == 0, me, 1 - me)]

    q = jnp.transpose(q_ref[...], (2, 0, 1, 3, 4)).reshape(tokens, width)
    column = lax.broadcasted_iota(jnp.int32, (128, local_docs * half), 1) // rows
    spread = (column == lax.broadcasted_iota(jnp.int32, (128, local_docs * half), 0)).astype(f32)
    signal = jnp.dot(
        n_ref[:, :, local_docs * half :].reshape(pair * lines, 128),
        spread,
        preferred_element_type=f32,
        precision=HIGHEST,
    )
    for line in range(lines):
        for e in range(local_docs):
            at = (line * local_docs + e) * length
            here = slice(e * half, (e + 1) * half)
            d = dr_ref[at : at + length, :]
            s = lax.dot_general(d, q, (((1,), (1,)), ((), ())), preferred_element_type=f32)
            z = jnp.concatenate([n_ref[j, line : line + 1, here] for j in range(pair)], axis=1)
            p = jnp.concatenate(
                [signal[j * lines + line : j * lines + line + 1, here] for j in range(pair)], axis=1
            )
            t = jnp.minimum(s * (SHARPNESS * LOG2E) - z, 0.0)
            w_ref[at : at + length, :] = (jnp.exp2(t) * p).astype(bf16)
    w = w_ref[...]
    qg = lax.dot_general(w, dr_ref[...], (((0,), (0,)), ((), ())), preferred_element_type=f32)
    here = jnp.max(jnp.abs(qg).reshape(-1, 8, width), axis=0)
    qg = qg.reshape(pair, nx, nzh, rows, width)
    for j in range(pair):
        for x in range(nx):
            for zh in range(nzh):
                at = pl.multiple_of((zh * pl.num_programs(0) * pair + step * pair + j) * rows, rows)
                qg_ref[x, pl.ds(at, rows), :] = qg[j, x, zh]
    dg = jnp.dot(w, q, preferred_element_type=f32)
    own = mine_ref.shape[0]

    @pl.when(step == 0)
    def _():
        mine_ref[...] = dg[:own]
        other_ref[...] = dg[own:]
        top_ref[...] = here

    @pl.when(step > 0)
    def _():
        mine_ref[...] += dg[:own]
        other_ref[...] += dg[own:]
        top_ref[...] = jnp.maximum(top_ref[...], here)

    @pl.when(step == pl.num_programs(0) - 1)
    def _():
        largest = jnp.maximum(jnp.max(top_ref[...], keepdims=True), 1e-30)
        top = jnp.broadcast_to(jnp.ceil(jnp.log2(largest)), (1, width))
        piece = qg_ref.shape[1] - EXPONENT_ROWS
        factor = jnp.exp2(TOP - top)
        for x in range(nx):
            qg_ref[x, :piece, :] = qg_ref[x, :piece, :] * factor
            qg_ref[x, piece:, :] = jnp.broadcast_to(top, (EXPONENT_ROWS, width))


def tile_gradients(q, d, n):
    nx, nzh, nzl, rows, width = q.shape
    ny, nc, local_slots, _ = d.shape
    pair = 2
    slots = ny * nc * local_slots
    tokens = pair * nx * nzh * rows
    return pl.pallas_call(
        tile_body,
        grid=(nzl // pair,),
        in_specs=[
            pl.BlockSpec((nx, nzh, pair, rows, width), lambda i: (0, 0, i, 0, 0)),
            pl.BlockSpec(d.shape, lambda i: (0, 0, 0, 0)),
            pl.BlockSpec((pair, *n.shape[1:]), lambda i: (i, 0, 0)),
        ],
        out_specs=[
            pl.BlockSpec((nx, nzh * nzl * rows + EXPONENT_ROWS, width), lambda i: (0, 0, 0)),
            pl.BlockSpec((slots // nc, width), lambda i: (0, 0)),
            pl.BlockSpec((slots // nc, width), lambda i: (0, 0)),
        ],
        out_shape=[
            jax.ShapeDtypeStruct((nx, nzh * nzl * rows + EXPONENT_ROWS, width), f32),
            jax.ShapeDtypeStruct((slots // nc, width), f32),
            jax.ShapeDtypeStruct((slots // nc, width), f32),
        ],
        scratch_shapes=[
            pltpu.VMEM((8, width), f32),
            pltpu.VMEM((slots, width), bf16),
            pltpu.VMEM((slots, tokens), bf16),
        ],
        name="pair_tile",
        compiler_params=pltpu.CompilerParams(vmem_limit_bytes=48 * 1024 * 1024),
    )(q, d, n)


def exchange(x, axes):
    return lax.all_to_all(x, axes, split_axis=0, concat_axis=0, tiled=True)


def summed(sent, axes):
    got = exchange(sent, axes).astype(f32)
    tops = got[:, -EXPONENT_ROWS : 1 - EXPONENT_ROWS]
    return jnp.sum(got[:, :-EXPONENT_ROWS] * jnp.exp2(tops - TOP), axis=0), jnp.max(tops, axis=0)


def per_device(queries, documents, lengths, normalizers, probs, positives):
    sizes = tuple(lax.axis_size(a) for a in ("x", "zh", "c", "y", "zl"))
    nx, nzh, nc, ny, nzl = sizes
    nz = nzh * nzl
    rows, width = queries.shape
    length = documents.shape[0] // lengths.shape[0]

    q = exchange(jnp.broadcast_to(queries, (nz, rows, width)), RING).reshape(nz * rows, width)
    q = lax.all_gather(q, "x", tiled=True).reshape(nx, nzh, nzl, rows, width)

    mine, other, live_docs = make_table(sizes, positives, lengths, normalizers, probs, documents)
    swap = [(i, 1 - i) for i in range(nc)]
    table = jnp.concatenate([mine, lax.ppermute(other, "c", swap)], axis=1)
    table = exchange(table, "zl")
    d = lax.all_gather(live_docs, ("y", "c"), tiled=True).reshape(ny, nc, -1, width)

    qg, mine, other = tile_gradients(q, d, table)

    mine = (mine + lax.ppermute(other, "c", swap)).reshape(ny, -1, width)
    y = lax.axis_index("y")
    doc_grad = lax.dynamic_index_in_dim(mine, y, 0, keepdims=False)
    for k in range(1, ny):
        away = lax.dynamic_index_in_dim(mine, lax.rem(y + k, ny), 0, keepdims=False)
        doc_grad = doc_grad + lax.ppermute(away, "y", [(i, (i + k) % ny) for i in range(ny)])
    live = (jnp.arange(length, dtype=jnp.int32)[None, :] < lengths[:, None]).reshape(-1, 1)
    doc_grad = jnp.where(live, doc_grad, 0.0)

    total, top = summed(qg.astype(f16), "x")
    top = top + (nx - 1).bit_length()
    sent = (total * jnp.exp2(TOP - top)).reshape(nz, rows, width)
    sent = jnp.concatenate([sent, jnp.broadcast_to(top, (nz, EXPONENT_ROWS, width))], axis=1)
    query_grad, _ = summed(sent.astype(f16), RING)
    return query_grad, doc_grad


def solution(mesh):
    split = Mesh(mesh.devices.reshape(4, 2, 2, 4, 8), ("x", "zh", "c", "y", "zl"))
    return jax.shard_map(
        per_device,
        mesh=split,
        in_specs=(
            P((*QUERY_AXES, *DOC_AXES), None),
            P((*DOC_AXES, *QUERY_AXES), None),
            P((*DOC_AXES, *QUERY_AXES)),
            P(DOC_AXES, QUERY_AXES),
            P(QUERY_AXES, DOC_AXES),
            P(QUERY_AXES),
        ),
        out_specs=(P((*QUERY_AXES, *DOC_AXES), None), P((*DOC_AXES, *QUERY_AXES), None)),
        check_vma=False,
    )
```

time: 139 us -> 113 us (0.81)
  the two profiles are of different devices: /device:TPU:8 before, /device:TPU:32 now
where the time goes in v3:
time: 113 us
  starting transfers between devices  46.6 us (41%)
  blocking collectives  27 us (24%)
  waiting for transfers between devices  21 us (19%)
  Pallas kernels  11.1 us (10%)
  other arithmetic  4.94 us (4%)
  local copies, waits for them, and re-layouts  1.42 us (1%)
    all_to_all x4, starting transfers between devices, exchange(): return lax.all_to_all(x, axes, split_axis=0, concat_axis=0, tiled=True)  33.7 us
    all_gather x1, blocking collectives, per_device(): lax.all_gather(live_docs, ('y', 'c'), tiled=True).reshape(ny, nc, -1, width)  13.8 us
    all_to_all x4, waiting for transfers between devices, exchange(): return lax.all_to_all(x, axes, split_axis=0, concat_axis=0, tiled=True)  13.5 us
    all_gather x1, blocking collectives, per_device(): q = lax.all_gather(q, 'x', tiled=True).reshape(nx, nzh, nzl, rows, width)  13.2 us
    ppermute x3, starting transfers between devices, per_device(): lax.ppermute(away, 'y', [(i, (i + k) % ny) for i in range(ny)])  9.09 us
    pallas_call x1, Pallas kernels, tile_gradients(): pl.pallas_call(tile_body, grid=(nzl // pair,), in_specs=[pl.BlockSpec((nx...  9.05 us
    ppermute x3, waiting for transfers between devices, per_device(): lax.ppermute(away, 'y', [(i, (i + k) % ny) for i in range(ny)])  6.06 us
  transfers between devices with their start and end apart: 9, of which 5 were waited for; matrix products, arithmetic and copies ran while one was open for 3% of the time, Pallas kernels for 2%

profile of v3, /device:TPU:32, one launch (start us, length us, event | category | flops | bytes accessed | tf_op | source)
XLA Modules:
  0.0 112.8 jit_solution(3272489420191605113)
XLA Ops:
  0.6 1.4 %broadcast_in_dim.22 = bf16[16,32,128]{2,1,0:T(8,128)(2,1)} broadcast(bf16[32,128]{1,0:T(8,128)(2,1)} %param.6), dimensions={1,2} | broadcast | bytes 139264 | tf_op jit(solution)/shard_map/broadcast_in_dim | solution.py:225
  2.0 15.2 %all-to-all-start = ((bf16[16,32,128]{2,1,0:T(8,128)(2,1)}), bf16[16,32,128]{2,1,0:T(8,128)(2,1)S(1)}, u32[]{:S(2)}, u32[]{:S(2)}) async-start(bf16[16,32,128]{2,1,0:T(8,128)(2,1)} %broadcast_in_dim.22), calls=%async_computation | async-start | bytes 262144 | tf_op jit(solution)/shard_map/all_to_all | solution.py:209
  17.2 2.0 %pair_table.1 = (f32[8,4,640]{2,1,0:T(4,128)}, f32[8,4,640]{2,1,0:T(4,128)}, bf16[256,128]{1,0:T(8,128)(2,1)}) custom-call(s32[16]{0:T(128)} %refs_0_.1, s32[2]{0:T(128)} %refs_1_.1, f32[64,512]{1,0:T(8,128)} %refs_2_.1, f32[16,64]{1,0:T(8,128)} %refs_3_.1, bf16[256,128]{1,0:T(8,128)(2,1)} %refs_4_.1), custom_call_target="tpu_custom_call" | custom-call | tf_op jit(solution)/shard_map/pair_table/pallas_call | solution.py:85
  19.2 1.9 %collective-permute-start = (f32[8,4,640]{2,1,0:T(4,128)}, f32[8,4,640]{2,1,0:T(4,128)S(1)}, u32[]{:S(2)}, u32[]{:S(2)}) collective-permute-start(f32[8,4,640]{2,1,0:T(4,128)} %get-tuple-element.10), channel_id=1, source_target_pairs={{0,32},{32,0},{1,33},{33,1},{2,34},{34,2},{3,35},{35,3},{4,36},{36... | collective-permute-start | bytes 245768 | tf_op jit(solution)/shard_map/ppermute | solution.py:230
  21.2 1.5 %collective-permute-done = f32[8,4,640]{2,1,0:T(4,128)S(1)} collective-permute-done((f32[8,4,640]{2,1,0:T(4,128)}, f32[8,4,640]{2,1,0:T(4,128)S(1)}, u32[]{:S(2)}, u32[]{:S(2)}) %collective-permute-start) | collective-permute-done | bytes 81952 | tf_op jit(solution)/shard_map/ppermute | solution.py:230
  22.6 1.6 %pad_maximum_fusion = f32[8,8,640]{2,1,0:T(8,128)} fusion(f32[8,4,640]{2,1,0:T(4,128)S(1)} %collective-permute-done, f32[8,4,640]{2,1,0:T(4,128)} %get-tuple-element.9), kind=kLoop, calls=%fused_computation.5 | loop fusion | flops 40960 | bytes 327680 | tf_op jit(solution)/shard_map/concatenate | solution.py:230
  24.2 7.2 %all-to-all-done = bf16[16,32,128]{2,1,0:T(8,128)(2,1)S(1)} async-done(((bf16[16,32,128]{2,1,0:T(8,128)(2,1)}), bf16[16,32,128]{2,1,0:T(8,128)(2,1)S(1)}, u32[]{:S(2)}, u32[]{:S(2)}) %all-to-all-start) | async-done | bytes 131104 | tf_op jit(solution)/shard_map/all_to_all | solution.py:209
  31.4 4.3 %all-to-all-start.1 = ((f32[8,8,640]{2,1,0:T(8,128)}), f32[8,8,640]{2,1,0:T(8,128)S(1)}, u32[]{:S(2)}, u32[]{:S(2)}) async-start(f32[8,8,640]{2,1,0:T(8,128)} %pad_maximum_fusion), calls=%async_computation.1 | async-start | bytes 327680 | tf_op jit(solution)/shard_map/all_to_all | solution.py:209
  35.7 13.8 %all_gather.7 = bf16[2048,128]{1,0:T(8,128)(2,1)S(1)} all-gather(bf16[256,128]{1,0:T(8,128)(2,1)} %get-tuple-element.8), channel_id=1, replica_groups=mesh['x'=4,'zh'=2,'c'=2,'y'=4,'zl'=8] {'y','c'}, dimensions={0}, use_global_device_ids=true | all-gather | bytes 589824 | tf_op jit(solution)/shard_map/all_gather | solution.py:232
  49.6 13.2 %all_gather.6 = bf16[2048,128]{1,0:T(8,128)(2,1)S(1)} all-gather(bf16[512,128]{1,0:T(8,128)(2,1)S(1)} %bitcast.28), channel_id=1, replica_groups=mesh['x'=4,'zh'=2,'c'=2,'y'=4,'zl'=8] {'x'}, dimensions={0}, use_global_device_ids=true | all-gather | bytes 655360 | tf_op jit(solution)/shard_map/all_gather | solution.py:226
  62.8 0.0 all-to-all-done.1.n_ref
  62.8 9.1 %pair_tile.1 = (f32[4,520,128]{2,1,0:T(8,128)S(1)}, f32[1024,128]{1,0:T(8,128)S(1)}, f32[1024,128]{1,0:T(8,128)S(1)}) custom-call(bf16[4,2,8,32,128]{4,3,2,1,0:T(8,128)(2,1)S(1)} %bitcast.24, bf16[4,2,256,128]{3,2,1,0:T(8,128)(2,1)S(1)} %bitcast.23, f32[8,8,640]{2,1,0:T(8,128)S(1)} %all-to-all-done.1.n_ref), custom_call_target="tpu_custom_call" | custom-call | tf_op jit(solution)/shard_map/pair_tile/pallas_call | solution.py:180
  71.8 0.9 convert_element_type.10
  72.7 4.3 %all-to-all-start.2 = ((f16[4,520,128]{2,1,0:T(8,128)(2,1)}), f16[4,520,128]{2,1,0:T(8,128)(2,1)S(1)}, u32[]{:S(2)}, u32[]{:S(2)}) async-start(f16[4,520,128]{2,1,0:T(8,128)(2,1)} %convert_element_type.10), calls=%async_computation.2 | async-start | bytes 1064960 | tf_op jit(solution)/shard_map/all_to_all | solution.py:209
  77.0 1.9 %collective-permute-start.1 = (f32[1024,128]{1,0:T(8,128)S(1)}, f32[1024,128]{1,0:T(8,128)S(1)}, u32[]{:S(2)}, u32[]{:S(2)}) collective-permute-start(f32[1024,128]{1,0:T(8,128)S(1)} %get-tuple-element.13), channel_id=1, source_target_pairs={{0,32},{32,0},{1,33},{33,1},{2,34},{34,2},{3,35},{35,3},{4,36},{36... | collective-permute-start | bytes 1572872 | tf_op jit(solution)/shard_map/ppermute | solution.py:236
  78.9 6.2 %all-to-all-done.2 = f16[4,520,128]{2,1,0:T(8,128)(2,1)S(1)} async-done(((f16[4,520,128]{2,1,0:T(8,128)(2,1)}), f16[4,520,128]{2,1,0:T(8,128)(2,1)S(1)}, u32[]{:S(2)}, u32[]{:S(2)}) %all-to-all-start.2) | async-done | bytes 532512 | tf_op jit(solution)/shard_map/all_to_all | solution.py:209
  85.1 0.1 convert_element_type.11
  85.2 0.1 fusion
  85.3 0.7 pad_maximum_fusion.1
  86.0 9.9 %all-to-all-start.3 = ((f16[16,40,128]{2,1,0:T(8,128)(2,1)}), f16[16,40,128]{2,1,0:T(8,128)(2,1)S(1)}, u32[]{:S(2)}, u32[]{:S(2)}) async-start(f16[16,40,128]{2,1,0:T(8,128)(2,1)} %pad_maximum_fusion.1), calls=%async_computation.3 | async-start | bytes 327680 | tf_op jit(solution)/shard_map/all_to_all | solution.py:209
  96.0 0.0 collective-permute-done.1
  96.0 0.0 copy-start
  96.0 0.1 add.51
  96.1 4.4 %collective-permute-start.4 = (f32[256,128]{1,0:T(8,128)S(1)}, f32[256,128]{1,0:T(8,128)S(1)}, u32[]{:S(2)}, u32[]{:S(2)}) collective-permute-start(f32[256,128]{1,0:T(8,128)S(1)} %get-tuple-element.17), channel_id=1, source_target_pairs={{0,24},{8,0},{16,8},{24,16},{1,25},{9,1},{17,9},{25,17},{2,26},{10... | collective-permute-start | bytes 393224 | tf_op jit(solution)/shard_map/ppermute | solution.py:241
  100.5 2.8 %collective-permute-start.3 = (f32[256,128]{1,0:T(8,128)S(1)}, f32[256,128]{1,0:T(8,128)S(1)}, u32[]{:S(2)}, u32[]{:S(2)}) collective-permute-start(f32[256,128]{1,0:T(8,128)S(1)} %get-tuple-element.18), channel_id=1, source_target_pairs={{0,16},{8,24},{16,0},{24,8},{1,17},{9,25},{17,1},{25,9},{2,18},{10... | collective-permute-start | bytes 393224 | tf_op jit(solution)/shard_map/ppermute | solution.py:241
  103.3 1.9 %collective-permute-start.2 = (f32[256,128]{1,0:T(8,128)S(1)}, f32[256,128]{1,0:T(8,128)S(1)}, u32[]{:S(2)}, u32[]{:S(2)}) collective-permute-start(f32[256,128]{1,0:T(8,128)S(1)} %get-tuple-element.16), channel_id=1, source_target_pairs={{0,8},{8,16},{16,24},{24,0},{1,9},{9,17},{17,25},{25,1},{2,10},{10... | collective-permute-start | bytes 393224 | tf_op jit(solution)/shard_map/ppermute | solution.py:241
  105.2 0.0 copy-done
  105.2 0.1 compare_bitcast_fusion
  105.3 0.0 collective-permute-done.4
  105.3 3.6 %collective-permute-done.3 = f32[256,128]{1,0:T(8,128)S(1)} collective-permute-done((f32[256,128]{1,0:T(8,128)S(1)}, f32[256,128]{1,0:T(8,128)S(1)}, u32[]{:S(2)}, u32[]{:S(2)}) %collective-permute-start.3) | collective-permute-done | bytes 131104 | tf_op jit(solution)/shard_map/ppermute | solution.py:241
  108.9 2.5 %collective-permute-done.2 = f32[256,128]{1,0:T(8,128)S(1)} collective-permute-done((f32[256,128]{1,0:T(8,128)S(1)}, f32[256,128]{1,0:T(8,128)S(1)}, u32[]{:S(2)}, u32[]{:S(2)}) %collective-permute-start.2) | collective-permute-done | bytes 131104 | tf_op jit(solution)/shard_map/ppermute | solution.py:241
  111.3 0.8 fusion.4
  112.1 0.0 all-to-all-done.3
  112.2 0.6 fusion.1
  (7 shorter events, 0.2 us)
Async XLA Ops:
  2.0 29.4 %all-to-all-start = ((bf16[16,32,128]{2,1,0:T(8,128)(2,1)}), bf16[16,32,128]{2,1,0:T(8,128)(2,1)S(1)}, u32[]{:S(2)}, u32[]{:S(2)}) async-start(bf16[16,32,128]{2,1,0:T(8,128)(2,1)} %broadcast_in_dim.22), calls=%async_computation | async-start | bytes 262144 | tf_op jit(solution)/shard_map/all_to_all | solution.py:209
  19.2 3.4 %collective-permute-start = (f32[8,4,640]{2,1,0:T(4,128)}, f32[8,4,640]{2,1,0:T(4,128)S(1)}, u32[]{:S(2)}, u32[]{:S(2)}) collective-permute-start(f32[8,4,640]{2,1,0:T(4,128)} %get-tuple-element.10), channel_id=1, source_target_pairs={{0,32},{32,0},{1,33},{33,1},{2,34},{34,2},{3,35},{35,3},{4,36},{36... | collective-permute-start | bytes 245768 | tf_op jit(solution)/shard_map/ppermute | solution.py:230
  31.4 31.3 %all-to-all-start.1 = ((f32[8,8,640]{2,1,0:T(8,128)}), f32[8,8,640]{2,1,0:T(8,128)S(1)}, u32[]{:S(2)}, u32[]{:S(2)}) async-start(f32[8,8,640]{2,1,0:T(8,128)} %pad_maximum_fusion), calls=%async_computation.1 | async-start | bytes 327680 | tf_op jit(solution)/shard_map/all_to_all | solution.py:209
  72.7 12.4 %all-to-all-start.2 = ((f16[4,520,128]{2,1,0:T(8,128)(2,1)}), f16[4,520,128]{2,1,0:T(8,128)(2,1)S(1)}, u32[]{:S(2)}, u32[]{:S(2)}) async-start(f16[4,520,128]{2,1,0:T(8,128)(2,1)} %convert_element_type.10), calls=%async_computation.2 | async-start | bytes 1064960 | tf_op jit(solution)/shard_map/all_to_all | solution.py:209
  77.0 19.0 %collective-permute-start.1 = (f32[1024,128]{1,0:T(8,128)S(1)}, f32[1024,128]{1,0:T(8,128)S(1)}, u32[]{:S(2)}, u32[]{:S(2)}) collective-permute-start(f32[1024,128]{1,0:T(8,128)S(1)} %get-tuple-element.13), channel_id=1, source_target_pairs={{0,32},{32,0},{1,33},{33,1},{2,34},{34,2},{3,35},{35,3},{4,36},{36... | collective-permute-start | bytes 1572872 | tf_op jit(solution)/shard_map/ppermute | solution.py:236
  86.0 26.1 %all-to-all-start.3 = ((f16[16,40,128]{2,1,0:T(8,128)(2,1)}), f16[16,40,128]{2,1,0:T(8,128)(2,1)S(1)}, u32[]{:S(2)}, u32[]{:S(2)}) async-start(f16[16,40,128]{2,1,0:T(8,128)(2,1)} %pad_maximum_fusion.1), calls=%async_computation.3 | async-start | bytes 327680 | tf_op jit(solution)/shard_map/all_to_all | solution.py:209
  96.0 9.2 %copy-start = (s32[2]{0:T(128)S(1)}, s32[2]{0:T(128)}, u32[]{:S(2)}) copy-start(s32[2]{0:T(128)} %refs_1_.1) | copy-start | bytes 28
  96.1 9.2 %collective-permute-start.4 = (f32[256,128]{1,0:T(8,128)S(1)}, f32[256,128]{1,0:T(8,128)S(1)}, u32[]{:S(2)}, u32[]{:S(2)}) collective-permute-start(f32[256,128]{1,0:T(8,128)S(1)} %get-tuple-element.17), channel_id=1, source_target_pairs={{0,24},{8,0},{16,8},{24,16},{1,25},{9,1},{17,9},{25,17},{2,26},{10... | collective-permute-start | bytes 393224 | tf_op jit(solution)/shard_map/ppermute | solution.py:241
  100.5 8.4 %collective-permute-start.3 = (f32[256,128]{1,0:T(8,128)S(1)}, f32[256,128]{1,0:T(8,128)S(1)}, u32[]{:S(2)}, u32[]{:S(2)}) collective-permute-start(f32[256,128]{1,0:T(8,128)S(1)} %get-tuple-element.18), channel_id=1, source_target_pairs={{0,16},{8,24},{16,0},{24,8},{1,17},{9,25},{17,1},{25,9},{2,18},{10... | collective-permute-start | bytes 393224 | tf_op jit(solution)/shard_map/ppermute | solution.py:241
  103.3 8.1 %collective-permute-start.2 = (f32[256,128]{1,0:T(8,128)S(1)}, f32[256,128]{1,0:T(8,128)S(1)}, u32[]{:S(2)}, u32[]{:S(2)}) collective-permute-start(f32[256,128]{1,0:T(8,128)S(1)} %get-tuple-element.16), channel_id=1, source_target_pairs={{0,8},{8,16},{16,24},{24,0},{1,9},{9,17},{17,25},{25,1},{2,10},{10... | collective-permute-start | bytes 393224 | tf_op jit(solution)/shard_map/ppermute | solution.py:241

commit v4 on v3

v4 whole, which is shorter than its diff:
```python
import jax
import jax.numpy as jnp
from jax import lax
from jax.experimental import pallas as pl
from jax.experimental.pallas import tpu as pltpu
from jax.sharding import Mesh
from jax.sharding import PartitionSpec as P

DOC_AXES = ("x", "zh", "c")
QUERY_AXES = ("y", "zl")
RING = ("zh", "zl")

SHARPNESS = 10.0
LOG2E = 1.4426950408889634
TOP = 14.0
EXPONENT_ROWS = 8
MIB = 1024 * 1024
f32, f16, bf16 = jnp.float32, jnp.float16, jnp.bfloat16
HIGHEST = lax.Precision.HIGHEST


def mask_body(lengths_ref, docs_ref, d_ref):
    local_docs = lengths_ref.shape[0]
    length = docs_ref.shape[0] // local_docs
    for e in range(local_docs):
        block = docs_ref[e * length : (e + 1) * length, :].astype(f32)
        live = lax.broadcasted_iota(jnp.int32, block.shape, 0) < lengths_ref[e]
        d_ref[e * length : (e + 1) * length, :] = jnp.where(live, block, 0.0).astype(bf16)


def without_padding(documents, lengths):
    smem, vmem = pl.BlockSpec(memory_space=pltpu.SMEM), pl.BlockSpec(memory_space=pltpu.VMEM)
    return pl.pallas_call(
        mask_body,
        in_specs=[smem, vmem],
        out_specs=vmem,
        out_shape=jax.ShapeDtypeStruct(documents.shape, bf16),
        name="live_documents",
        compiler_params=pltpu.CompilerParams(vmem_limit_bytes=12 * MIB),
    )(lengths, documents)


def table_body(nx, nzh, nc, ny, nzl, positives_ref, z_ref, probs_ref, after_ref, out_ref, t_ref):
    row_docs, row_tokens = z_ref.shape
    row_queries = probs_ref.shape[0]
    rows = row_tokens // row_queries
    local_docs = row_docs // (ny * nzl)
    groups = row_queries // nc
    half = groups * rows
    chunks = half // 128
    first_doc = ((lax.axis_index("x") * nzh + lax.axis_index("zh")) * nc + lax.axis_index("c")) * row_docs
    doc = first_doc + lax.broadcasted_iota(jnp.int32, probs_ref.shape, 1)
    query = lax.broadcasted_iota(jnp.int32, probs_ref.shape, 0)
    hit = jnp.zeros(probs_ref.shape, jnp.bool_)
    for i in range(row_queries):
        hit = hit | ((query == i) & (doc == positives_ref[i]))
    signal = probs_ref[...] - hit.astype(f32)

    z = z_ref[...] * LOG2E
    count = row_docs // local_docs
    for c in range(nc):
        columns = [z[:, (g * nc + c) * rows : (g * nc + c + 1) * rows] for g in range(groups)]
        columns = jnp.concatenate(columns, axis=1)
        one = (
            lax.broadcasted_iota(jnp.int32, (row_queries, 128), 0)
            == lax.broadcasted_iota(jnp.int32, (row_queries, 128), 1) * nc + c
        )
        turned = lax.dot_general(
            signal, one.astype(f32), (((0,), (0,)), ((), ())), preferred_element_type=f32, precision=HIGHEST
        )
        for k in range(chunks):
            t_ref[c, k] = columns[:, k * 128 : (k + 1) * 128]
        t_ref[c, chunks] = turned
        tail = jnp.zeros((count, 128), f32)
        for e in range(local_docs):
            lines = [t_ref.at[c, k][pl.ds(e, count, stride=local_docs), :] for k in range(chunks + 1)]
            for k in range(chunks):
                for y in range(ny):
                    at = e * half + k * 128
                    out_ref[:, c, y, at : at + 128] = lines[k][y * nzl : (y + 1) * nzl]
            tail = tail + (pltpu.roll(lines[chunks], e * groups, 1) if e else lines[chunks])
        for y in range(ny):
            out_ref[:, c, y, local_docs * half :] = tail[y * nzl : (y + 1) * nzl]


def make_table(sizes, positives, normalizers, probs, after):
    _, _, nc, ny, nzl = sizes
    row_docs, row_tokens = normalizers.shape
    half = row_tokens // nc
    local_docs = row_docs // (ny * nzl)
    smem, vmem = pl.BlockSpec(memory_space=pltpu.SMEM), pl.BlockSpec(memory_space=pltpu.VMEM)
    return pl.pallas_call(
        lambda *refs: table_body(*sizes, *refs),
        in_specs=[smem, vmem, vmem, pl.BlockSpec(memory_space=pl.ANY)],
        out_specs=vmem,
        out_shape=jax.ShapeDtypeStruct((nzl, nc, ny, local_docs * half + 128), f32),
        scratch_shapes=[pltpu.VMEM((nc, half // 128 + 1, row_docs, 128), f32)],
        name="pair_table",
        compiler_params=pltpu.CompilerParams(vmem_limit_bytes=12 * MIB),
    )(positives, normalizers, probs, after)


def tile_body(own, q_ref, d_ref, n_ref, *refs):
    prior_ref = refs[0] if own else None
    qg_ref, dg_ref, top_ref, dr_ref, w_ref = refs[1 if own else 0 :]
    step = pl.program_id(0)
    ny, nc, local_slots, width = d_ref.shape
    pair, _, lines, _ = n_ref.shape
    nx, nzh, _, rows, _ = q_ref.shape
    half = nx * nzh * rows
    tokens = pair * half
    local_docs = (n_ref.shape[3] - 128) // half
    length = local_slots // local_docs
    me = lax.axis_index("c")
    core = me if own else 1 - me

    @pl.when(step == 0)
    def _():
        for y in range(ny):
            dr_ref[y * local_slots : (y + 1) * local_slots, :] = d_ref[y, core]

    q = jnp.transpose(q_ref[...], (2, 0, 1, 3, 4)).reshape(tokens, width)
    n = [n_ref[j, core] for j in range(pair)]
    column = lax.broadcasted_iota(jnp.int32, (128, local_docs * half), 1) // rows
    spread = (column == lax.broadcasted_iota(jnp.int32, (128, local_docs * half), 0)).astype(f32)
    signal = jnp.dot(
        jnp.concatenate([v[:, local_docs * half :] for v in n], axis=0),
        spread,
        preferred_element_type=f32,
        precision=HIGHEST,
    )
    for line in range(lines):
        for e in range(local_docs):
            at = (line * local_docs + e) * length
            here = slice(e * half, (e + 1) * half)
            d = dr_ref[at : at + length, :]
            s = lax.dot_general(d, q, (((1,), (1,)), ((), ())), preferred_element_type=f32)
            z = jnp.concatenate([v[line : line + 1, here] for v in n], axis=1)
            p = jnp.concatenate(
                [signal[j * lines + line : j * lines + line + 1, here] for j in range(pair)], axis=1
            )
            t = jnp.minimum(s * (SHARPNESS * LOG2E) - z, 0.0)
            w_ref[at : at + length, :] = (jnp.exp2(t) * p).astype(bf16)
    w = w_ref[...]
    qg = lax.dot_general(w, dr_ref[...], (((0,), (0,)), ((), ())), preferred_element_type=f32)
    qg = qg.reshape(pair, nx, nzh, rows, width)
    largest = jnp.zeros((8, width), f32)
    for j in range(pair):
        for x in range(nx):
            for zh in range(nzh):
                at = pl.multiple_of((zh * pl.num_programs(0) * pair + step * pair + j) * rows, rows)
                block = qg[j, x, zh]
                if own:
                    block = block + prior_ref[x, pl.ds(at, rows), :]
                    largest = jnp.maximum(largest, jnp.max(jnp.abs(block).reshape(-1, 8, width), axis=0))
                qg_ref[x, pl.ds(at, rows), :] = block
    dg = jnp.dot(w, q, preferred_element_type=f32)

    @pl.when(step == 0)
    def _():
        dg_ref[...] = dg
        top_ref[...] = largest

    @pl.when(step > 0)
    def _():
        dg_ref[...] += dg
        top_ref[...] = jnp.maximum(top_ref[...], largest)


def tile_gradients(q, d, n, prior=None):
    nx, nzh, nzl, rows, width = q.shape
    ny, nc, local_slots, _ = d.shape
    pair = 2
    slots = ny * local_slots
    own = prior is not None
    piece = nzh * nzl * rows
    whole = pl.BlockSpec((nx, piece, width), lambda i: (0, 0, 0))
    return pl.pallas_call(
        lambda *refs: tile_body(own, *refs),
        grid=(nzl // pair,),
        in_specs=[
            pl.BlockSpec((nx, nzh, pair, rows, width), lambda i: (0, 0, i, 0, 0)),
            pl.BlockSpec(d.shape, lambda i: (0, 0, 0, 0)),
            pl.BlockSpec((pair, *n.shape[1:]), lambda i: (i, 0, 0, 0)),
            *([whole] if own else []),
        ],
        out_specs=[
            whole,
            pl.BlockSpec((slots, width), lambda i: (0, 0)),
            pl.BlockSpec((8, width), lambda i: (0, 0)),
        ],
        out_shape=[
            jax.ShapeDtypeStruct((nx, piece, width), f32),
            jax.ShapeDtypeStruct((slots, width), f32),
            jax.ShapeDtypeStruct((8, width), f32),
        ],
        scratch_shapes=[
            pltpu.VMEM((slots, width), bf16),
            pltpu.VMEM((slots, pair * nx * nzh * rows), bf16),
        ],
        name="own_documents" if own else "other_documents",
        compiler_params=pltpu.CompilerParams(vmem_limit_bytes=20 * MIB),
        cost_estimate=pl.CostEstimate(
            flops=6 * nx * piece * slots * width,
            bytes_accessed=8 * nx * piece * width,
            transcendentals=nx * piece * slots,
        ),
    )(q, d, n, *([prior] if own else []))


def neighbours(y, ny):
    return y + 1 - 2 * (y % 2), ny - 1 - y


def after_tile_body(ny, qg_ref, top_ref, mine_ref, other_ref, sent_ref, give_ref, keep_ref):
    nx, piece, width = qg_ref.shape
    most = jnp.maximum(jnp.max(top_ref[...], keepdims=True), 1e-30)
    top = jnp.broadcast_to(jnp.ceil(jnp.log2(most)), (1, width))
    factor = jnp.exp2(TOP - top)
    for x in range(nx):
        sent_ref[x, :piece, :] = qg_ref[x] * factor
        sent_ref[x, piece:, :] = jnp.broadcast_to(top, (EXPONENT_ROWS, width))
    block = mine_ref.shape[0] // ny
    y = lax.axis_index("y")
    first, second = neighbours(y, ny)
    for ref, owners in ((give_ref, (first, neighbours(first, ny)[1])), (keep_ref, (y, second))):
        for i, owner in enumerate(owners):
            rows = pl.ds(pl.multiple_of(owner * block, block), block)
            ref[i] = mine_ref[rows, :] + other_ref[rows, :]


def after_tile(ny, qg, top, mine, other):
    nx, piece, width = qg.shape
    block = mine.shape[0] // ny
    vmem = pl.BlockSpec(memory_space=pltpu.VMEM)
    return pl.pallas_call(
        lambda *refs: after_tile_body(ny, *refs),
        in_specs=[vmem] * 4,
        out_specs=[vmem] * 3,
        out_shape=[
            jax.ShapeDtypeStruct((nx, piece + EXPONENT_ROWS, width), f32),
            jax.ShapeDtypeStruct((2, block, width), f32),
            jax.ShapeDtypeStruct((2, block, width), f32),
        ],
        name="scale_pieces",
        compiler_params=pltpu.CompilerParams(vmem_limit_bytes=12 * MIB),
    )(qg, top, mine, other)


def after_x_body(spare, got_ref, keep_ref, came_ref, sent_ref, give_ref, own_ref):
    nx, lines, width = got_ref.shape
    nz, rows = sent_ref.shape[0], sent_ref.shape[1] - EXPONENT_ROWS
    tops = [got_ref[x, lines - EXPONENT_ROWS : lines, :][:1] for x in range(nx)]
    top = tops[0]
    for t in tops[1:]:
        top = jnp.maximum(top, t)
    top = top + spare
    factors = [jnp.exp2(t - top) for t in tops]
    for k in range(nz):
        here = slice(k * rows, (k + 1) * rows)
        total = got_ref[0, here, :] * factors[0]
        for x in range(1, nx):
            total = total + got_ref[x, here, :] * factors[x]
        sent_ref[k, :rows, :] = total
        sent_ref[k, rows:, :] = jnp.broadcast_to(top, (EXPONENT_ROWS, width))
    own_ref[...] = keep_ref[0] + came_ref[0]
    give_ref[...] = keep_ref[1] + came_ref[1]


def after_x(nz, got, keep, came):
    nx, lines, width = got.shape
    rows = (lines - EXPONENT_ROWS) // nz
    block = keep.shape[1]
    vmem = pl.BlockSpec(memory_space=pltpu.VMEM)
    return pl.pallas_call(
        lambda *refs: after_x_body(float((nx - 1).bit_length()), *refs),
        in_specs=[vmem] * 3,
        out_specs=[vmem] * 3,
        out_shape=[
            jax.ShapeDtypeStruct((nz, rows + EXPONENT_ROWS, width), f32),
            jax.ShapeDtypeStruct((block, width), f32),
            jax.ShapeDtypeStruct((block, width), f32),
        ],
        name="sum_pieces",
        compiler_params=pltpu.CompilerParams(vmem_limit_bytes=12 * MIB),
    )(got, keep, came)


def exchange(x, axes):
    return lax.all_to_all(x, axes, split_axis=0, concat_axis=0, tiled=True)


def per_device(queries, documents, lengths, normalizers, probs, positives):
    sizes = tuple(lax.axis_size(a) for a in ("x", "zh", "c", "y", "zl"))
    nx, nzh, nc, ny, nzl = sizes
    nz = nzh * nzl
    rows, width = queries.shape
    length = documents.shape[0] // lengths.shape[0]

    q = exchange(jnp.broadcast_to(queries, (nz, rows, width)), RING).reshape(nz * rows, width)
    q = lax.all_gather(q, "x", tiled=True).reshape(nx, nzh, nzl, rows, width)

    d = lax.all_gather(without_padding(documents, lengths), ("y", "c"), tiled=True)
    table = make_table(sizes, positives, normalizers, probs, d)
    table = exchange(table.reshape(nzl * nc, *table.shape[2:]), ("zl", "c")).reshape(table.shape)
    d = d.reshape(ny, nc, -1, width)

    part, other, _ = tile_gradients(q, d, table)
    other = lax.ppermute(other, "c", [(i, 1 - i) for i in range(nc)])
    qg, mine, top = tile_gradients(q, d, table, part)

    pairs = [neighbours(i, ny) for i in range(ny)]
    sent, give, keep = after_tile(ny, qg, top, mine, other)
    came = lax.ppermute(give, "y", [(i, int(p[0])) for i, p in enumerate(pairs)])
    got = exchange(sent.astype(f16), "x").astype(f32)
    sent, give, own = after_x(nz, got, keep, came)
    came = lax.ppermute(give, "y", [(i, int(p[1])) for i, p in enumerate(pairs)])
    got = exchange(sent.astype(f16), RING).astype(f32)
    tops = got[:, -EXPONENT_ROWS : 1 - EXPONENT_ROWS]
    query_grad = jnp.sum(got[:, :-EXPONENT_ROWS] * jnp.exp2(tops - TOP), axis=0)
    live = (jnp.arange(length, dtype=jnp.int32)[None, :] < lengths[:, None]).reshape(-1, 1)
    doc_grad = jnp.where(live, own + came, 0.0)
    return query_grad, doc_grad


def solution(mesh):
    split = Mesh(mesh.devices.reshape(4, 2, 2, 4, 8), ("x", "zh", "c", "y", "zl"))
    return jax.shard_map(
        per_device,
        mesh=split,
        in_specs=(
            P((*QUERY_AXES, *DOC_AXES), None),
            P((*DOC_AXES, *QUERY_AXES), None),
            P((*DOC_AXES, *QUERY_AXES)),
            P(DOC_AXES, QUERY_AXES),
            P(QUERY_AXES, DOC_AXES),
            P(QUERY_AXES),
        ),
        out_specs=(P((*QUERY_AXES, *DOC_AXES), None), P((*DOC_AXES, *QUERY_AXES), None)),
        check_vma=False,
    )
```

time: 113 us -> 112 us (level)
  the two profiles are of different devices: /device:TPU:32 before, /device:TPU:2 now
where the time goes in v4:
time: 112 us
  starting transfers between devices  49.5 us (44%)
  blocking collectives  26.7 us (24%)
  waiting for transfers between devices  15.9 us (14%)
  Pallas kernels  12.8 us (11%)
  other arithmetic  3.15 us (3%)
  local copies, waits for them, and re-layouts  2.91 us (3%)
    all_to_all x4, starting transfers between devices, exchange(): return lax.all_to_all(x, axes, split_axis=0, concat_axis=0, tiled=True)  39.2 us
    all_gather x1, blocking collectives, per_device(): lax.all_gather(without_padding(documents, lengths), ('y', 'c'), tiled=True)  13.6 us
    all_gather x1, blocking collectives, per_device(): q = lax.all_gather(q, 'x', tiled=True).reshape(nx, nzh, nzl, rows, width)  13.1 us
    all_to_all x4, waiting for transfers between devices, exchange(): return lax.all_to_all(x, axes, split_axis=0, concat_axis=0, tiled=True)  11.1 us
    pallas_call x2, Pallas kernels, tile_gradients(): pl.pallas_call(lambda *refs: tile_body(own, *refs), grid=(nzl // pair,),...  10.3 us
    ppermute x1, starting transfers between devices, per_device(): lax.ppermute(give, 'y', [(i, int(p[1])) for i, p in enumerate(pairs)])  4.4 us
    ppermute x1, waiting for transfers between devices, per_device(): lax.ppermute(give, 'y', [(i, int(p[1])) for i, p in enumerate(pairs)])  3.58 us
    ppermute x1, starting transfers between devices, per_device(): lax.ppermute(give, 'y', [(i, int(p[0])) for i, p in enumerate(pairs)])  3.18 us
  transfers between devices with their start and end apart: 7, of which 4 were waited for; matrix products, arithmetic and copies ran while one was open for 1% of the time, Pallas kernels for 6%

profile of v4, /device:TPU:2, one launch (start us, length us, event | category | flops | bytes accessed | tf_op | source)
XLA Modules:
  0.0 111.7 jit_solution(6752882211570176584)
XLA Ops:
  0.6 0.0 copy-start.2
  0.6 0.0 copy-start.5
  0.7 0.0 copy-start
  0.7 1.4 %broadcast_in_dim.17 = bf16[16,32,128]{2,1,0:T(8,128)(2,1)} broadcast(bf16[32,128]{1,0:T(8,128)(2,1)} %param.6), dimensions={1,2} | broadcast | bytes 139264 | tf_op jit(solution)/shard_map/broadcast_in_dim | solution.py:300
  2.1 15.2 %all-to-all-start = ((bf16[16,32,128]{2,1,0:T(8,128)(2,1)}), bf16[16,32,128]{2,1,0:T(8,128)(2,1)S(1)}, u32[]{:S(2)}, u32[]{:S(2)}) async-start(bf16[16,32,128]{2,1,0:T(8,128)(2,1)} %broadcast_in_dim.17), calls=%async_computation | async-start | bytes 262144 | tf_op jit(solution)/shard_map/all_to_all | solution.py:290
  17.3 0.0 copy-start.1
  17.3 0.8 copy-done.1
  18.1 0.0 copy-start.3
  18.1 0.7 copy-done.3
  18.8 0.6 live_documents.1
  19.3 13.6 %all_gather.7.refs_3_ = bf16[2048,128]{1,0:T(8,128)(2,1)S(1)} all-gather(bf16[256,128]{1,0:T(8,128)(2,1)S(1)} %live_documents.1), channel_id=1, replica_groups=mesh['x'=4,'zh'=2,'c'=2,'y'=4,'zl'=8] {'y','c'}, dimensions={0}, use_global_device_ids=true | all-gather | bytes 589824 | tf_op jit(solution)/shard_map/all_gather | solution.py:303
  33.0 0.0 copy-done.2
  33.0 0.0 copy-done.5
  33.0 0.0 copy-done
  33.0 1.6 %pair_table.1 = f32[8,2,4,640]{3,2,1,0:T(4,128)} custom-call(s32[16]{0:T(128)S(1)} %copy-done.5, f32[64,512]{1,0:T(8,128)S(1)} %copy-done, f32[16,64]{1,0:T(8,128)S(1)} %copy-done.2, bf16[2048,128]{1,0:T(8,128)(2,1)S(1)} %all_gather.7.refs_3_), custom_call_target="tpu_custom_call" | custom-call | tf_op jit(solution)/shard_map/pair_table/pallas_call | solution.py:92
  34.6 0.0 all-to-all-done
  34.6 9.9 %all-to-all-start.1 = ((f32[16,4,640]{2,1,0:T(4,128)}), f32[16,4,640]{2,1,0:T(4,128)S(1)}, u32[]{:S(2)}, u32[]{:S(2)}) async-start(f32[16,4,640]{2,1,0:T(4,128)} %bitcast.3), calls=%async_computation.1 | async-start | bytes 327680 | tf_op jit(solution)/shard_map/all_to_all | solution.py:290
  44.5 13.1 %all_gather.6 = bf16[2048,128]{1,0:T(8,128)(2,1)S(1)} all-gather(bf16[512,128]{1,0:T(8,128)(2,1)S(1)} %bitcast.14), channel_id=1, replica_groups=mesh['x'=4,'zh'=2,'c'=2,'y'=4,'zl'=8] {'x'}, dimensions={0}, use_global_device_ids=true | all-gather | bytes 655360 | tf_op jit(solution)/shard_map/all_gather | solution.py:301
  57.6 0.0 all-to-all-done.1
  57.6 5.4 %other_documents.1 = (f32[4,512,128]{2,1,0:T(8,128)S(1)}, f32[1024,128]{1,0:T(8,128)S(1)}, f32[8,128]{1,0:T(8,128)}) custom-call(bf16[4,2,8,32,128]{4,3,2,1,0:T(8,128)(2,1)S(1)} %bitcast.10, bf16[4,2,256,128]{3,2,1,0:T(8,128)(2,1)S(1)} %bitcast.8, f32[8,2,4,640]{3,2,1,0:T(4,128)S(1)} %bitcast.12), custom_call_target="tpu_custom_call" | custom-call | flops 1610612736 | bytes 2097152 | tf_op jit(solution)/shard_map/other_documents/pallas_call | solution.py:178
  63.0 2.7 %collective-permute-start = (f32[1024,128]{1,0:T(8,128)S(1)}, f32[1024,128]{1,0:T(8,128)S(1)}, u32[]{:S(2)}, u32[]{:S(2)}) collective-permute-start(f32[1024,128]{1,0:T(8,128)S(1)} %get-tuple-element.17), channel_id=1, source_target_pairs={{0,32},{32,0},{1,33},{33,1},{2,34},{34,2},{3,35},{35,3},{4,36},{36... | collective-permute-start | bytes 1572872 | tf_op jit(solution)/shard_map/ppermute | solution.py:309
  65.7 4.9 %own_documents.1 = (f32[4,512,128]{2,1,0:T(8,128)S(1)}, f32[1024,128]{1,0:T(8,128)S(1)}, f32[8,128]{1,0:T(8,128)S(1)}) custom-call(bf16[4,2,8,32,128]{4,3,2,1,0:T(8,128)(2,1)S(1)} %bitcast.11, bf16[4,2,256,128]{3,2,1,0:T(8,128)(2,1)S(1)} %bitcast.9, f32[8,2,4,640]{3,2,1,0:T(4,128)S(1)} %bitcast.13, f32[4,512,128]{2,1,0:T(8,128)S(1)} %get-tuple-element.13.refs_3_), custom_call_target="tpu_custom_call" | custom-call | flops 1610612736 | bytes 2097152 | tf_op jit(solution)/shard_map/own_documents/pallas_call | solution.py:178
  70.6 0.0 collective-permute-done.refs_3_
  70.6 0.2 scale_pieces.1
  70.9 0.9 convert_element_type.12
  71.8 4.8 %all-to-all-start.2 = ((f16[4,520,128]{2,1,0:T(8,128)(2,1)}), f16[4,520,128]{2,1,0:T(8,128)(2,1)S(1)}, u32[]{:S(2)}, u32[]{:S(2)}) async-start(f16[4,520,128]{2,1,0:T(8,128)(2,1)} %convert_element_type.12), calls=%async_computation.2 | async-start | bytes 1064960 | tf_op jit(solution)/shard_map/all_to_all | solution.py:290
  76.6 3.2 %collective-permute-start.1 = (f32[2,256,128]{2,1,0:T(8,128)S(1)}, f32[2,256,128]{2,1,0:T(8,128)S(1)}, u32[]{:S(2)}, u32[]{:S(2)}) collective-permute-start(f32[2,256,128]{2,1,0:T(8,128)S(1)} %get-tuple-element.20), channel_id=1, source_target_pairs={{0,8},{8,0},{16,24},{24,16},{1,9},{9,1},{17,25},{25,17},{2,10},{10... | collective-permute-start | bytes 786440 | tf_op jit(solution)/shard_map/ppermute | solution.py:314
  79.8 5.1 %all-to-all-done.2 = f16[4,520,128]{2,1,0:T(8,128)(2,1)S(1)} async-done(((f16[4,520,128]{2,1,0:T(8,128)(2,1)}), f16[4,520,128]{2,1,0:T(8,128)(2,1)S(1)}, u32[]{:S(2)}, u32[]{:S(2)}) %all-to-all-start.2) | async-done | bytes 532512 | tf_op jit(solution)/shard_map/all_to_all | solution.py:290
  84.9 0.1 convert_element_type.13.refs_0_
  84.9 1.2 %collective-permute-done.1.refs_2_ = f32[2,256,128]{2,1,0:T(8,128)S(1)} collective-permute-done((f32[2,256,128]{2,1,0:T(8,128)S(1)}, f32[2,256,128]{2,1,0:T(8,128)S(1)}, u32[]{:S(2)}, u32[]{:S(2)}) %collective-permute-start.1) | collective-permute-done | bytes 262176 | tf_op jit(solution)/shard_map/ppermute | solution.py:314
  86.1 0.0 copy-start.4
  86.1 0.1 sum_pieces.1
  86.2 0.7 convert_element_type.14
  86.9 9.2 %all-to-all-start.3 = ((f16[16,40,128]{2,1,0:T(8,128)(2,1)}), f16[16,40,128]{2,1,0:T(8,128)(2,1)S(1)}, u32[]{:S(2)}, u32[]{:S(2)}) async-start(f16[16,40,128]{2,1,0:T(8,128)(2,1)} %convert_element_type.14), calls=%async_computation.3 | async-start | bytes 327680 | tf_op jit(solution)/shard_map/all_to_all | solution.py:290
  96.2 4.4 %collective-permute-start.2 = (f32[256,128]{1,0:T(8,128)S(1)}, f32[256,128]{1,0:T(8,128)S(1)}, u32[]{:S(2)}, u32[]{:S(2)}) collective-permute-start(f32[256,128]{1,0:T(8,128)S(1)} %get-tuple-element.23), channel_id=1, source_target_pairs={{0,24},{8,16},{16,8},{24,0},{1,25},{9,17},{17,9},{25,1},{2,26},{10... | collective-permute-start | bytes 393224 | tf_op jit(solution)/shard_map/ppermute | solution.py:317
  100.6 0.0 copy-done.4
  100.6 0.1 compare_bitcast_fusion
  100.7 3.6 %collective-permute-done.2 = f32[256,128]{1,0:T(8,128)S(1)} collective-permute-done((f32[256,128]{1,0:T(8,128)S(1)}, f32[256,128]{1,0:T(8,128)S(1)}, u32[]{:S(2)}, u32[]{:S(2)}) %collective-permute-start.2) | collective-permute-done | bytes 131104 | tf_op jit(solution)/shard_map/ppermute | solution.py:317
  104.2 0.8 add_select_fusion
  105.0 6.0 %all-to-all-done.3 = f16[16,40,128]{2,1,0:T(8,128)(2,1)S(1)} async-done(((f16[16,40,128]{2,1,0:T(8,128)(2,1)}), f16[16,40,128]{2,1,0:T(8,128)(2,1)S(1)}, u32[]{:S(2)}, u32[]{:S(2)}) %all-to-all-start.3) | async-done | bytes 163872 | tf_op jit(solution)/shard_map/all_to_all | solution.py:290
  111.1 0.6 fusion
  (2 shorter events, 0.0 us)
Async XLA Ops:
  0.6 32.3 %copy-start.2 = (f32[16,64]{1,0:T(8,128)S(1)}, f32[16,64]{1,0:T(8,128)}, u32[]{:S(2)}) copy-start(f32[16,64]{1,0:T(8,128)} %refs_2_.1) | copy-start | bytes 12292
  0.6 32.3 %copy-start.5 = (s32[16]{0:T(128)S(1)}, s32[16]{0:T(128)}, u32[]{:S(2)}) copy-start(s32[16]{0:T(128)} %refs_0_.1) | copy-start | bytes 196
  0.7 32.3 %copy-start = (f32[64,512]{1,0:T(8,128)S(1)}, f32[64,512]{1,0:T(8,128)}, u32[]{:S(2)}) copy-start(f32[64,512]{1,0:T(8,128)} %refs_1_.1) | copy-start | bytes 393220
  2.1 32.5 %all-to-all-start = ((bf16[16,32,128]{2,1,0:T(8,128)(2,1)}), bf16[16,32,128]{2,1,0:T(8,128)(2,1)S(1)}, u32[]{:S(2)}, u32[]{:S(2)}) async-start(bf16[16,32,128]{2,1,0:T(8,128)(2,1)} %broadcast_in_dim.17), calls=%async_computation | async-start | bytes 262144 | tf_op jit(solution)/shard_map/all_to_all | solution.py:290
  17.3 0.8 copy-start.1
  18.1 0.7 copy-start.3
  34.6 23.0 %all-to-all-start.1 = ((f32[16,4,640]{2,1,0:T(4,128)}), f32[16,4,640]{2,1,0:T(4,128)S(1)}, u32[]{:S(2)}, u32[]{:S(2)}) async-start(f32[16,4,640]{2,1,0:T(4,128)} %bitcast.3), calls=%async_computation.1 | async-start | bytes 327680 | tf_op jit(solution)/shard_map/all_to_all | solution.py:290
  63.0 7.7 %collective-permute-start = (f32[1024,128]{1,0:T(8,128)S(1)}, f32[1024,128]{1,0:T(8,128)S(1)}, u32[]{:S(2)}, u32[]{:S(2)}) collective-permute-start(f32[1024,128]{1,0:T(8,128)S(1)} %get-tuple-element.17), channel_id=1, source_target_pairs={{0,32},{32,0},{1,33},{33,1},{2,34},{34,2},{3,35},{35,3},{4,36},{36... | collective-permute-start | bytes 1572872 | tf_op jit(solution)/shard_map/ppermute | solution.py:309
  71.8 13.1 %all-to-all-start.2 = ((f16[4,520,128]{2,1,0:T(8,128)(2,1)}), f16[4,520,128]{2,1,0:T(8,128)(2,1)S(1)}, u32[]{:S(2)}, u32[]{:S(2)}) async-start(f16[4,520,128]{2,1,0:T(8,128)(2,1)} %convert_element_type.12), calls=%async_computation.2 | async-start | bytes 1064960 | tf_op jit(solution)/shard_map/all_to_all | solution.py:290
  76.6 9.5 %collective-permute-start.1 = (f32[2,256,128]{2,1,0:T(8,128)S(1)}, f32[2,256,128]{2,1,0:T(8,128)S(1)}, u32[]{:S(2)}, u32[]{:S(2)}) collective-permute-start(f32[2,256,128]{2,1,0:T(8,128)S(1)} %get-tuple-element.20), channel_id=1, source_target_pairs={{0,8},{8,0},{16,24},{24,16},{1,9},{9,1},{17,25},{25,17},{2,10},{10... | collective-permute-start | bytes 786440 | tf_op jit(solution)/shard_map/ppermute | solution.py:314
  86.1 14.5 %copy-start.4 = (s32[2]{0:T(128)S(1)}, s32[2]{0:T(128)}, u32[]{:S(2)}) copy-start(s32[2]{0:T(128)} %lengths_ref.1) | copy-start | bytes 28
  86.9 24.1 %all-to-all-start.3 = ((f16[16,40,128]{2,1,0:T(8,128)(2,1)}), f16[16,40,128]{2,1,0:T(8,128)(2,1)S(1)}, u32[]{:S(2)}, u32[]{:S(2)}) async-start(f16[16,40,128]{2,1,0:T(8,128)(2,1)} %convert_element_type.14), calls=%async_computation.3 | async-start | bytes 327680 | tf_op jit(solution)/shard_map/all_to_all | solution.py:290
  96.2 8.1 %collective-permute-start.2 = (f32[256,128]{1,0:T(8,128)S(1)}, f32[256,128]{1,0:T(8,128)S(1)}, u32[]{:S(2)}, u32[]{:S(2)}) collective-permute-start(f32[256,128]{1,0:T(8,128)S(1)} %get-tuple-element.23), channel_id=1, source_target_pairs={{0,24},{8,16},{16,8},{24,0},{1,25},{9,17},{17,9},{25,1},{2,26},{10... | collective-permute-start | bytes 393224 | tf_op jit(solution)/shard_map/ppermute | solution.py:317

commit v5 on v4

v5 whole, which is shorter than its diff:
```python
import jax
import jax.numpy as jnp
from jax import lax
from jax.experimental import pallas as pl
from jax.experimental.pallas import tpu as pltpu
from jax.sharding import Mesh
from jax.sharding import PartitionSpec as P

DOC_AXES = ("x", "zh", "c")
QUERY_AXES = ("y", "zl")
RING = ("zh", "zl")

SHARPNESS = 10.0
LOG2E = 1.4426950408889634
TOP = 14.0
EXPONENT_ROWS = 8
MIB = 1024 * 1024
f32, f16, bf16 = jnp.float32, jnp.float16, jnp.bfloat16
HIGHEST = lax.Precision.HIGHEST


def first_body(lengths_ref, queries_ref, docs_ref, copies_ref, d_ref):
    local_docs = lengths_ref.shape[0]
    length = docs_ref.shape[0] // local_docs
    for k in range(copies_ref.shape[0]):
        copies_ref[k] = queries_ref[...]
    for e in range(local_docs):
        block = docs_ref[e * length : (e + 1) * length, :].astype(f32)
        live = lax.broadcasted_iota(jnp.int32, block.shape, 0) < lengths_ref[e]
        d_ref[e * length : (e + 1) * length, :] = jnp.where(live, block, 0.0).astype(bf16)


def first(nz, lengths, queries, documents):
    smem, vmem = pl.BlockSpec(memory_space=pltpu.SMEM), pl.BlockSpec(memory_space=pltpu.VMEM)
    return pl.pallas_call(
        first_body,
        in_specs=[smem, vmem, vmem],
        out_specs=[vmem, vmem],
        out_shape=[
            jax.ShapeDtypeStruct((nz, *queries.shape), bf16),
            jax.ShapeDtypeStruct(documents.shape, bf16),
        ],
        name="first",
    )(lengths, queries, documents)


def table_body(nx, nzh, nc, ny, nzl, positives_ref, z_ref, probs_ref, after_ref, out_ref, t_ref):
    row_docs, row_tokens = z_ref.shape
    row_queries = probs_ref.shape[0]
    rows = row_tokens // row_queries
    local_docs = row_docs // (ny * nzl)
    groups = row_queries // nc
    half = groups * rows
    chunks = half // 128
    first_doc = ((lax.axis_index("x") * nzh + lax.axis_index("zh")) * nc + lax.axis_index("c")) * row_docs
    doc = first_doc + lax.broadcasted_iota(jnp.int32, probs_ref.shape, 1)
    query = lax.broadcasted_iota(jnp.int32, probs_ref.shape, 0)
    hit = jnp.zeros(probs_ref.shape, jnp.bool_)
    for i in range(row_queries):
        hit = hit | ((query == i) & (doc == positives_ref[i]))
    signal = probs_ref[...] - hit.astype(f32)

    z = z_ref[...] * LOG2E
    count = row_docs // local_docs
    for c in range(nc):
        columns = [z[:, (g * nc + c) * rows : (g * nc + c + 1) * rows] for g in range(groups)]
        columns = jnp.concatenate(columns, axis=1)
        one = (
            lax.broadcasted_iota(jnp.int32, (row_queries, 128), 0)
            == lax.broadcasted_iota(jnp.int32, (row_queries, 128), 1) * nc + c
        )
        turned = lax.dot_general(
            signal, one.astype(f32), (((0,), (0,)), ((), ())), preferred_element_type=f32, precision=HIGHEST
        )
        for k in range(chunks):
            t_ref[c, k] = columns[:, k * 128 : (k + 1) * 128]
        t_ref[c, chunks] = turned
        tail = jnp.zeros((count, 128), f32)
        for e in range(local_docs):
            lines = [t_ref.at[c, k][pl.ds(e, count, stride=local_docs), :] for k in range(chunks + 1)]
            for k in range(chunks):
                for y in range(ny):
                    at = e * half + k * 128
                    out_ref[:, c, y, at : at + 128] = lines[k][y * nzl : (y + 1) * nzl]
            tail = tail + (pltpu.roll(lines[chunks], e * groups, 1) if e else lines[chunks])
        for y in range(ny):
            out_ref[:, c, y, local_docs * half :] = tail[y * nzl : (y + 1) * nzl]


def make_table(sizes, positives, normalizers, probs, after):
    _, _, nc, ny, nzl = sizes
    row_docs, row_tokens = normalizers.shape
    half = row_tokens // nc
    local_docs = row_docs // (ny * nzl)
    smem, vmem = pl.BlockSpec(memory_space=pltpu.SMEM), pl.BlockSpec(memory_space=pltpu.VMEM)
    return pl.pallas_call(
        lambda *refs: table_body(*sizes, *refs),
        in_specs=[smem, vmem, vmem, pl.BlockSpec(memory_space=pl.ANY)],
        out_specs=vmem,
        out_shape=jax.ShapeDtypeStruct((nzl, nc, ny, local_docs * half + 128), f32),
        scratch_shapes=[pltpu.VMEM((nc, half // 128 + 1, row_docs, 128), f32)],
        name="pair_table",
    )(positives, normalizers, probs, after)


def tile_body(q_ref, d_ref, n_ref, sent_ref, mine_ref, other_ref, top_ref, dr_ref, nr_ref, w_ref):
    step = pl.program_id(0)
    ny, nc, local_slots, width = d_ref.shape
    pair, _, _, lanes = n_ref.shape
    lines = nc * ny
    nx, nzh, _, rows, _ = q_ref.shape
    half = nx * nzh * rows
    tokens = pair * half
    local_docs = (lanes - 128) // half
    length = local_slots // local_docs
    me = lax.axis_index("c")
    cores = (me, 1 - me)

    @pl.when(step == 0)
    def _():
        for r in range(nc):
            for y in range(ny):
                at = (r * ny + y) * local_slots
                dr_ref[at : at + local_slots, :] = d_ref[y, cores[r]]

    for j in range(pair):
        for r in range(nc):
            nr_ref[j * lines + r * ny : j * lines + (r + 1) * ny, :] = n_ref[j, cores[r]]
    q = jnp.transpose(q_ref[...], (2, 0, 1, 3, 4)).reshape(tokens, width)
    column = lax.broadcasted_iota(jnp.int32, (128, local_docs * half), 1) // rows
    spread = (column == lax.broadcasted_iota(jnp.int32, (128, local_docs * half), 0)).astype(f32)
    signal = jnp.dot(
        nr_ref[:, local_docs * half :], spread, preferred_element_type=f32, precision=HIGHEST
    )
    for line in range(lines):
        for e in range(local_docs):
            at = (line * local_docs + e) * length
            here = slice(e * half, (e + 1) * half)
            d = dr_ref[at : at + length, :]
            s = lax.dot_general(d, q, (((1,), (1,)), ((), ())), preferred_element_type=f32)
            which = [j * lines + line for j in range(pair)]
            z = jnp.concatenate([nr_ref[k : k + 1, here] for k in which], axis=1)
            p = jnp.concatenate([signal[k : k + 1, here] for k in which], axis=1)
            t = jnp.minimum(s * (SHARPNESS * LOG2E) - z, 0.0)
            w_ref[at : at + length, :] = (jnp.exp2(t) * p).astype(bf16)
    w = w_ref[...]
    qg = lax.dot_general(w, dr_ref[...], (((0,), (0,)), ((), ())), preferred_element_type=f32)
    largest = jnp.max(jnp.abs(qg).reshape(-1, 8, width), axis=0)
    qg = qg.reshape(pair, nx, nzh, rows, width)
    for j in range(pair):
        for x in range(nx):
            for zh in range(nzh):
                at = pl.multiple_of((zh * pl.num_programs(0) * pair + step * pair + j) * rows, rows)
                sent_ref[x, pl.ds(at, rows), :] = qg[j, x, zh]
    dg = jnp.dot(w, q, preferred_element_type=f32)
    own = mine_ref.shape[0]

    @pl.when(step == 0)
    def _():
        mine_ref[...] = dg[:own]
        other_ref[...] = dg[own:]
        top_ref[...] = largest

    @pl.when(step > 0)
    def _():
        mine_ref[...] += dg[:own]
        other_ref[...] += dg[own:]
        top_ref[...] = jnp.maximum(top_ref[...], largest)

    @pl.when(step == pl.num_programs(0) - 1)
    def _():
        most = jnp.maximum(jnp.max(top_ref[...], keepdims=True), 1e-30)
        top = jnp.broadcast_to(jnp.ceil(jnp.log2(most)), (1, width))
        piece = sent_ref.shape[1] - EXPONENT_ROWS
        factor = jnp.exp2(TOP - top)
        for x in range(nx):
            sent_ref[x, :piece, :] = sent_ref[x, :piece, :] * factor
            sent_ref[x, piece:, :] = jnp.broadcast_to(top, (EXPONENT_ROWS, width))


def tile_gradients(q, d, n):
    nx, nzh, nzl, rows, width = q.shape
    ny, nc, local_slots, _ = d.shape
    pair = 2
    slots = ny * nc * local_slots
    piece = nzh * nzl * rows
    part = pl.BlockSpec((slots // nc, width), lambda i: (0, 0))
    return pl.pallas_call(
        tile_body,
        grid=(nzl // pair,),
        in_specs=[
            pl.BlockSpec((nx, nzh, pair, rows, width), lambda i: (0, 0, i, 0, 0)),
            pl.BlockSpec(d.shape, lambda i: (0, 0, 0, 0)),
            pl.BlockSpec((pair, *n.shape[1:]), lambda i: (i, 0, 0, 0)),
        ],
        out_specs=[pl.BlockSpec((nx, piece + EXPONENT_ROWS, width), lambda i: (0, 0, 0)), part, part],
        out_shape=[
            jax.ShapeDtypeStruct((nx, piece + EXPONENT_ROWS, width), f32),
            jax.ShapeDtypeStruct((slots // nc, width), f32),
            jax.ShapeDtypeStruct((slots // nc, width), f32),
        ],
        scratch_shapes=[
            pltpu.VMEM((8, width), f32),
            pltpu.VMEM((slots, width), bf16),
            pltpu.VMEM((pair * nc * ny, n.shape[3]), f32),
            pltpu.VMEM((slots, pair * nx * nzh * rows), bf16),
        ],
        name="pair_tile",
        compiler_params=pltpu.CompilerParams(vmem_limit_bytes=20 * MIB),
        cost_estimate=pl.CostEstimate(
            flops=6 * nx * piece * slots * width,
            bytes_accessed=8 * nx * piece * width,
            transcendentals=nx * piece * slots,
        ),
    )(q, d, n)


def neighbours(y, ny):
    return y + 1 - 2 * (y % 2), ny - 1 - y


def sum_body(spare, got_ref, sent_ref):
    nx, lines, width = got_ref.shape
    nz, rows = sent_ref.shape[0], sent_ref.shape[1] - EXPONENT_ROWS
    tops = [got_ref[x, lines - EXPONENT_ROWS : lines, :][:1] for x in range(nx)]
    top = tops[0]
    for t in tops[1:]:
        top = jnp.maximum(top, t)
    top = top + spare
    factors = [jnp.exp2(t - top) for t in tops]
    for k in range(nz):
        here = slice(k * rows, (k + 1) * rows)
        total = got_ref[0, here, :] * factors[0]
        for x in range(1, nx):
            total = total + got_ref[x, here, :] * factors[x]
        sent_ref[k, :rows, :] = total
        sent_ref[k, rows:, :] = jnp.broadcast_to(top, (EXPONENT_ROWS, width))


def sum_pieces(nz, got):
    nx, lines, width = got.shape
    rows = (lines - EXPONENT_ROWS) // nz
    vmem = pl.BlockSpec(memory_space=pltpu.VMEM)
    return pl.pallas_call(
        lambda *refs: sum_body(float((nx - 1).bit_length()), *refs),
        in_specs=[vmem],
        out_specs=vmem,
        out_shape=jax.ShapeDtypeStruct((nz, rows + EXPONENT_ROWS, width), f32),
        name="sum_pieces",
        compiler_params=pltpu.CompilerParams(vmem_limit_bytes=12 * MIB),
    )(got)


def cores_body(ny, mine_ref, other_ref, give_ref, keep_ref):
    block = mine_ref.shape[0] // ny
    y = lax.axis_index("y")
    one, two = neighbours(y, ny)
    for ref, owners in ((give_ref, (one, neighbours(one, ny)[1])), (keep_ref, (y, two))):
        for i, owner in enumerate(owners):
            here = pl.ds(pl.multiple_of(owner * block, block), block)
            ref[i] = mine_ref[here, :] + other_ref[here, :]


def cores_added(ny, mine, other):
    block, width = mine.shape[0] // ny, mine.shape[1]
    vmem = pl.BlockSpec(memory_space=pltpu.VMEM)
    half = jax.ShapeDtypeStruct((2, block, width), f32)
    return pl.pallas_call(
        lambda *refs: cores_body(ny, *refs),
        in_specs=[vmem] * 2,
        out_specs=[vmem] * 2,
        out_shape=[half, half],
        name="cores_added",
        compiler_params=pltpu.CompilerParams(vmem_limit_bytes=12 * MIB),
    )(mine, other)


def exchange(x, axes):
    return lax.all_to_all(x, axes, split_axis=0, concat_axis=0, tiled=True)


def per_device(queries, documents, lengths, normalizers, probs, positives):
    sizes = tuple(lax.axis_size(a) for a in ("x", "zh", "c", "y", "zl"))
    nx, nzh, nc, ny, nzl = sizes
    nz = nzh * nzl
    rows, width = queries.shape
    length = documents.shape[0] // lengths.shape[0]

    copies, live_docs = first(nz, lengths, queries, documents)
    q = exchange(copies, RING).reshape(nz * rows, width)
    q = lax.all_gather(q, "x", tiled=True).reshape(nx, nzh, nzl, rows, width)

    d = lax.all_gather(live_docs, ("y", "c"), tiled=True)
    table = make_table(sizes, positives, normalizers, probs, d)
    table = exchange(table.reshape(nzl * nc, *table.shape[2:]), ("zl", "c")).reshape(table.shape)
    d = d.reshape(ny, nc, -1, width)

    sent, mine, other = tile_gradients(q, d, table)

    other = lax.ppermute(other, "c", [(i, 1 - i) for i in range(nc)])
    got = exchange(sent.astype(f16), "x").astype(f32)
    got = exchange(sum_pieces(nz, got).astype(f16), RING).astype(f32)
    give, keep = cores_added(ny, mine, other)
    pairs = [neighbours(i, ny) for i in range(ny)]
    keep = keep + lax.ppermute(give, "y", [(i, p[0]) for i, p in enumerate(pairs)])
    own = keep[0] + lax.ppermute(keep[1], "y", [(i, p[1]) for i, p in enumerate(pairs)])
    tops = got[:, -EXPONENT_ROWS : 1 - EXPONENT_ROWS]
    query_grad = jnp.sum(got[:, :-EXPONENT_ROWS] * jnp.exp2(tops - TOP), axis=0)
    live = (jnp.arange(length, dtype=jnp.int32)[None, :] < lengths[:, None]).reshape(-1, 1)
    return query_grad, jnp.where(live, own, 0.0)


def solution(mesh):
    split = Mesh(mesh.devices.reshape(4, 2, 2, 4, 8), ("x", "zh", "c", "y", "zl"))
    return jax.shard_map(
        per_device,
        mesh=split,
        in_specs=(
            P((*QUERY_AXES, *DOC_AXES), None),
            P((*DOC_AXES, *QUERY_AXES), None),
            P((*DOC_AXES, *QUERY_AXES)),
            P(DOC_AXES, QUERY_AXES),
            P(QUERY_AXES, DOC_AXES),
            P(QUERY_AXES),
        ),
        out_specs=(P((*QUERY_AXES, *DOC_AXES), None), P((*DOC_AXES, *QUERY_AXES), None)),
        check_vma=False,
    )
```

time: 112 us -> 111 us (level)
  the two profiles are of different devices: /device:TPU:2 before, /device:TPU:32 now
where the time goes in v5:
time: 111 us; the launch traced here: 110 us
  starting transfers between devices  48.5 us (44%)
  blocking collectives  28 us (25%)
  waiting for transfers between devices  16.5 us (15%)
  Pallas kernels  13.1 us (12%)
  other arithmetic  3.17 us (3%)
    all_to_all x4, starting transfers between devices, exchange(): return lax.all_to_all(x, axes, split_axis=0, concat_axis=0, tiled=True)  38.9 us
    all_gather x1, blocking collectives, per_device(): d = lax.all_gather(live_docs, ('y', 'c'), tiled=True)  14.9 us
    all_gather x1, blocking collectives, per_device(): q = lax.all_gather(q, 'x', tiled=True).reshape(nx, nzh, nzl, rows, width)  13.1 us
    all_to_all x4, waiting for transfers between devices, exchange(): return lax.all_to_all(x, axes, split_axis=0, concat_axis=0, tiled=True)  12.9 us
    pallas_call x1, Pallas kernels, tile_gradients(): pl.pallas_call(tile_body, grid=(nzl // pair,), in_specs=[pl.BlockSpec((nx...  9.37 us
    ppermute x1, starting transfers between devices, per_device(): lax.ppermute(keep[1], 'y', [(i, p[1]) for i, p in enumerate(pairs)])  4.4 us
    ppermute x1, waiting for transfers between devices, per_device(): lax.ppermute(keep[1], 'y', [(i, p[1]) for i, p in enumerate(pairs)])  3.58 us
    ppermute x1, starting transfers between devices, per_device(): lax.ppermute(give, 'y', [(i, p[0]) for i, p in enumerate(pairs)])  3.19 us
  transfers between devices with their start and end apart: 7, of which 3 were waited for; matrix products, arithmetic and copies ran while one was open for 2% of the time, Pallas kernels for 2%

profile of v5, /device:TPU:32, one launch (start us, length us, event | category | flops | bytes accessed | tf_op | source)
XLA Modules:
  0.0 109.9 jit_solution(7704398730487362566)
XLA Ops:
  0.6 1.5 %first.1 = (bf16[16,32,128]{2,1,0:T(8,128)(2,1)}, bf16[256,128]{1,0:T(8,128)(2,1)}) custom-call(s32[2]{0:T(128)} %lengths_ref.1, bf16[32,128]{1,0:T(8,128)(2,1)} %queries_ref.1, bf16[256,128]{1,0:T(8,128)(2,1)} %docs_ref.1), custom_call_target="tpu_custom_call" | custom-call | tf_op jit(solution)/shard_map/first/pallas_call | solution.py:35
  2.2 15.2 %all-to-all-start = ((bf16[16,32,128]{2,1,0:T(8,128)(2,1)}), bf16[16,32,128]{2,1,0:T(8,128)(2,1)S(1)}, u32[]{:S(2)}, u32[]{:S(2)}) async-start(bf16[16,32,128]{2,1,0:T(8,128)(2,1)} %get-tuple-element.9), calls=%async_computation | async-start | bytes 262144 | tf_op jit(solution)/shard_map/all_to_all | solution.py:279
  17.4 14.9 %all_gather.7.refs_3_ = bf16[2048,128]{1,0:T(8,128)(2,1)} all-gather(bf16[256,128]{1,0:T(8,128)(2,1)} %get-tuple-element.10), channel_id=1, replica_groups=mesh['x'=4,'zh'=2,'c'=2,'y'=4,'zl'=8] {'y','c'}, dimensions={0}, use_global_device_ids=true | all-gather | bytes 589824 | tf_op jit(solution)/shard_map/all_gather | solution.py:293
  32.3 0.0 copy-start
  32.3 2.0 %pair_table.1 = f32[8,2,4,640]{3,2,1,0:T(4,128)} custom-call(s32[16]{0:T(128)} %refs_0_.1, f32[64,512]{1,0:T(8,128)} %refs_1_.1, f32[16,64]{1,0:T(8,128)} %refs_2_.1, bf16[2048,128]{1,0:T(8,128)(2,1)} %all_gather.7.refs_3_), custom_call_target="tpu_custom_call" | custom-call | tf_op jit(solution)/shard_map/pair_table/pallas_call | solution.py:96
  34.3 0.0 all-to-all-done
  34.3 9.9 %all-to-all-start.1 = ((f32[16,4,640]{2,1,0:T(4,128)}), f32[16,4,640]{2,1,0:T(4,128)S(1)}, u32[]{:S(2)}, u32[]{:S(2)}) async-start(f32[16,4,640]{2,1,0:T(4,128)} %bitcast.19), calls=%async_computation.1 | async-start | bytes 327680 | tf_op jit(solution)/shard_map/all_to_all | solution.py:279
  44.2 13.1 %all_gather.6 = bf16[2048,128]{1,0:T(8,128)(2,1)S(1)} all-gather(bf16[512,128]{1,0:T(8,128)(2,1)S(1)} %bitcast.20), channel_id=1, replica_groups=mesh['x'=4,'zh'=2,'c'=2,'y'=4,'zl'=8] {'x'}, dimensions={0}, use_global_device_ids=true | all-gather | bytes 655360 | tf_op jit(solution)/shard_map/all_gather | solution.py:291
  57.4 0.0 all-to-all-done.1
  57.4 0.0 copy-done
  57.4 9.4 %pair_tile.1 = (f32[4,520,128]{2,1,0:T(8,128)S(1)}, f32[1024,128]{1,0:T(8,128)S(1)}, f32[1024,128]{1,0:T(8,128)S(1)}) custom-call(bf16[4,2,8,32,128]{4,3,2,1,0:T(8,128)(2,1)S(1)} %bitcast.17, bf16[4,2,256,128]{3,2,1,0:T(8,128)(2,1)S(1)} %bitcast.16, f32[8,2,4,640]{3,2,1,0:T(4,128)S(1)} %bitcast.18), custom_call_target="tpu_custom_call" | custom-call | flops 3221225472 | bytes 2097152 | tf_op jit(solution)/shard_map/pair_tile/pallas_call | solution.py:188
  66.8 1.9 %collective-permute-start = (f32[1024,128]{1,0:T(8,128)S(1)}, f32[1024,128]{1,0:T(8,128)S(1)}, u32[]{:S(2)}, u32[]{:S(2)}) collective-permute-start(f32[1024,128]{1,0:T(8,128)S(1)} %get-tuple-element.13), channel_id=1, source_target_pairs={{0,32},{32,0},{1,33},{33,1},{2,34},{34,2},{3,35},{35,3},{4,36},{36... | collective-permute-start | bytes 1572872 | tf_op jit(solution)/shard_map/ppermute | solution.py:300
  68.7 0.9 convert_element_type.12
  69.5 4.1 %all-to-all-start.2 = ((f16[4,520,128]{2,1,0:T(8,128)(2,1)}), f16[4,520,128]{2,1,0:T(8,128)(2,1)S(1)}, u32[]{:S(2)}, u32[]{:S(2)}) async-start(f16[4,520,128]{2,1,0:T(8,128)(2,1)} %convert_element_type.12), calls=%async_computation.2 | async-start | bytes 1064960 | tf_op jit(solution)/shard_map/all_to_all | solution.py:279
  73.6 0.0 collective-permute-done.refs_1_
  73.7 0.1 cores_added.1
  73.7 3.2 %collective-permute-start.1 = (f32[2,256,128]{2,1,0:T(8,128)S(1)}, f32[2,256,128]{2,1,0:T(8,128)S(1)}, u32[]{:S(2)}, u32[]{:S(2)}) collective-permute-start(f32[2,256,128]{2,1,0:T(8,128)S(1)} %get-tuple-element.15), channel_id=1, source_target_pairs={{0,8},{8,0},{16,24},{24,16},{1,9},{9,1},{17,25},{25,17},{2,10},{10... | collective-permute-start | bytes 786440 | tf_op jit(solution)/shard_map/ppermute | solution.py:305
  76.9 7.0 %all-to-all-done.2 = f16[4,520,128]{2,1,0:T(8,128)(2,1)S(1)} async-done(((f16[4,520,128]{2,1,0:T(8,128)(2,1)}), f16[4,520,128]{2,1,0:T(8,128)(2,1)S(1)}, u32[]{:S(2)}, u32[]{:S(2)}) %all-to-all-start.2) | async-done | bytes 532512 | tf_op jit(solution)/shard_map/all_to_all | solution.py:279
  83.9 0.1 convert_element_type.13.refs_0_
  84.0 0.1 sum_pieces.1
  84.0 0.0 copy-start.1
  84.0 0.7 convert_element_type.14
  84.7 9.7 %all-to-all-start.3 = ((f16[16,40,128]{2,1,0:T(8,128)(2,1)}), f16[16,40,128]{2,1,0:T(8,128)(2,1)S(1)}, u32[]{:S(2)}, u32[]{:S(2)}) async-start(f16[16,40,128]{2,1,0:T(8,128)(2,1)} %convert_element_type.14), calls=%async_computation.3 | async-start | bytes 327680 | tf_op jit(solution)/shard_map/all_to_all | solution.py:279
  94.5 0.0 collective-permute-done.1
  94.5 4.4 %collective-permute-start.2 = (f32[256,128]{1,0:T(8,128)S(1)}, f32[256,128]{1,0:T(8,128)S(1)}, u32[]{:S(2)}, u32[]{:S(2)}) collective-permute-start(f32[256,128]{1,0:T(8,128)S(1)} %slice_bitcast_fusion), channel_id=1, source_target_pairs={{0,24},{8,16},{16,8},{24,0},{1,25},{9,17},{17,9},{25,1},{2,26},{10... | collective-permute-start | bytes 393224 | tf_op jit(solution)/shard_map/ppermute | solution.py:306
  98.9 0.0 copy-done.1
  98.9 0.1 compare_bitcast_fusion
  99.0 3.6 %collective-permute-done.2 = f32[256,128]{1,0:T(8,128)S(1)} collective-permute-done((f32[256,128]{1,0:T(8,128)S(1)}, f32[256,128]{1,0:T(8,128)S(1)}, u32[]{:S(2)}, u32[]{:S(2)}) %collective-permute-start.2) | collective-permute-done | bytes 131104 | tf_op jit(solution)/shard_map/ppermute | solution.py:306
  102.6 0.8 fusion.2
  103.3 5.9 %all-to-all-done.3 = f16[16,40,128]{2,1,0:T(8,128)(2,1)S(1)} async-done(((f16[16,40,128]{2,1,0:T(8,128)(2,1)}), f16[16,40,128]{2,1,0:T(8,128)(2,1)S(1)}, u32[]{:S(2)}, u32[]{:S(2)}) %all-to-all-start.3) | async-done | bytes 163872 | tf_op jit(solution)/shard_map/all_to_all | solution.py:279
  109.3 0.6 fusion
  (4 shorter events, 0.1 us)
Async XLA Ops:
  2.2 32.2 %all-to-all-start = ((bf16[16,32,128]{2,1,0:T(8,128)(2,1)}), bf16[16,32,128]{2,1,0:T(8,128)(2,1)S(1)}, u32[]{:S(2)}, u32[]{:S(2)}) async-start(bf16[16,32,128]{2,1,0:T(8,128)(2,1)} %get-tuple-element.9), calls=%async_computation | async-start | bytes 262144 | tf_op jit(solution)/shard_map/all_to_all | solution.py:279
  32.3 25.1 %copy-start = (bf16[2048,128]{1,0:T(8,128)(2,1)S(1)}, bf16[2048,128]{1,0:T(8,128)(2,1)}, u32[]{:S(2)}) copy-start(bf16[2048,128]{1,0:T(8,128)(2,1)} %all_gather.7.refs_3_) | copy-start | bytes 1572868
  34.3 23.0 %all-to-all-start.1 = ((f32[16,4,640]{2,1,0:T(4,128)}), f32[16,4,640]{2,1,0:T(4,128)S(1)}, u32[]{:S(2)}, u32[]{:S(2)}) async-start(f32[16,4,640]{2,1,0:T(4,128)} %bitcast.19), calls=%async_computation.1 | async-start | bytes 327680 | tf_op jit(solution)/shard_map/all_to_all | solution.py:279
  66.8 6.9 %collective-permute-start = (f32[1024,128]{1,0:T(8,128)S(1)}, f32[1024,128]{1,0:T(8,128)S(1)}, u32[]{:S(2)}, u32[]{:S(2)}) collective-permute-start(f32[1024,128]{1,0:T(8,128)S(1)} %get-tuple-element.13), channel_id=1, source_target_pairs={{0,32},{32,0},{1,33},{33,1},{2,34},{34,2},{3,35},{35,3},{4,36},{36... | collective-permute-start | bytes 1572872 | tf_op jit(solution)/shard_map/ppermute | solution.py:300
  69.5 14.3 %all-to-all-start.2 = ((f16[4,520,128]{2,1,0:T(8,128)(2,1)}), f16[4,520,128]{2,1,0:T(8,128)(2,1)S(1)}, u32[]{:S(2)}, u32[]{:S(2)}) async-start(f16[4,520,128]{2,1,0:T(8,128)(2,1)} %convert_element_type.12), calls=%async_computation.2 | async-start | bytes 1064960 | tf_op jit(solution)/shard_map/all_to_all | solution.py:279
  73.7 20.7 %collective-permute-start.1 = (f32[2,256,128]{2,1,0:T(8,128)S(1)}, f32[2,256,128]{2,1,0:T(8,128)S(1)}, u32[]{:S(2)}, u32[]{:S(2)}) collective-permute-start(f32[2,256,128]{2,1,0:T(8,128)S(1)} %get-tuple-element.15), channel_id=1, source_target_pairs={{0,8},{8,0},{16,24},{24,16},{1,9},{9,1},{17,25},{25,17},{2,10},{10... | collective-permute-start | bytes 786440 | tf_op jit(solution)/shard_map/ppermute | solution.py:305
  84.0 14.9 %copy-start.1 = (s32[2]{0:T(128)S(1)}, s32[2]{0:T(128)}, u32[]{:S(2)}) copy-start(s32[2]{0:T(128)} %lengths_ref.1) | copy-start | bytes 28
  84.7 24.5 %all-to-all-start.3 = ((f16[16,40,128]{2,1,0:T(8,128)(2,1)}), f16[16,40,128]{2,1,0:T(8,128)(2,1)S(1)}, u32[]{:S(2)}, u32[]{:S(2)}) async-start(f16[16,40,128]{2,1,0:T(8,128)(2,1)} %convert_element_type.14), calls=%async_computation.3 | async-start | bytes 327680 | tf_op jit(solution)/shard_map/all_to_all | solution.py:279
  94.5 8.1 %collective-permute-start.2 = (f32[256,128]{1,0:T(8,128)S(1)}, f32[256,128]{1,0:T(8,128)S(1)}, u32[]{:S(2)}, u32[]{:S(2)}) collective-permute-start(f32[256,128]{1,0:T(8,128)S(1)} %slice_bitcast_fusion), channel_id=1, source_target_pairs={{0,24},{8,16},{16,8},{24,0},{1,25},{9,17},{17,9},{25,1},{2,26},{10... | collective-permute-start | bytes 393224 | tf_op jit(solution)/shard_map/ppermute | solution.py:306

commit v6 on v5

--- a/solution.py
+++ b/solution.py
@@ -14,6 +14,7 @@
 LOG2E = 1.4426950408889634
 TOP = 14.0
 EXPONENT_ROWS = 8
+GROUP = 4
 MIB = 1024 * 1024
 f32, f16, bf16 = jnp.float32, jnp.float16, jnp.bfloat16
 HIGHEST = lax.Precision.HIGHEST
@@ -103,110 +104,78 @@
     )(positives, normalizers, probs, after)
 
 
-def tile_body(q_ref, d_ref, n_ref, sent_ref, mine_ref, other_ref, top_ref, dr_ref, nr_ref, w_ref):
-    step = pl.program_id(0)
+def tile_body(q_ref, d_ref, n_ref, sent_ref, mine_ref, other_ref, dr_ref, nr_ref, w_ref):
     ny, nc, local_slots, width = d_ref.shape
-    pair, _, _, lanes = n_ref.shape
+    nzl, _, _, lanes = n_ref.shape
     lines = nc * ny
     nx, nzh, _, rows, _ = q_ref.shape
     half = nx * nzh * rows
-    tokens = pair * half
+    tokens = nzl * half
     local_docs = (lanes - 128) // half
     length = local_slots // local_docs
     me = lax.axis_index("c")
-    cores = (me, 1 - me)
-
-    @pl.when(step == 0)
-    def _():
-        for r in range(nc):
-            for y in range(ny):
-                at = (r * ny + y) * local_slots
-                dr_ref[at : at + local_slots, :] = d_ref[y, cores[r]]
-
-    for j in range(pair):
-        for r in range(nc):
-            nr_ref[j * lines + r * ny : j * lines + (r + 1) * ny, :] = n_ref[j, cores[r]]
+    for r, core in enumerate((me, 1 - me)):
+        for y in range(ny):
+            at = (r * ny + y) * local_slots
+            dr_ref[at : at + local_slots, :] = d_ref[y, core]
+        for j in range(nzl):
+            nr_ref[j * lines + r * ny : j * lines + (r + 1) * ny, :] = n_ref[j, core]
     q = jnp.transpose(q_ref[...], (2, 0, 1, 3, 4)).reshape(tokens, width)
     column = lax.broadcasted_iota(jnp.int32, (128, local_docs * half), 1) // rows
     spread = (column == lax.broadcasted_iota(jnp.int32, (128, local_docs * half), 0)).astype(f32)
     signal = jnp.dot(
         nr_ref[:, local_docs * half :], spread, preferred_element_type=f32, precision=HIGHEST
     )
-    for line in range(lines):
-        for e in range(local_docs):
-            at = (line * local_docs + e) * length
+    for first_doc in range(0, lines * local_docs, GROUP):
+        at = first_doc * length
+        d = dr_ref[at : at + GROUP * length, :]
+        s = lax.dot_general(d, q, (((1,), (1,)), ((), ())), preferred_element_type=f32)
+        for k in range(GROUP):
+            line, e = divmod(first_doc + k, local_docs)
             here = slice(e * half, (e + 1) * half)
-            d = dr_ref[at : at + length, :]
-            s = lax.dot_general(d, q, (((1,), (1,)), ((), ())), preferred_element_type=f32)
-            which = [j * lines + line for j in range(pair)]
-            z = jnp.concatenate([nr_ref[k : k + 1, here] for k in which], axis=1)
-            p = jnp.concatenate([signal[k : k + 1, here] for k in which], axis=1)
-            t = jnp.minimum(s * (SHARPNESS * LOG2E) - z, 0.0)
-            w_ref[at : at + length, :] = (jnp.exp2(t) * p).astype(bf16)
+            which = [j * lines + line for j in range(nzl)]
+            z = jnp.concatenate([nr_ref[i : i + 1, here] for i in which], axis=1)
+            p = jnp.concatenate([signal[i : i + 1, here] for i in which], axis=1)
+            t = jnp.minimum(s[k * length : (k + 1) * length] * (SHARPNESS * LOG2E) - z, 0.0)
+            w_ref[at + k * length : at + (k + 1) * length, :] = (jnp.exp2(t) * p).astype(bf16)
     w = w_ref[...]
-    qg = lax.dot_general(w, dr_ref[...], (((0,), (0,)), ((), ())), preferred_element_type=f32)
-    largest = jnp.max(jnp.abs(qg).reshape(-1, 8, width), axis=0)
-    qg = qg.reshape(pair, nx, nzh, rows, width)
-    for j in range(pair):
-        for x in range(nx):
+    qg = lax.dot_general(dr_ref[...], w, (((0,), (0,)), ((), ())), preferred_element_type=f32).T
+    most = jnp.max(jnp.max(jnp.abs(qg).reshape(-1, 8, width), axis=0), keepdims=True)
+    top = jnp.broadcast_to(jnp.ceil(jnp.log2(jnp.maximum(most, 1e-30))), (1, width))
+    qg = (qg * jnp.exp2(TOP - top)).reshape(nzl, nx, nzh, rows, width)
+    for x in range(nx):
+        for j in range(nzl):
             for zh in range(nzh):
-                at = pl.multiple_of((zh * pl.num_programs(0) * pair + step * pair + j) * rows, rows)
-                sent_ref[x, pl.ds(at, rows), :] = qg[j, x, zh]
-    dg = jnp.dot(w, q, preferred_element_type=f32)
+                at = (zh * nzl + j) * rows
+                sent_ref[x, at : at + rows, :] = qg[j, x, zh]
+        sent_ref[x, nzh * nzl * rows :, :] = jnp.broadcast_to(top, (EXPONENT_ROWS, width))
     own = mine_ref.shape[0]
-
-    @pl.when(step == 0)
-    def _():
-        mine_ref[...] = dg[:own]
-        other_ref[...] = dg[own:]
-        top_ref[...] = largest
-
-    @pl.when(step > 0)
-    def _():
-        mine_ref[...] += dg[:own]
-        other_ref[...] += dg[own:]
-        top_ref[...] = jnp.maximum(top_ref[...], largest)
-
-    @pl.when(step == pl.num_programs(0) - 1)
-    def _():
-        most = jnp.maximum(jnp.max(top_ref[...], keepdims=True), 1e-30)
-        top = jnp.broadcast_to(jnp.ceil(jnp.log2(most)), (1, width))
-        piece = sent_ref.shape[1] - EXPONENT_ROWS
-        factor = jnp.exp2(TOP - top)
-        for x in range(nx):
-            sent_ref[x, :piece, :] = sent_ref[x, :piece, :] * factor
-            sent_ref[x, piece:, :] = jnp.broadcast_to(top, (EXPONENT_ROWS, width))
+    mine_ref[...] = jnp.dot(w[:own], q, preferred_element_type=f32)
+    other_ref[...] = jnp.dot(w[own:], q, preferred_element_type=f32)
 
 
 def tile_gradients(q, d, n):
     nx, nzh, nzl, rows, width = q.shape
     ny, nc, local_slots, _ = d.shape
-    pair = 2
     slots = ny * nc * local_slots
     piece = nzh * nzl * rows
-    part = pl.BlockSpec((slots // nc, width), lambda i: (0, 0))
+    vmem = pl.BlockSpec(memory_space=pltpu.VMEM)
     return pl.pallas_call(
         tile_body,
-        grid=(nzl // pair,),
-        in_specs=[
-            pl.BlockSpec((nx, nzh, pair, rows, width), lambda i: (0, 0, i, 0, 0)),
-            pl.BlockSpec(d.shape, lambda i: (0, 0, 0, 0)),
-            pl.BlockSpec((pair, *n.shape[1:]), lambda i: (i, 0, 0, 0)),
-        ],
-        out_specs=[pl.BlockSpec((nx, piece + EXPONENT_ROWS, width), lambda i: (0, 0, 0)), part, part],
+        in_specs=[vmem] * 3,
+        out_specs=[vmem] * 3,
         out_shape=[
             jax.ShapeDtypeStruct((nx, piece + EXPONENT_ROWS, width), f32),
             jax.ShapeDtypeStruct((slots // nc, width), f32),
             jax.ShapeDtypeStruct((slots // nc, width), f32),
         ],
         scratch_shapes=[
-            pltpu.VMEM((8, width), f32),
             pltpu.VMEM((slots, width), bf16),
-            pltpu.VMEM((pair * nc * ny, n.shape[3]), f32),
-            pltpu.VMEM((slots, pair * nx * nzh * rows), bf16),
+            pltpu.VMEM((nzl * nc * ny, n.shape[3]), f32),
+            pltpu.VMEM((slots, nx * piece), bf16),
         ],
         name="pair_tile",
-        compiler_params=pltpu.CompilerParams(vmem_limit_bytes=20 * MIB),
+        compiler_params=pltpu.CompilerParams(vmem_limit_bytes=40 * MIB),
         cost_estimate=pl.CostEstimate(
             flops=6 * nx * piece * slots * width,
             bytes_accessed=8 * nx * piece * width,

time: 111 us -> 108 us (0.973)
  Pallas kernels: 13.1 us -> 10.8 us
    pallas_call x1, Pallas kernels: 9.37 us -> 7.07 us  [tile_gradients(): pl.pallas_call(tile_body, in_specs=[vmem] * 3, out_specs=[vmem] * 3, out_...]
where the time goes in v6:
time: 108 us
  starting transfers between devices  48.5 us (45%)
  blocking collectives  28 us (26%)
  waiting for transfers between devices  16.5 us (15%)
  Pallas kernels  10.8 us (10%)
  other arithmetic  3.17 us (3%)
    all_to_all x4, starting transfers between devices, exchange(): return lax.all_to_all(x, axes, split_axis=0, concat_axis=0, tiled=True)  39 us
    all_gather x1, blocking collectives, per_device(): d = lax.all_gather(live_docs, ('y', 'c'), tiled=True)  14.9 us
    all_gather x1, blocking collectives, per_device(): q = lax.all_gather(q, 'x', tiled=True).reshape(nx, nzh, nzl, rows, width)  13.1 us
    all_to_all x4, waiting for transfers between devices, exchange(): return lax.all_to_all(x, axes, split_axis=0, concat_axis=0, tiled=True)  12.9 us
    pallas_call x1, Pallas kernels, tile_gradients(): pl.pallas_call(tile_body, in_specs=[vmem] * 3, out_specs=[vmem] * 3, out_...  7.07 us
    ppermute x1, starting transfers between devices, per_device(): lax.ppermute(keep[1], 'y', [(i, p[1]) for i, p in enumerate(pairs)])  4.4 us
    ppermute x1, waiting for transfers between devices, per_device(): lax.ppermute(keep[1], 'y', [(i, p[1]) for i, p in enumerate(pairs)])  3.58 us
    ppermute x1, starting transfers between devices, per_device(): lax.ppermute(give, 'y', [(i, p[0]) for i, p in enumerate(pairs)])  3.19 us
  transfers between devices with their start and end apart: 7, of which 3 were waited for; matrix products, arithmetic and copies ran while one was open for 2% of the time, Pallas kernels for 2%

profile of v6, /device:TPU:32, one launch (start us, length us, event | category | flops | bytes accessed | tf_op | source)
XLA Modules:
  0.0 107.6 jit_solution(3956893174179535022)
XLA Ops:
  0.6 1.5 %first.1 = (bf16[16,32,128]{2,1,0:T(8,128)(2,1)}, bf16[256,128]{1,0:T(8,128)(2,1)}) custom-call(s32[2]{0:T(128)} %lengths_ref.1, bf16[32,128]{1,0:T(8,128)(2,1)} %queries_ref.1, bf16[256,128]{1,0:T(8,128)(2,1)} %docs_ref.1), custom_call_target="tpu_custom_call" | custom-call | tf_op jit(solution)/shard_map/first/pallas_call | solution.py:36
  2.2 15.2 %all-to-all-start = ((bf16[16,32,128]{2,1,0:T(8,128)(2,1)}), bf16[16,32,128]{2,1,0:T(8,128)(2,1)S(1)}, u32[]{:S(2)}, u32[]{:S(2)}) async-start(bf16[16,32,128]{2,1,0:T(8,128)(2,1)} %get-tuple-element.9), calls=%async_computation | async-start | bytes 262144 | tf_op jit(solution)/shard_map/all_to_all | solution.py:248
  17.4 14.9 %all_gather.7.refs_3_ = bf16[2048,128]{1,0:T(8,128)(2,1)} all-gather(bf16[256,128]{1,0:T(8,128)(2,1)} %get-tuple-element.10), channel_id=1, replica_groups=mesh['x'=4,'zh'=2,'c'=2,'y'=4,'zl'=8] {'y','c'}, dimensions={0}, use_global_device_ids=true | all-gather | bytes 589824 | tf_op jit(solution)/shard_map/all_gather | solution.py:262
  32.3 0.0 copy-start
  32.3 2.0 %pair_table.1 = f32[8,2,4,640]{3,2,1,0:T(4,128)} custom-call(s32[16]{0:T(128)} %refs_0_.1, f32[64,512]{1,0:T(8,128)} %refs_1_.1, f32[16,64]{1,0:T(8,128)} %refs_2_.1, bf16[2048,128]{1,0:T(8,128)(2,1)} %all_gather.7.refs_3_), custom_call_target="tpu_custom_call" | custom-call | tf_op jit(solution)/shard_map/pair_table/pallas_call | solution.py:97
  34.3 0.0 all-to-all-done
  34.3 9.9 %all-to-all-start.1 = ((f32[16,4,640]{2,1,0:T(4,128)}), f32[16,4,640]{2,1,0:T(4,128)S(1)}, u32[]{:S(2)}, u32[]{:S(2)}) async-start(f32[16,4,640]{2,1,0:T(4,128)} %bitcast.19), calls=%async_computation.1 | async-start | bytes 327680 | tf_op jit(solution)/shard_map/all_to_all | solution.py:248
  44.2 13.1 %all_gather.6 = bf16[2048,128]{1,0:T(8,128)(2,1)S(1)} all-gather(bf16[512,128]{1,0:T(8,128)(2,1)S(1)} %bitcast.20), channel_id=1, replica_groups=mesh['x'=4,'zh'=2,'c'=2,'y'=4,'zl'=8] {'x'}, dimensions={0}, use_global_device_ids=true | all-gather | bytes 655360 | tf_op jit(solution)/shard_map/all_gather | solution.py:260
  57.4 0.0 all-to-all-done.1
  57.4 0.0 copy-done
  57.4 7.1 %pair_tile.1 = (f32[4,520,128]{2,1,0:T(8,128)S(1)}, f32[1024,128]{1,0:T(8,128)S(1)}, f32[1024,128]{1,0:T(8,128)S(1)}) custom-call(bf16[4,2,8,32,128]{4,3,2,1,0:T(8,128)(2,1)S(1)} %bitcast.17, bf16[4,2,256,128]{3,2,1,0:T(8,128)(2,1)S(1)} %bitcast.16, f32[8,2,4,640]{3,2,1,0:T(4,128)S(1)} %bitcast.18), custom_call_target="tpu_custom_call" | custom-call | flops 3221225472 | bytes 2097152 | tf_op jit(solution)/shard_map/pair_tile/pallas_call | solution.py:163
  64.4 1.9 %collective-permute-start = (f32[1024,128]{1,0:T(8,128)S(1)}, f32[1024,128]{1,0:T(8,128)S(1)}, u32[]{:S(2)}, u32[]{:S(2)}) collective-permute-start(f32[1024,128]{1,0:T(8,128)S(1)} %get-tuple-element.13), channel_id=1, source_target_pairs={{0,32},{32,0},{1,33},{33,1},{2,34},{34,2},{3,35},{35,3},{4,36},{36... | collective-permute-start | bytes 1572872 | tf_op jit(solution)/shard_map/ppermute | solution.py:269
  66.4 0.9 convert_element_type.12
  67.2 4.1 %all-to-all-start.2 = ((f16[4,520,128]{2,1,0:T(8,128)(2,1)}), f16[4,520,128]{2,1,0:T(8,128)(2,1)S(1)}, u32[]{:S(2)}, u32[]{:S(2)}) async-start(f16[4,520,128]{2,1,0:T(8,128)(2,1)} %convert_element_type.12), calls=%async_computation.2 | async-start | bytes 1064960 | tf_op jit(solution)/shard_map/all_to_all | solution.py:248
  71.4 0.0 collective-permute-done.refs_1_
  71.4 0.1 cores_added.1
  71.4 3.2 %collective-permute-start.1 = (f32[2,256,128]{2,1,0:T(8,128)S(1)}, f32[2,256,128]{2,1,0:T(8,128)S(1)}, u32[]{:S(2)}, u32[]{:S(2)}) collective-permute-start(f32[2,256,128]{2,1,0:T(8,128)S(1)} %get-tuple-element.15), channel_id=1, source_target_pairs={{0,8},{8,0},{16,24},{24,16},{1,9},{9,1},{17,25},{25,17},{2,10},{10... | collective-permute-start | bytes 786440 | tf_op jit(solution)/shard_map/ppermute | solution.py:274
  74.6 7.0 %all-to-all-done.2 = f16[4,520,128]{2,1,0:T(8,128)(2,1)S(1)} async-done(((f16[4,520,128]{2,1,0:T(8,128)(2,1)}), f16[4,520,128]{2,1,0:T(8,128)(2,1)S(1)}, u32[]{:S(2)}, u32[]{:S(2)}) %all-to-all-start.2) | async-done | bytes 532512 | tf_op jit(solution)/shard_map/all_to_all | solution.py:248
  81.6 0.1 convert_element_type.13.refs_0_
  81.7 0.1 sum_pieces.1
  81.7 0.0 copy-start.1
  81.7 0.7 convert_element_type.14
  82.4 9.7 %all-to-all-start.3 = ((f16[16,40,128]{2,1,0:T(8,128)(2,1)}), f16[16,40,128]{2,1,0:T(8,128)(2,1)S(1)}, u32[]{:S(2)}, u32[]{:S(2)}) async-start(f16[16,40,128]{2,1,0:T(8,128)(2,1)} %convert_element_type.14), calls=%async_computation.3 | async-start | bytes 327680 | tf_op jit(solution)/shard_map/all_to_all | solution.py:248
  92.2 0.0 collective-permute-done.1
  92.2 4.4 %collective-permute-start.2 = (f32[256,128]{1,0:T(8,128)S(1)}, f32[256,128]{1,0:T(8,128)S(1)}, u32[]{:S(2)}, u32[]{:S(2)}) collective-permute-start(f32[256,128]{1,0:T(8,128)S(1)} %slice_bitcast_fusion), channel_id=1, source_target_pairs={{0,24},{8,16},{16,8},{24,0},{1,25},{9,17},{17,9},{25,1},{2,26},{10... | collective-permute-start | bytes 393224 | tf_op jit(solution)/shard_map/ppermute | solution.py:275
  96.6 0.0 copy-done.1
  96.6 0.1 compare_bitcast_fusion
  96.7 3.6 %collective-permute-done.2 = f32[256,128]{1,0:T(8,128)S(1)} collective-permute-done((f32[256,128]{1,0:T(8,128)S(1)}, f32[256,128]{1,0:T(8,128)S(1)}, u32[]{:S(2)}, u32[]{:S(2)}) %collective-permute-start.2) | collective-permute-done | bytes 131104 | tf_op jit(solution)/shard_map/ppermute | solution.py:275
  100.3 0.8 fusion.2
  101.0 5.9 %all-to-all-done.3 = f16[16,40,128]{2,1,0:T(8,128)(2,1)S(1)} async-done(((f16[16,40,128]{2,1,0:T(8,128)(2,1)}), f16[16,40,128]{2,1,0:T(8,128)(2,1)S(1)}, u32[]{:S(2)}, u32[]{:S(2)}) %all-to-all-start.3) | async-done | bytes 163872 | tf_op jit(solution)/shard_map/all_to_all | solution.py:248
  107.0 0.6 fusion
  (4 shorter events, 0.1 us)
Async XLA Ops:
  2.2 32.2 %all-to-all-start = ((bf16[16,32,128]{2,1,0:T(8,128)(2,1)}), bf16[16,32,128]{2,1,0:T(8,128)(2,1)S(1)}, u32[]{:S(2)}, u32[]{:S(2)}) async-start(bf16[16,32,128]{2,1,0:T(8,128)(2,1)} %get-tuple-element.9), calls=%async_computation | async-start | bytes 262144 | tf_op jit(solution)/shard_map/all_to_all | solution.py:248
  32.3 25.1 %copy-start = (bf16[2048,128]{1,0:T(8,128)(2,1)S(1)}, bf16[2048,128]{1,0:T(8,128)(2,1)}, u32[]{:S(2)}) copy-start(bf16[2048,128]{1,0:T(8,128)(2,1)} %all_gather.7.refs_3_) | copy-start | bytes 1572868
  34.3 23.0 %all-to-all-start.1 = ((f32[16,4,640]{2,1,0:T(4,128)}), f32[16,4,640]{2,1,0:T(4,128)S(1)}, u32[]{:S(2)}, u32[]{:S(2)}) async-start(f32[16,4,640]{2,1,0:T(4,128)} %bitcast.19), calls=%async_computation.1 | async-start | bytes 327680 | tf_op jit(solution)/shard_map/all_to_all | solution.py:248
  64.4 6.9 %collective-permute-start = (f32[1024,128]{1,0:T(8,128)S(1)}, f32[1024,128]{1,0:T(8,128)S(1)}, u32[]{:S(2)}, u32[]{:S(2)}) collective-permute-start(f32[1024,128]{1,0:T(8,128)S(1)} %get-tuple-element.13), channel_id=1, source_target_pairs={{0,32},{32,0},{1,33},{33,1},{2,34},{34,2},{3,35},{35,3},{4,36},{36... | collective-permute-start | bytes 1572872 | tf_op jit(solution)/shard_map/ppermute | solution.py:269
  67.2 14.3 %all-to-all-start.2 = ((f16[4,520,128]{2,1,0:T(8,128)(2,1)}), f16[4,520,128]{2,1,0:T(8,128)(2,1)S(1)}, u32[]{:S(2)}, u32[]{:S(2)}) async-start(f16[4,520,128]{2,1,0:T(8,128)(2,1)} %convert_element_type.12), calls=%async_computation.2 | async-start | bytes 1064960 | tf_op jit(solution)/shard_map/all_to_all | solution.py:248
  71.4 20.7 %collective-permute-start.1 = (f32[2,256,128]{2,1,0:T(8,128)S(1)}, f32[2,256,128]{2,1,0:T(8,128)S(1)}, u32[]{:S(2)}, u32[]{:S(2)}) collective-permute-start(f32[2,256,128]{2,1,0:T(8,128)S(1)} %get-tuple-element.15), channel_id=1, source_target_pairs={{0,8},{8,0},{16,24},{24,16},{1,9},{9,1},{17,25},{25,17},{2,10},{10... | collective-permute-start | bytes 786440 | tf_op jit(solution)/shard_map/ppermute | solution.py:274
  81.7 14.9 %copy-start.1 = (s32[2]{0:T(128)S(1)}, s32[2]{0:T(128)}, u32[]{:S(2)}) copy-start(s32[2]{0:T(128)} %lengths_ref.1) | copy-start | bytes 28
  82.4 24.5 %all-to-all-start.3 = ((f16[16,40,128]{2,1,0:T(8,128)(2,1)}), f16[16,40,128]{2,1,0:T(8,128)(2,1)S(1)}, u32[]{:S(2)}, u32[]{:S(2)}) async-start(f16[16,40,128]{2,1,0:T(8,128)(2,1)} %convert_element_type.14), calls=%async_computation.3 | async-start | bytes 327680 | tf_op jit(solution)/shard_map/all_to_all | solution.py:248
  92.2 8.1 %collective-permute-start.2 = (f32[256,128]{1,0:T(8,128)S(1)}, f32[256,128]{1,0:T(8,128)S(1)}, u32[]{:S(2)}, u32[]{:S(2)}) collective-permute-start(f32[256,128]{1,0:T(8,128)S(1)} %slice_bitcast_fusion), channel_id=1, source_target_pairs={{0,24},{8,16},{16,8},{24,0},{1,25},{9,17},{17,9},{25,1},{2,26},{10... | collective-permute-start | bytes 393224 | tf_op jit(solution)/shard_map/ppermute | solution.py:275

commit v7 on v6

--- a/solution.py
+++ b/solution.py
@@ -220,28 +220,70 @@
     )(got)
 
 
+def scaled(blocks, out_ref):
+    rows, width = blocks[0].shape
+    most = jnp.max(jnp.abs(blocks[0]).reshape(-1, 8, width), axis=0)
+    for b in blocks[1:]:
+        most = jnp.maximum(most, jnp.max(jnp.abs(b).reshape(-1, 8, width), axis=0))
+    most = jnp.maximum(jnp.max(most, keepdims=True), 1e-30)
+    top = jnp.broadcast_to(jnp.ceil(jnp.log2(most)), (1, width))
+    factor = jnp.exp2(TOP - top)
+    for i, b in enumerate(blocks):
+        out_ref[i * rows : (i + 1) * rows, :] = b * factor
+    out_ref[len(blocks) * rows :, :] = jnp.broadcast_to(top, (EXPONENT_ROWS, width))
+
+
 def cores_body(ny, mine_ref, other_ref, give_ref, keep_ref):
     block = mine_ref.shape[0] // ny
     y = lax.axis_index("y")
     one, two = neighbours(y, ny)
-    for ref, owners in ((give_ref, (one, neighbours(one, ny)[1])), (keep_ref, (y, two))):
-        for i, owner in enumerate(owners):
-            here = pl.ds(pl.multiple_of(owner * block, block), block)
-            ref[i] = mine_ref[here, :] + other_ref[here, :]
+
+    def added(owner):
+        here = pl.ds(pl.multiple_of(owner * block, block), block)
+        return mine_ref[here, :] + other_ref[here, :]
+
+    scaled([added(one), added(neighbours(one, ny)[1])], give_ref)
+    keep_ref[0] = added(y)
+    keep_ref[1] = added(two)
 
 
 def cores_added(ny, mine, other):
     block, width = mine.shape[0] // ny, mine.shape[1]
     vmem = pl.BlockSpec(memory_space=pltpu.VMEM)
-    half = jax.ShapeDtypeStruct((2, block, width), f32)
     return pl.pallas_call(
         lambda *refs: cores_body(ny, *refs),
         in_specs=[vmem] * 2,
         out_specs=[vmem] * 2,
-        out_shape=[half, half],
+        out_shape=[
+            jax.ShapeDtypeStruct((2 * block + EXPONENT_ROWS, width), f32),
+            jax.ShapeDtypeStruct((2, block, width), f32),
+        ],
         name="cores_added",
         compiler_params=pltpu.CompilerParams(vmem_limit_bytes=12 * MIB),
     )(mine, other)
+
+
+def neighbour_body(keep_ref, came_ref, own_ref, give_ref):
+    block = keep_ref.shape[1]
+    factor = jnp.exp2(came_ref[2 * block :, :][:1] - TOP)
+    own_ref[...] = keep_ref[0] + came_ref[:block, :] * factor
+    scaled([keep_ref[1] + came_ref[block : 2 * block, :] * factor], give_ref)
+
+
+def neighbour_added(keep, came):
+    _, block, width = keep.shape
+    vmem = pl.BlockSpec(memory_space=pltpu.VMEM)
+    return pl.pallas_call(
+        neighbour_body,
+        in_specs=[vmem] * 2,
+        out_specs=[vmem] * 2,
+        out_shape=[
+            jax.ShapeDtypeStruct((block, width), f32),
+            jax.ShapeDtypeStruct((block + EXPONENT_ROWS, width), f32),
+        ],
+        name="neighbour_added",
+        compiler_params=pltpu.CompilerParams(vmem_limit_bytes=12 * MIB),
+    )(keep, came)
 
 
 def exchange(x, axes):
@@ -271,8 +313,10 @@
     got = exchange(sum_pieces(nz, got).astype(f16), RING).astype(f32)
     give, keep = cores_added(ny, mine, other)
     pairs = [neighbours(i, ny) for i in range(ny)]
-    keep = keep + lax.ppermute(give, "y", [(i, p[0]) for i, p in enumerate(pairs)])
-    own = keep[0] + lax.ppermute(keep[1], "y", [(i, p[1]) for i, p in enumerate(pairs)])
+    came = lax.ppermute(give.astype(f16), "y", [(i, p[0]) for i, p in enumerate(pairs)])
+    own, give = neighbour_added(keep, came.astype(f32))
+    came = lax.ppermute(give.astype(f16), "y", [(i, p[1]) for i, p in enumerate(pairs)]).astype(f32)
+    own = own + came[:-EXPONENT_ROWS] * jnp.exp2(came[-EXPONENT_ROWS : 1 - EXPONENT_ROWS] - TOP)
     tops = got[:, -EXPONENT_ROWS : 1 - EXPONENT_ROWS]
     query_grad = jnp.sum(got[:, :-EXPONENT_ROWS] * jnp.exp2(tops - TOP), axis=0)
     live = (jnp.arange(length, dtype=jnp.int32)[None, :] < lengths[:, None]).reshape(-1, 1)

time: 108 us -> 108 us (level)
  no operation moved by 1% of the time
where the time goes in v7:
time: 108 us
  starting transfers between devices  48.5 us (45%)
  blocking collectives  28 us (26%)
  waiting for transfers between devices  16.1 us (15%)
  Pallas kernels  11.1 us (10%)
  other arithmetic  3.21 us (3%)
    all_to_all x4, starting transfers between devices, exchange(): return lax.all_to_all(x, axes, split_axis=0, concat_axis=0, tiled=True)  39 us
    all_gather x1, blocking collectives, per_device(): d = lax.all_gather(live_docs, ('y', 'c'), tiled=True)  14.9 us
    all_to_all x4, waiting for transfers between devices, exchange(): return lax.all_to_all(x, axes, split_axis=0, concat_axis=0, tiled=True)  13.2 us
    all_gather x1, blocking collectives, per_device(): q = lax.all_gather(q, 'x', tiled=True).reshape(nx, nzh, nzl, rows, width)  13.1 us
    pallas_call x1, Pallas kernels, tile_gradients(): pl.pallas_call(tile_body, in_specs=[vmem] * 3, out_specs=[vmem] * 3, out_...  7.07 us
    ppermute x1, starting transfers between devices, per_device(): lax.ppermute(give.astype(f16), 'y', [(i, p[1]) for i, p in enumerate(pair...  4.39 us
    ppermute x1, starting transfers between devices, per_device(): lax.ppermute(give.astype(f16), 'y', [(i, p[0]) for i, p in enumerate(pair...  3.19 us
    ppermute x1, waiting for transfers between devices, per_device(): lax.ppermute(give.astype(f16), 'y', [(i, p[1]) for i, p in enumerate(pair...  2.91 us
  transfers between devices with their start and end apart: 7, of which 3 were waited for; matrix products, arithmetic and copies ran while one was open for 2% of the time, Pallas kernels for 2%

profile of v7, /device:TPU:32, one launch (start us, length us, event | category | flops | bytes accessed | tf_op | source)
XLA Modules:
  0.0 107.7 jit_solution(4559737154923141603)
XLA Ops:
  0.6 1.5 %first.1 = (bf16[16,32,128]{2,1,0:T(8,128)(2,1)}, bf16[256,128]{1,0:T(8,128)(2,1)}) custom-call(s32[2]{0:T(128)} %lengths_ref.1, bf16[32,128]{1,0:T(8,128)(2,1)} %queries_ref.1, bf16[256,128]{1,0:T(8,128)(2,1)} %docs_ref.1), custom_call_target="tpu_custom_call" | custom-call | tf_op jit(solution)/shard_map/first/pallas_call | solution.py:36
  2.2 15.2 %all-to-all-start = ((bf16[16,32,128]{2,1,0:T(8,128)(2,1)}), bf16[16,32,128]{2,1,0:T(8,128)(2,1)S(1)}, u32[]{:S(2)}, u32[]{:S(2)}) async-start(bf16[16,32,128]{2,1,0:T(8,128)(2,1)} %get-tuple-element.11), calls=%async_computation | async-start | bytes 262144 | tf_op jit(solution)/shard_map/all_to_all | solution.py:290
  17.4 14.9 %all_gather.7.refs_3_ = bf16[2048,128]{1,0:T(8,128)(2,1)} all-gather(bf16[256,128]{1,0:T(8,128)(2,1)} %get-tuple-element.12), channel_id=1, replica_groups=mesh['x'=4,'zh'=2,'c'=2,'y'=4,'zl'=8] {'y','c'}, dimensions={0}, use_global_device_ids=true | all-gather | bytes 589824 | tf_op jit(solution)/shard_map/all_gather | solution.py:304
  32.3 0.0 copy-start
  32.3 2.0 %pair_table.1 = f32[8,2,4,640]{3,2,1,0:T(4,128)} custom-call(s32[16]{0:T(128)} %refs_0_.1, f32[64,512]{1,0:T(8,128)} %refs_1_.1, f32[16,64]{1,0:T(8,128)} %refs_2_.1, bf16[2048,128]{1,0:T(8,128)(2,1)} %all_gather.7.refs_3_), custom_call_target="tpu_custom_call" | custom-call | tf_op jit(solution)/shard_map/pair_table/pallas_call | solution.py:97
  34.3 0.0 all-to-all-done
  34.3 9.9 %all-to-all-start.1 = ((f32[16,4,640]{2,1,0:T(4,128)}), f32[16,4,640]{2,1,0:T(4,128)S(1)}, u32[]{:S(2)}, u32[]{:S(2)}) async-start(f32[16,4,640]{2,1,0:T(4,128)} %bitcast.13), calls=%async_computation.1 | async-start | bytes 327680 | tf_op jit(solution)/shard_map/all_to_all | solution.py:290
  44.3 13.1 %all_gather.6 = bf16[2048,128]{1,0:T(8,128)(2,1)S(1)} all-gather(bf16[512,128]{1,0:T(8,128)(2,1)S(1)} %bitcast.14), channel_id=1, replica_groups=mesh['x'=4,'zh'=2,'c'=2,'y'=4,'zl'=8] {'x'}, dimensions={0}, use_global_device_ids=true | all-gather | bytes 655360 | tf_op jit(solution)/shard_map/all_gather | solution.py:302
  57.4 0.0 all-to-all-done.1
  57.4 0.0 copy-done
  57.4 7.1 %pair_tile.1 = (f32[4,520,128]{2,1,0:T(8,128)S(1)}, f32[1024,128]{1,0:T(8,128)S(1)}, f32[1024,128]{1,0:T(8,128)S(1)}) custom-call(bf16[4,2,8,32,128]{4,3,2,1,0:T(8,128)(2,1)S(1)} %bitcast.11, bf16[4,2,256,128]{3,2,1,0:T(8,128)(2,1)S(1)} %bitcast.10, f32[8,2,4,640]{3,2,1,0:T(4,128)S(1)} %bitcast.12), custom_call_target="tpu_custom_call" | custom-call | flops 3221225472 | bytes 2097152 | tf_op jit(solution)/shard_map/pair_tile/pallas_call | solution.py:163
  64.5 1.9 %collective-permute-start = (f32[1024,128]{1,0:T(8,128)S(1)}, f32[1024,128]{1,0:T(8,128)S(1)}, u32[]{:S(2)}, u32[]{:S(2)}) collective-permute-start(f32[1024,128]{1,0:T(8,128)S(1)} %get-tuple-element.15), channel_id=1, source_target_pairs={{0,32},{32,0},{1,33},{33,1},{2,34},{34,2},{3,35},{35,3},{4,36},{36... | collective-permute-start | bytes 1572872 | tf_op jit(solution)/shard_map/ppermute | solution.py:311
  66.4 0.9 convert_element_type.24
  67.3 4.1 %all-to-all-start.2 = ((f16[4,520,128]{2,1,0:T(8,128)(2,1)}), f16[4,520,128]{2,1,0:T(8,128)(2,1)S(1)}, u32[]{:S(2)}, u32[]{:S(2)}) async-start(f16[4,520,128]{2,1,0:T(8,128)(2,1)} %convert_element_type.24), calls=%async_computation.2 | async-start | bytes 1064960 | tf_op jit(solution)/shard_map/all_to_all | solution.py:290
  71.4 0.0 collective-permute-done.refs_1_
  71.4 0.2 cores_added.1
  71.6 3.2 %collective-permute-start.1 = (f16[520,128]{1,0:T(8,128)(2,1)S(1)}, f16[520,128]{1,0:T(8,128)(2,1)S(1)}, u32[]{:S(2)}, u32[]{:S(2)}) collective-permute-start(f16[520,128]{1,0:T(8,128)(2,1)S(1)} %convert_element_type.28), channel_id=1, source_target_pairs={{0,8},{8,0},{16,24},{24,16},{1,9},{9,1},{17,25},{25,17},{2,10},{10... | collective-permute-start | bytes 399368 | tf_op jit(solution)/shard_map/ppermute | solution.py:316
  74.8 6.8 %all-to-all-done.2 = f16[4,520,128]{2,1,0:T(8,128)(2,1)S(1)} async-done(((f16[4,520,128]{2,1,0:T(8,128)(2,1)}), f16[4,520,128]{2,1,0:T(8,128)(2,1)S(1)}, u32[]{:S(2)}, u32[]{:S(2)}) %all-to-all-start.2) | async-done | bytes 532512 | tf_op jit(solution)/shard_map/all_to_all | solution.py:290
  81.6 0.1 convert_element_type.25.refs_0_
  81.7 0.1 sum_pieces.1
  81.7 0.0 copy-start.1
  81.8 0.7 convert_element_type.26
  82.5 9.7 %all-to-all-start.3 = ((f16[16,40,128]{2,1,0:T(8,128)(2,1)}), f16[16,40,128]{2,1,0:T(8,128)(2,1)S(1)}, u32[]{:S(2)}, u32[]{:S(2)}) async-start(f16[16,40,128]{2,1,0:T(8,128)(2,1)} %convert_element_type.26), calls=%async_computation.3 | async-start | bytes 327680 | tf_op jit(solution)/shard_map/all_to_all | solution.py:290
  92.2 0.0 collective-permute-done.1
  92.2 0.2 neighbour_added.1
  92.4 4.4 %collective-permute-start.2 = (f16[264,128]{1,0:T(8,128)(2,1)S(1)}, f16[264,128]{1,0:T(8,128)(2,1)S(1)}, u32[]{:S(2)}, u32[]{:S(2)}) collective-permute-start(f16[264,128]{1,0:T(8,128)(2,1)S(1)} %convert_element_type.30), channel_id=1, source_target_pairs={{0,24},{8,16},{16,8},{24,0},{1,25},{9,17},{17,9},{25,1},{2,26},{10... | collective-permute-start | bytes 202760 | tf_op jit(solution)/shard_map/ppermute | solution.py:318
  96.8 0.0 copy-done.1
  96.8 0.1 compare_bitcast_fusion
  96.9 2.9 %collective-permute-done.2 = f16[264,128]{1,0:T(8,128)(2,1)S(1)} collective-permute-done((f16[264,128]{1,0:T(8,128)(2,1)S(1)}, f16[264,128]{1,0:T(8,128)(2,1)S(1)}, u32[]{:S(2)}, u32[]{:S(2)}) %collective-permute-start.2) | collective-permute-done | bytes 67616 | tf_op jit(solution)/shard_map/ppermute | solution.py:318
  99.8 0.8 fusion.2
  100.6 6.4 %all-to-all-done.3 = f16[16,40,128]{2,1,0:T(8,128)(2,1)S(1)} async-done(((f16[16,40,128]{2,1,0:T(8,128)(2,1)}), f16[16,40,128]{2,1,0:T(8,128)(2,1)S(1)}, u32[]{:S(2)}, u32[]{:S(2)}) %all-to-all-start.3) | async-done | bytes 163872 | tf_op jit(solution)/shard_map/all_to_all | solution.py:290
  107.0 0.6 fusion
  (7 shorter events, 0.1 us)
Async XLA Ops:
  2.2 32.2 %all-to-all-start = ((bf16[16,32,128]{2,1,0:T(8,128)(2,1)}), bf16[16,32,128]{2,1,0:T(8,128)(2,1)S(1)}, u32[]{:S(2)}, u32[]{:S(2)}) async-start(bf16[16,32,128]{2,1,0:T(8,128)(2,1)} %get-tuple-element.11), calls=%async_computation | async-start | bytes 262144 | tf_op jit(solution)/shard_map/all_to_all | solution.py:290
  32.3 25.1 %copy-start = (bf16[2048,128]{1,0:T(8,128)(2,1)S(1)}, bf16[2048,128]{1,0:T(8,128)(2,1)}, u32[]{:S(2)}) copy-start(bf16[2048,128]{1,0:T(8,128)(2,1)} %all_gather.7.refs_3_) | copy-start | bytes 1572868
  34.3 23.0 %all-to-all-start.1 = ((f32[16,4,640]{2,1,0:T(4,128)}), f32[16,4,640]{2,1,0:T(4,128)S(1)}, u32[]{:S(2)}, u32[]{:S(2)}) async-start(f32[16,4,640]{2,1,0:T(4,128)} %bitcast.13), calls=%async_computation.1 | async-start | bytes 327680 | tf_op jit(solution)/shard_map/all_to_all | solution.py:290
  64.5 6.9 %collective-permute-start = (f32[1024,128]{1,0:T(8,128)S(1)}, f32[1024,128]{1,0:T(8,128)S(1)}, u32[]{:S(2)}, u32[]{:S(2)}) collective-permute-start(f32[1024,128]{1,0:T(8,128)S(1)} %get-tuple-element.15), channel_id=1, source_target_pairs={{0,32},{32,0},{1,33},{33,1},{2,34},{34,2},{3,35},{35,3},{4,36},{36... | collective-permute-start | bytes 1572872 | tf_op jit(solution)/shard_map/ppermute | solution.py:311
  67.3 14.3 %all-to-all-start.2 = ((f16[4,520,128]{2,1,0:T(8,128)(2,1)}), f16[4,520,128]{2,1,0:T(8,128)(2,1)S(1)}, u32[]{:S(2)}, u32[]{:S(2)}) async-start(f16[4,520,128]{2,1,0:T(8,128)(2,1)} %convert_element_type.24), calls=%async_computation.2 | async-start | bytes 1064960 | tf_op jit(solution)/shard_map/all_to_all | solution.py:290
  71.6 20.5 %collective-permute-start.1 = (f16[520,128]{1,0:T(8,128)(2,1)S(1)}, f16[520,128]{1,0:T(8,128)(2,1)S(1)}, u32[]{:S(2)}, u32[]{:S(2)}) collective-permute-start(f16[520,128]{1,0:T(8,128)(2,1)S(1)} %convert_element_type.28), channel_id=1, source_target_pairs={{0,8},{8,0},{16,24},{24,16},{1,9},{9,1},{17,25},{25,17},{2,10},{10... | collective-permute-start | bytes 399368 | tf_op jit(solution)/shard_map/ppermute | solution.py:316
  81.7 15.1 %copy-start.1 = (s32[2]{0:T(128)S(1)}, s32[2]{0:T(128)}, u32[]{:S(2)}) copy-start(s32[2]{0:T(128)} %lengths_ref.1) | copy-start | bytes 28
  82.5 24.5 %all-to-all-start.3 = ((f16[16,40,128]{2,1,0:T(8,128)(2,1)}), f16[16,40,128]{2,1,0:T(8,128)(2,1)S(1)}, u32[]{:S(2)}, u32[]{:S(2)}) async-start(f16[16,40,128]{2,1,0:T(8,128)(2,1)} %convert_element_type.26), calls=%async_computation.3 | async-start | bytes 327680 | tf_op jit(solution)/shard_map/all_to_all | solution.py:290
  92.4 7.4 %collective-permute-start.2 = (f16[264,128]{1,0:T(8,128)(2,1)S(1)}, f16[264,128]{1,0:T(8,128)(2,1)S(1)}, u32[]{:S(2)}, u32[]{:S(2)}) collective-permute-start(f16[264,128]{1,0:T(8,128)(2,1)S(1)} %convert_element_type.30), channel_id=1, source_target_pairs={{0,24},{8,16},{16,8},{24,0},{1,25},{9,17},{17,9},{25,1},{2,26},{10... | collective-permute-start | bytes 202760 | tf_op jit(solution)/shard_map/ppermute | solution.py:318

commit v8 on v6

--- a/solution.py
+++ b/solution.py
@@ -184,11 +184,29 @@
     )(q, d, n)
 
 
-def neighbours(y, ny):
-    return y + 1 - 2 * (y % 2), ny - 1 - y
-
-
-def sum_body(spare, got_ref, sent_ref):
+def cores_body(ny, mine_ref, other_ref, *refs):
+    block = mine_ref.shape[0] // ny
+    y = lax.axis_index("y")
+    for k, ref in enumerate(refs):
+        here = pl.ds(pl.multiple_of(lax.rem(y + k, ny) * block, block), block)
+        ref[...] = mine_ref[here, :] + other_ref[here, :]
+
+
+def cores_added(ny, mine, other):
+    block, width = mine.shape[0] // ny, mine.shape[1]
+    vmem = pl.BlockSpec(memory_space=pltpu.VMEM)
+    return pl.pallas_call(
+        lambda *refs: cores_body(ny, *refs),
+        in_specs=[vmem] * 2,
+        out_specs=[vmem] * ny,
+        out_shape=[jax.ShapeDtypeStruct((block, width), f32)] * ny,
+        name="cores_added",
+        compiler_params=pltpu.CompilerParams(vmem_limit_bytes=12 * MIB),
+    )(mine, other)
+
+
+def sum_body(spare, lengths_ref, got_ref, *refs):
+    *part_refs, sent_ref, doc_ref = refs
     nx, lines, width = got_ref.shape
     nz, rows = sent_ref.shape[0], sent_ref.shape[1] - EXPONENT_ROWS
     tops = [got_ref[x, lines - EXPONENT_ROWS : lines, :][:1] for x in range(nx)]
@@ -204,44 +222,32 @@
             total = total + got_ref[x, here, :] * factors[x]
         sent_ref[k, :rows, :] = total
         sent_ref[k, rows:, :] = jnp.broadcast_to(top, (EXPONENT_ROWS, width))
-
-
-def sum_pieces(nz, got):
+    local_docs = lengths_ref.shape[0]
+    length = doc_ref.shape[0] // local_docs
+    for e in range(local_docs):
+        here = slice(e * length, (e + 1) * length)
+        total = part_refs[0][here, :]
+        for part in part_refs[1:]:
+            total = total + part[here, :]
+        live = lax.broadcasted_iota(jnp.int32, total.shape, 0) < lengths_ref[e]
+        doc_ref[here, :] = jnp.where(live, total, 0.0)
+
+
+def sum_pieces(nz, lengths, got, parts):
     nx, lines, width = got.shape
     rows = (lines - EXPONENT_ROWS) // nz
-    vmem = pl.BlockSpec(memory_space=pltpu.VMEM)
+    smem, vmem = pl.BlockSpec(memory_space=pltpu.SMEM), pl.BlockSpec(memory_space=pltpu.VMEM)
     return pl.pallas_call(
         lambda *refs: sum_body(float((nx - 1).bit_length()), *refs),
-        in_specs=[vmem],
-        out_specs=vmem,
-        out_shape=jax.ShapeDtypeStruct((nz, rows + EXPONENT_ROWS, width), f32),
+        in_specs=[smem, *[vmem] * (1 + len(parts))],
+        out_specs=[vmem, vmem],
+        out_shape=[
+            jax.ShapeDtypeStruct((nz, rows + EXPONENT_ROWS, width), f32),
+            jax.ShapeDtypeStruct(parts[0].shape, f32),
+        ],
         name="sum_pieces",
         compiler_params=pltpu.CompilerParams(vmem_limit_bytes=12 * MIB),
-    )(got)
-
-
-def cores_body(ny, mine_ref, other_ref, give_ref, keep_ref):
-    block = mine_ref.shape[0] // ny
-    y = lax.axis_index("y")
-    one, two = neighbours(y, ny)
-    for ref, owners in ((give_ref, (one, neighbours(one, ny)[1])), (keep_ref, (y, two))):
-        for i, owner in enumerate(owners):
-            here = pl.ds(pl.multiple_of(owner * block, block), block)
-            ref[i] = mine_ref[here, :] + other_ref[here, :]
-
-
-def cores_added(ny, mine, other):
-    block, width = mine.shape[0] // ny, mine.shape[1]
-    vmem = pl.BlockSpec(memory_space=pltpu.VMEM)
-    half = jax.ShapeDtypeStruct((2, block, width), f32)
-    return pl.pallas_call(
-        lambda *refs: cores_body(ny, *refs),
-        in_specs=[vmem] * 2,
-        out_specs=[vmem] * 2,
-        out_shape=[half, half],
-        name="cores_added",
-        compiler_params=pltpu.CompilerParams(vmem_limit_bytes=12 * MIB),
-    )(mine, other)
+    )(lengths, got, *parts)
 
 
 def exchange(x, axes):
@@ -253,7 +259,6 @@
     nx, nzh, nc, ny, nzl = sizes
     nz = nzh * nzl
     rows, width = queries.shape
-    length = documents.shape[0] // lengths.shape[0]
 
     copies, live_docs = first(nz, lengths, queries, documents)
     q = exchange(copies, RING).reshape(nz * rows, width)
@@ -268,15 +273,14 @@
 
     other = lax.ppermute(other, "c", [(i, 1 - i) for i in range(nc)])
     got = exchange(sent.astype(f16), "x").astype(f32)
-    got = exchange(sum_pieces(nz, got).astype(f16), RING).astype(f32)
-    give, keep = cores_added(ny, mine, other)
-    pairs = [neighbours(i, ny) for i in range(ny)]
-    keep = keep + lax.ppermute(give, "y", [(i, p[0]) for i, p in enumerate(pairs)])
-    own = keep[0] + lax.ppermute(keep[1], "y", [(i, p[1]) for i, p in enumerate(pairs)])
+    parts = list(cores_added(ny, mine, other))
+    for k in sorted(range(1, ny), key=lambda k: -min(k, ny - k)):
+        parts[k] = lax.ppermute(parts[k], "y", [(i, (i + k) % ny) for i in range(ny)])
+    sent, doc_grad = sum_pieces(nz, lengths, got, parts)
+    got = exchange(sent.astype(f16), RING).astype(f32)
     tops = got[:, -EXPONENT_ROWS : 1 - EXPONENT_ROWS]
     query_grad = jnp.sum(got[:, :-EXPONENT_ROWS] * jnp.exp2(tops - TOP), axis=0)
-    live = (jnp.arange(length, dtype=jnp.int32)[None, :] < lengths[:, None]).reshape(-1, 1)
-    return query_grad, jnp.where(live, own, 0.0)
+    return query_grad, doc_grad
 
 
 def solution(mesh):

time: 108 us -> 113 us (1.046)
  the two profiles are of different devices: /device:TPU:32 before, /device:TPU:2 now
where the time goes in v8:
time: 113 us
  blocking collectives  51.1 us (45%)
  starting transfers between devices  42.5 us (38%)
  Pallas kernels  12 us (11%)
  waiting for transfers between devices  4.72 us (4%)
  other arithmetic  1.64 us (1%)
    all_to_all x3, starting transfers between devices, exchange(): return lax.all_to_all(x, axes, split_axis=0, concat_axis=0, tiled=True)  29.9 us
    all_to_all x1, blocking collectives, exchange(): return lax.all_to_all(x, axes, split_axis=0, concat_axis=0, tiled=True)  23.1 us
    all_gather x1, blocking collectives, per_device(): d = lax.all_gather(live_docs, ('y', 'c'), tiled=True)  14.9 us
    all_gather x1, blocking collectives, per_device(): q = lax.all_gather(q, 'x', tiled=True).reshape(nx, nzh, nzl, rows, width)  13.1 us
    ppermute x3, starting transfers between devices, per_device(): lax.ppermute(parts[k], 'y', [(i, (i + k) % ny) for i in range(ny)])  9.82 us
    pallas_call x1, Pallas kernels, tile_gradients(): pl.pallas_call(tile_body, in_specs=[vmem] * 3, out_specs=[vmem] * 3, out_...  7.15 us
    ppermute x3, waiting for transfers between devices, per_device(): lax.ppermute(parts[k], 'y', [(i, (i + k) % ny) for i in range(ny)])  4.71 us
    ppermute x1, starting transfers between devices, per_device(): other = lax.ppermute(other, 'c', [(i, 1 - i) for i in range(nc)])  2.72 us
  transfers between devices with their start and end apart: 7, of which 2 were waited for; matrix products, arithmetic and copies ran while one was open for 1% of the time, Pallas kernels for 2%

profile of v8, /device:TPU:2, one launch (start us, length us, event | category | flops | bytes accessed | tf_op | source)
XLA Modules:
  0.0 112.7 jit_solution(9265945130092897633)
XLA Ops:
  0.6 1.5 %first.1 = (bf16[16,32,128]{2,1,0:T(8,128)(2,1)}, bf16[256,128]{1,0:T(8,128)(2,1)}) custom-call(s32[2]{0:T(128)} %refs_0_.3, bf16[32,128]{1,0:T(8,128)(2,1)} %queries_ref.1, bf16[256,128]{1,0:T(8,128)(2,1)} %docs_ref.1), custom_call_target="tpu_custom_call" | custom-call | tf_op jit(solution)/shard_map/first/pallas_call | solution.py:36
  2.2 15.2 %all-to-all-start = ((bf16[16,32,128]{2,1,0:T(8,128)(2,1)}), bf16[16,32,128]{2,1,0:T(8,128)(2,1)S(1)}, u32[]{:S(2)}, u32[]{:S(2)}) async-start(bf16[16,32,128]{2,1,0:T(8,128)(2,1)} %get-tuple-element.13), calls=%async_computation | async-start | bytes 262144 | tf_op jit(solution)/shard_map/all_to_all | solution.py:254
  17.4 14.9 %all_gather.7.refs_3_ = bf16[2048,128]{1,0:T(8,128)(2,1)} all-gather(bf16[256,128]{1,0:T(8,128)(2,1)} %get-tuple-element.14), channel_id=1, replica_groups=mesh['x'=4,'zh'=2,'c'=2,'y'=4,'zl'=8] {'y','c'}, dimensions={0}, use_global_device_ids=true | all-gather | bytes 589824 | tf_op jit(solution)/shard_map/all_gather | solution.py:267
  32.3 0.0 copy-start
  32.3 2.0 %pair_table.1 = f32[8,2,4,640]{3,2,1,0:T(4,128)} custom-call(s32[16]{0:T(128)} %refs_0_.2, f32[64,512]{1,0:T(8,128)} %refs_1_.1, f32[16,64]{1,0:T(8,128)} %refs_2_.1, bf16[2048,128]{1,0:T(8,128)(2,1)} %all_gather.7.refs_3_), custom_call_target="tpu_custom_call" | custom-call | tf_op jit(solution)/shard_map/pair_table/pallas_call | solution.py:97
  34.3 0.0 all-to-all-done
  34.3 9.9 %all-to-all-start.1 = ((f32[16,4,640]{2,1,0:T(4,128)}), f32[16,4,640]{2,1,0:T(4,128)S(1)}, u32[]{:S(2)}, u32[]{:S(2)}) async-start(f32[16,4,640]{2,1,0:T(4,128)} %bitcast.9), calls=%async_computation.1 | async-start | bytes 327680 | tf_op jit(solution)/shard_map/all_to_all | solution.py:254
  44.2 13.1 %all_gather.6 = bf16[2048,128]{1,0:T(8,128)(2,1)S(1)} all-gather(bf16[512,128]{1,0:T(8,128)(2,1)S(1)} %bitcast.10), channel_id=1, replica_groups=mesh['x'=4,'zh'=2,'c'=2,'y'=4,'zl'=8] {'x'}, dimensions={0}, use_global_device_ids=true | all-gather | bytes 655360 | tf_op jit(solution)/shard_map/all_gather | solution.py:265
  57.3 0.0 all-to-all-done.1
  57.3 0.0 copy-done
  57.3 7.2 %pair_tile.1 = (f32[4,520,128]{2,1,0:T(8,128)S(1)}, f32[1024,128]{1,0:T(8,128)S(1)}, f32[1024,128]{1,0:T(8,128)S(1)}) custom-call(bf16[4,2,8,32,128]{4,3,2,1,0:T(8,128)(2,1)S(1)} %bitcast.7, bf16[4,2,256,128]{3,2,1,0:T(8,128)(2,1)S(1)} %bitcast.6, f32[8,2,4,640]{3,2,1,0:T(4,128)S(1)} %bitcast.8), custom_call_target="tpu_custom_call" | custom-call | flops 3221225472 | bytes 2097152 | tf_op jit(solution)/shard_map/pair_tile/pallas_call | solution.py:163
  64.5 2.7 %collective-permute-start = (f32[1024,128]{1,0:T(8,128)S(1)}, f32[1024,128]{1,0:T(8,128)S(1)}, u32[]{:S(2)}, u32[]{:S(2)}) collective-permute-start(f32[1024,128]{1,0:T(8,128)S(1)} %get-tuple-element.17), channel_id=1, source_target_pairs={{0,32},{32,0},{1,33},{33,1},{2,34},{34,2},{3,35},{35,3},{4,36},{36... | collective-permute-start | bytes 1572872 | tf_op jit(solution)/shard_map/ppermute | solution.py:274
  67.2 0.9 convert_element_type.12
  68.1 4.8 %all-to-all-start.2 = ((f16[4,520,128]{2,1,0:T(8,128)(2,1)}), f16[4,520,128]{2,1,0:T(8,128)(2,1)S(1)}, u32[]{:S(2)}, u32[]{:S(2)}) async-start(f16[4,520,128]{2,1,0:T(8,128)(2,1)} %convert_element_type.12), calls=%async_computation.2 | async-start | bytes 1064960 | tf_op jit(solution)/shard_map/all_to_all | solution.py:254
  72.9 0.0 collective-permute-done.refs_1_
  72.9 0.0 copy-start.1
  72.9 0.1 cores_added.1
  73.0 3.2 %collective-permute-start.1 = (f32[256,128]{1,0:T(8,128)S(1)}, f32[256,128]{1,0:T(8,128)S(1)}, u32[]{:S(2)}, u32[]{:S(2)}) collective-permute-start(f32[256,128]{1,0:T(8,128)S(1)} %get-tuple-element.19), channel_id=1, source_target_pairs={{0,8},{8,16},{16,24},{24,0},{1,9},{9,17},{17,25},{25,1},{2,10},{10... | collective-permute-start | bytes 393224 | tf_op jit(solution)/shard_map/ppermute | solution.py:278
  76.2 4.6 %collective-permute-start.2 = (f32[256,128]{1,0:T(8,128)S(1)}, f32[256,128]{1,0:T(8,128)S(1)}, u32[]{:S(2)}, u32[]{:S(2)}) collective-permute-start(f32[256,128]{1,0:T(8,128)S(1)} %get-tuple-element.20), channel_id=1, source_target_pairs={{0,16},{8,24},{16,0},{24,8},{1,17},{9,25},{17,1},{25,9},{2,18},{10... | collective-permute-start | bytes 393224 | tf_op jit(solution)/shard_map/ppermute | solution.py:278
  80.8 2.0 %collective-permute-start.3 = (f32[256,128]{1,0:T(8,128)S(1)}, f32[256,128]{1,0:T(8,128)S(1)}, u32[]{:S(2)}, u32[]{:S(2)}) collective-permute-start(f32[256,128]{1,0:T(8,128)S(1)} %get-tuple-element.21), channel_id=1, source_target_pairs={{0,24},{8,0},{16,8},{24,16},{1,25},{9,1},{17,9},{25,17},{2,26},{10... | collective-permute-start | bytes 393224 | tf_op jit(solution)/shard_map/ppermute | solution.py:278
  82.8 0.0 all-to-all-done.2
  82.8 0.1 convert_element_type.13.refs_1_
  82.9 0.0 collective-permute-done.1.refs_3_
  82.9 1.7 %collective-permute-done.2.refs_4_ = f32[256,128]{1,0:T(8,128)S(1)} collective-permute-done((f32[256,128]{1,0:T(8,128)S(1)}, f32[256,128]{1,0:T(8,128)S(1)}, u32[]{:S(2)}, u32[]{:S(2)}) %collective-permute-start.2) | collective-permute-done | bytes 131104 | tf_op jit(solution)/shard_map/ppermute | solution.py:278
  84.6 3.0 %collective-permute-done.3.refs_5_ = f32[256,128]{1,0:T(8,128)S(1)} collective-permute-done((f32[256,128]{1,0:T(8,128)S(1)}, f32[256,128]{1,0:T(8,128)S(1)}, u32[]{:S(2)}, u32[]{:S(2)}) %collective-permute-start.3) | collective-permute-done | bytes 131104 | tf_op jit(solution)/shard_map/ppermute | solution.py:278
  87.6 0.0 copy-done.1
  87.6 1.2 %sum_pieces.1 = (f32[16,40,128]{2,1,0:T(8,128)S(1)}, f32[256,128]{1,0:T(8,128)}) custom-call(s32[2]{0:T(128)S(1)} %copy-done.1, f32[4,520,128]{2,1,0:T(8,128)S(1)} %convert_element_type.13.refs_1_, f32[256,128]{1,0:T(8,128)S(1)} %get-tuple-element.18.refs_2_, f32[256,128]{1,0:T(8,128)S(1)} %collective-permute-done.1.refs_3_, ...), custom_call_target="tpu_custom_call" | custom-call | tf_op jit(solution)/shard_map/sum_pieces/pallas_call | solution.py:240
  88.9 23.1 %all_to_all.20 = f16[16,40,128]{2,1,0:T(8,128)(2,1)S(1)} all-to-all(f16[16,40,128]{2,1,0:T(8,128)(2,1)S(1)} %convert_element_type.14), channel_id=1, replica_groups=mesh['x'=4,'zh'=2,'c'=2,'y'=4,'zl'=8] {'zh','zl'}, dimensions={0} | all-to-all | bytes 327680 | tf_op jit(solution)/shard_map/all_to_all | solution.py:254
  112.0 0.6 fusion
  (3 shorter events, 0.1 us)
Async XLA Ops:
  2.2 32.2 %all-to-all-start = ((bf16[16,32,128]{2,1,0:T(8,128)(2,1)}), bf16[16,32,128]{2,1,0:T(8,128)(2,1)S(1)}, u32[]{:S(2)}, u32[]{:S(2)}) async-start(bf16[16,32,128]{2,1,0:T(8,128)(2,1)} %get-tuple-element.13), calls=%async_computation | async-start | bytes 262144 | tf_op jit(solution)/shard_map/all_to_all | solution.py:254
  32.3 25.0 %copy-start = (bf16[2048,128]{1,0:T(8,128)(2,1)S(1)}, bf16[2048,128]{1,0:T(8,128)(2,1)}, u32[]{:S(2)}) copy-start(bf16[2048,128]{1,0:T(8,128)(2,1)} %all_gather.7.refs_3_) | copy-start | bytes 1572868
  34.3 23.0 %all-to-all-start.1 = ((f32[16,4,640]{2,1,0:T(4,128)}), f32[16,4,640]{2,1,0:T(4,128)S(1)}, u32[]{:S(2)}, u32[]{:S(2)}) async-start(f32[16,4,640]{2,1,0:T(4,128)} %bitcast.9), calls=%async_computation.1 | async-start | bytes 327680 | tf_op jit(solution)/shard_map/all_to_all | solution.py:254
  64.5 8.4 %collective-permute-start = (f32[1024,128]{1,0:T(8,128)S(1)}, f32[1024,128]{1,0:T(8,128)S(1)}, u32[]{:S(2)}, u32[]{:S(2)}) collective-permute-start(f32[1024,128]{1,0:T(8,128)S(1)} %get-tuple-element.17), channel_id=1, source_target_pairs={{0,32},{32,0},{1,33},{33,1},{2,34},{34,2},{3,35},{35,3},{4,36},{36... | collective-permute-start | bytes 1572872 | tf_op jit(solution)/shard_map/ppermute | solution.py:274
  68.1 14.7 %all-to-all-start.2 = ((f16[4,520,128]{2,1,0:T(8,128)(2,1)}), f16[4,520,128]{2,1,0:T(8,128)(2,1)S(1)}, u32[]{:S(2)}, u32[]{:S(2)}) async-start(f16[4,520,128]{2,1,0:T(8,128)(2,1)} %convert_element_type.12), calls=%async_computation.2 | async-start | bytes 1064960 | tf_op jit(solution)/shard_map/all_to_all | solution.py:254
  72.9 14.7 %copy-start.1 = (s32[2]{0:T(128)S(1)}, s32[2]{0:T(128)}, u32[]{:S(2)}) copy-start(s32[2]{0:T(128)} %refs_0_.3) | copy-start | bytes 28
  73.0 9.9 %collective-permute-start.1 = (f32[256,128]{1,0:T(8,128)S(1)}, f32[256,128]{1,0:T(8,128)S(1)}, u32[]{:S(2)}, u32[]{:S(2)}) collective-permute-start(f32[256,128]{1,0:T(8,128)S(1)} %get-tuple-element.19), channel_id=1, source_target_pairs={{0,8},{8,16},{16,24},{24,0},{1,9},{9,17},{17,25},{25,1},{2,10},{10... | collective-permute-start | bytes 393224 | tf_op jit(solution)/shard_map/ppermute | solution.py:278
  76.2 8.4 %collective-permute-start.2 = (f32[256,128]{1,0:T(8,128)S(1)}, f32[256,128]{1,0:T(8,128)S(1)}, u32[]{:S(2)}, u32[]{:S(2)}) collective-permute-start(f32[256,128]{1,0:T(8,128)S(1)} %get-tuple-element.20), channel_id=1, source_target_pairs={{0,16},{8,24},{16,0},{24,8},{1,17},{9,25},{17,1},{25,9},{2,18},{10... | collective-permute-start | bytes 393224 | tf_op jit(solution)/shard_map/ppermute | solution.py:278
  80.8 6.9 %collective-permute-start.3 = (f32[256,128]{1,0:T(8,128)S(1)}, f32[256,128]{1,0:T(8,128)S(1)}, u32[]{:S(2)}, u32[]{:S(2)}) collective-permute-start(f32[256,128]{1,0:T(8,128)S(1)} %get-tuple-element.21), channel_id=1, source_target_pairs={{0,24},{8,0},{16,8},{24,16},{1,25},{9,1},{17,9},{25,17},{2,26},{10... | collective-permute-start | bytes 393224 | tf_op jit(solution)/shard_map/ppermute | solution.py:278

commit v9 on v6

--- a/solution.py
+++ b/solution.py
@@ -184,68 +184,14 @@
     )(q, d, n)
 
 
-def neighbours(y, ny):
-    return y + 1 - 2 * (y % 2), ny - 1 - y
-
-
-def sum_body(spare, got_ref, sent_ref):
-    nx, lines, width = got_ref.shape
-    nz, rows = sent_ref.shape[0], sent_ref.shape[1] - EXPONENT_ROWS
-    tops = [got_ref[x, lines - EXPONENT_ROWS : lines, :][:1] for x in range(nx)]
-    top = tops[0]
-    for t in tops[1:]:
-        top = jnp.maximum(top, t)
-    top = top + spare
-    factors = [jnp.exp2(t - top) for t in tops]
-    for k in range(nz):
-        here = slice(k * rows, (k + 1) * rows)
-        total = got_ref[0, here, :] * factors[0]
-        for x in range(1, nx):
-            total = total + got_ref[x, here, :] * factors[x]
-        sent_ref[k, :rows, :] = total
-        sent_ref[k, rows:, :] = jnp.broadcast_to(top, (EXPONENT_ROWS, width))
-
-
-def sum_pieces(nz, got):
-    nx, lines, width = got.shape
-    rows = (lines - EXPONENT_ROWS) // nz
-    vmem = pl.BlockSpec(memory_space=pltpu.VMEM)
-    return pl.pallas_call(
-        lambda *refs: sum_body(float((nx - 1).bit_length()), *refs),
-        in_specs=[vmem],
-        out_specs=vmem,
-        out_shape=jax.ShapeDtypeStruct((nz, rows + EXPONENT_ROWS, width), f32),
-        name="sum_pieces",
-        compiler_params=pltpu.CompilerParams(vmem_limit_bytes=12 * MIB),
-    )(got)
-
-
-def cores_body(ny, mine_ref, other_ref, give_ref, keep_ref):
-    block = mine_ref.shape[0] // ny
-    y = lax.axis_index("y")
-    one, two = neighbours(y, ny)
-    for ref, owners in ((give_ref, (one, neighbours(one, ny)[1])), (keep_ref, (y, two))):
-        for i, owner in enumerate(owners):
-            here = pl.ds(pl.multiple_of(owner * block, block), block)
-            ref[i] = mine_ref[here, :] + other_ref[here, :]
-
-
-def cores_added(ny, mine, other):
-    block, width = mine.shape[0] // ny, mine.shape[1]
-    vmem = pl.BlockSpec(memory_space=pltpu.VMEM)
-    half = jax.ShapeDtypeStruct((2, block, width), f32)
-    return pl.pallas_call(
-        lambda *refs: cores_body(ny, *refs),
-        in_specs=[vmem] * 2,
-        out_specs=[vmem] * 2,
-        out_shape=[half, half],
-        name="cores_added",
-        compiler_params=pltpu.CompilerParams(vmem_limit_bytes=12 * MIB),
-    )(mine, other)
-
-
 def exchange(x, axes):
     return lax.all_to_all(x, axes, split_axis=0, concat_axis=0, tiled=True)
+
+
+def summed(sent, axes):
+    got = exchange(sent, axes).astype(f32)
+    tops = got[:, -EXPONENT_ROWS : 1 - EXPONENT_ROWS]
+    return jnp.sum(got[:, :-EXPONENT_ROWS] * jnp.exp2(tops - TOP), axis=0), jnp.max(tops, axis=0)
 
 
 def per_device(queries, documents, lengths, normalizers, probs, positives):
@@ -266,17 +212,21 @@
 
     sent, mine, other = tile_gradients(q, d, table)
 
-    other = lax.ppermute(other, "c", [(i, 1 - i) for i in range(nc)])
-    got = exchange(sent.astype(f16), "x").astype(f32)
-    got = exchange(sum_pieces(nz, got).astype(f16), RING).astype(f32)
-    give, keep = cores_added(ny, mine, other)
-    pairs = [neighbours(i, ny) for i in range(ny)]
-    keep = keep + lax.ppermute(give, "y", [(i, p[0]) for i, p in enumerate(pairs)])
-    own = keep[0] + lax.ppermute(keep[1], "y", [(i, p[1]) for i, p in enumerate(pairs)])
-    tops = got[:, -EXPONENT_ROWS : 1 - EXPONENT_ROWS]
-    query_grad = jnp.sum(got[:, :-EXPONENT_ROWS] * jnp.exp2(tops - TOP), axis=0)
+    mine = (mine + lax.ppermute(other, "c", [(i, 1 - i) for i in range(nc)])).reshape(ny, -1, width)
+    y = lax.axis_index("y")
+    doc_grad = lax.dynamic_index_in_dim(mine, y, 0, keepdims=False)
+    for k in range(1, ny):
+        away = lax.dynamic_index_in_dim(mine, lax.rem(y + k, ny), 0, keepdims=False)
+        doc_grad = doc_grad + lax.ppermute(away, "y", [(i, (i + k) % ny) for i in range(ny)])
     live = (jnp.arange(length, dtype=jnp.int32)[None, :] < lengths[:, None]).reshape(-1, 1)
-    return query_grad, jnp.where(live, own, 0.0)
+    doc_grad = jnp.where(live, doc_grad, 0.0)
+
+    total, top = summed(sent.astype(f16), "x")
+    top = top + (nx - 1).bit_length()
+    sent = (total * jnp.exp2(TOP - top)).reshape(nz, rows, width)
+    sent = jnp.concatenate([sent, jnp.broadcast_to(top, (nz, EXPONENT_ROWS, width))], axis=1)
+    query_grad, _ = summed(sent.astype(f16), RING)
+    return query_grad, doc_grad
 
 
 def solution(mesh):

time: 108 us -> 106 us (0.981)
  waiting for transfers between devices: 16.5 us -> 13.6 us
    all_to_all x4, waiting for transfers between devices: 12.9 us -> 7.54 us  [exchange(): return lax.all_to_all(x, axes, split_axis=0, concat_axis=0, tiled=True)]
    ppermute x3 -> x4, waiting for transfers between devices: 3.58 us -> 6.06 us  [the longest x3 6.06 us: per_device(): lax.ppermute(away, 'y', [(i, (i + k) % ny) for i in range(ny)])]
    ppermute x3 -> x4, starting transfers between devices: 9.51 us -> 11 us  [the longest x3 9.09 us: per_device(): lax.ppermute(away, 'y', [(i, (i + k) % ny) for i in range(ny)])]
    all_to_all x4, starting transfers between devices: 39 us -> 37.6 us  [exchange(): return lax.all_to_all(x, axes, split_axis=0, concat_axis=0, tiled=True)]
  transfers between devices with their start and end apart: 7 -> 8, of which waited for: 3 -> 3; matrix products, arithmetic and copies ran while one was open for 2% -> 2% of each run, Pallas kernels for 2% -> 2%
where the time goes in v9:
time: 106 us; the launch traced here: 105 us
  starting transfers between devices  48.6 us (46%)
  blocking collectives  28 us (26%)
  waiting for transfers between devices  13.6 us (13%)
  Pallas kernels  10.7 us (10%)
  other arithmetic  3.34 us (3%)
    all_to_all x4, starting transfers between devices, exchange(): return lax.all_to_all(x, axes, split_axis=0, concat_axis=0, tiled=True)  37.6 us
    all_gather x1, blocking collectives, per_device(): d = lax.all_gather(live_docs, ('y', 'c'), tiled=True)  14.9 us
    all_gather x1, blocking collectives, per_device(): q = lax.all_gather(q, 'x', tiled=True).reshape(nx, nzh, nzl, rows, width)  13.1 us
    ppermute x3, starting transfers between devices, per_device(): lax.ppermute(away, 'y', [(i, (i + k) % ny) for i in range(ny)])  9.09 us
    all_to_all x4, waiting for transfers between devices, exchange(): return lax.all_to_all(x, axes, split_axis=0, concat_axis=0, tiled=True)  7.54 us
    pallas_call x1, Pallas kernels, tile_gradients(): pl.pallas_call(tile_body, in_specs=[vmem] * 3, out_specs=[vmem] * 3, out_...  7.07 us
    ppermute x3, waiting for transfers between devices, per_device(): lax.ppermute(away, 'y', [(i, (i + k) % ny) for i in range(ny)])  6.06 us
  transfers between devices with their start and end apart: 8, of which 3 were waited for; matrix products, arithmetic and copies ran while one was open for 2% of the time, Pallas kernels for 2%

profile of v9, /device:TPU:32, one launch (start us, length us, event | category | flops | bytes accessed | tf_op | source)
XLA Modules:
  0.0 105.1 jit_solution(5115535217775447536)
XLA Ops:
  0.6 1.6 %first.1 = (bf16[16,32,128]{2,1,0:T(8,128)(2,1)}, bf16[256,128]{1,0:T(8,128)(2,1)}) custom-call(s32[2]{0:T(128)} %lengths_ref.1, bf16[32,128]{1,0:T(8,128)(2,1)} %queries_ref.1, bf16[256,128]{1,0:T(8,128)(2,1)} %docs_ref.1), custom_call_target="tpu_custom_call" | custom-call | tf_op jit(solution)/shard_map/first/pallas_call | solution.py:36
  2.2 15.2 %all-to-all-start = ((bf16[16,32,128]{2,1,0:T(8,128)(2,1)}), bf16[16,32,128]{2,1,0:T(8,128)(2,1)S(1)}, u32[]{:S(2)}, u32[]{:S(2)}) async-start(bf16[16,32,128]{2,1,0:T(8,128)(2,1)} %get-tuple-element.7), calls=%async_computation | async-start | bytes 262144 | tf_op jit(solution)/shard_map/all_to_all | solution.py:188
  17.4 14.9 %all_gather.7.refs_3_ = bf16[2048,128]{1,0:T(8,128)(2,1)} all-gather(bf16[256,128]{1,0:T(8,128)(2,1)} %get-tuple-element.8), channel_id=1, replica_groups=mesh['x'=4,'zh'=2,'c'=2,'y'=4,'zl'=8] {'y','c'}, dimensions={0}, use_global_device_ids=true | all-gather | bytes 589824 | tf_op jit(solution)/shard_map/all_gather | solution.py:208
  32.3 0.0 copy-start
  32.3 2.0 %pair_table.1 = f32[8,2,4,640]{3,2,1,0:T(4,128)} custom-call(s32[16]{0:T(128)} %refs_0_.1, f32[64,512]{1,0:T(8,128)} %refs_1_.1, f32[16,64]{1,0:T(8,128)} %refs_2_.1, bf16[2048,128]{1,0:T(8,128)(2,1)} %all_gather.7.refs_3_), custom_call_target="tpu_custom_call" | custom-call | tf_op jit(solution)/shard_map/pair_table/pallas_call | solution.py:97
  34.3 0.0 all-to-all-done
  34.3 9.9 %all-to-all-start.1 = ((f32[16,4,640]{2,1,0:T(4,128)}), f32[16,4,640]{2,1,0:T(4,128)S(1)}, u32[]{:S(2)}, u32[]{:S(2)}) async-start(f32[16,4,640]{2,1,0:T(4,128)} %bitcast.31), calls=%async_computation.1 | async-start | bytes 327680 | tf_op jit(solution)/shard_map/all_to_all | solution.py:188
  44.3 13.1 %all_gather.6 = bf16[2048,128]{1,0:T(8,128)(2,1)S(1)} all-gather(bf16[512,128]{1,0:T(8,128)(2,1)S(1)} %bitcast.32), channel_id=1, replica_groups=mesh['x'=4,'zh'=2,'c'=2,'y'=4,'zl'=8] {'x'}, dimensions={0}, use_global_device_ids=true | all-gather | bytes 655360 | tf_op jit(solution)/shard_map/all_gather | solution.py:206
  57.4 0.0 all-to-all-done.1
  57.4 0.0 copy-done
  57.4 7.1 %pair_tile.1 = (f32[4,520,128]{2,1,0:T(8,128)S(1)}, f32[1024,128]{1,0:T(8,128)S(1)}, f32[1024,128]{1,0:T(8,128)S(1)}) custom-call(bf16[4,2,8,32,128]{4,3,2,1,0:T(8,128)(2,1)S(1)} %bitcast.26, bf16[4,2,256,128]{3,2,1,0:T(8,128)(2,1)S(1)} %bitcast.25, f32[8,2,4,640]{3,2,1,0:T(4,128)S(1)} %bitcast.27), custom_call_target="tpu_custom_call" | custom-call | flops 3221225472 | bytes 2097152 | tf_op jit(solution)/shard_map/pair_tile/pallas_call | solution.py:163
  64.5 0.9 convert_element_type.10
  65.3 4.1 %all-to-all-start.2 = ((f16[4,520,128]{2,1,0:T(8,128)(2,1)}), f16[4,520,128]{2,1,0:T(8,128)(2,1)S(1)}, u32[]{:S(2)}, u32[]{:S(2)}) async-start(f16[4,520,128]{2,1,0:T(8,128)(2,1)} %convert_element_type.10), calls=%async_computation.2 | async-start | bytes 1064960 | tf_op jit(solution)/shard_map/all_to_all | solution.py:188
  69.4 1.9 %collective-permute-start = (f32[1024,128]{1,0:T(8,128)S(1)}, f32[1024,128]{1,0:T(8,128)S(1)}, u32[]{:S(2)}, u32[]{:S(2)}) collective-permute-start(f32[1024,128]{1,0:T(8,128)S(1)} %get-tuple-element.11), channel_id=1, source_target_pairs={{0,32},{32,0},{1,33},{33,1},{2,34},{34,2},{3,35},{35,3},{4,36},{36... | collective-permute-start | bytes 1572872 | tf_op jit(solution)/shard_map/ppermute | solution.py:215
  71.3 7.5 %all-to-all-done.2 = f16[4,520,128]{2,1,0:T(8,128)(2,1)S(1)} async-done(((f16[4,520,128]{2,1,0:T(8,128)(2,1)}), f16[4,520,128]{2,1,0:T(8,128)(2,1)S(1)}, u32[]{:S(2)}, u32[]{:S(2)}) %all-to-all-start.2) | async-done | bytes 532512 | tf_op jit(solution)/shard_map/all_to_all | solution.py:188
  78.9 0.1 convert_element_type.11
  79.0 0.1 fusion
  79.1 0.7 pad_maximum_fusion
  79.8 8.4 %all-to-all-start.3 = ((f16[16,40,128]{2,1,0:T(8,128)(2,1)}), f16[16,40,128]{2,1,0:T(8,128)(2,1)S(1)}, u32[]{:S(2)}, u32[]{:S(2)}) async-start(f16[16,40,128]{2,1,0:T(8,128)(2,1)} %pad_maximum_fusion), calls=%async_computation.3 | async-start | bytes 327680 | tf_op jit(solution)/shard_map/all_to_all | solution.py:188
  88.2 0.0 collective-permute-done
  88.2 0.0 copy-start.1
  88.2 0.1 add.51
  88.3 4.4 %collective-permute-start.3 = (f32[256,128]{1,0:T(8,128)S(1)}, f32[256,128]{1,0:T(8,128)S(1)}, u32[]{:S(2)}, u32[]{:S(2)}) collective-permute-start(f32[256,128]{1,0:T(8,128)S(1)} %get-tuple-element.15), channel_id=1, source_target_pairs={{0,24},{8,0},{16,8},{24,16},{1,25},{9,1},{17,9},{25,17},{2,26},{10... | collective-permute-start | bytes 393224 | tf_op jit(solution)/shard_map/ppermute | solution.py:220
  92.7 2.8 %collective-permute-start.2 = (f32[256,128]{1,0:T(8,128)S(1)}, f32[256,128]{1,0:T(8,128)S(1)}, u32[]{:S(2)}, u32[]{:S(2)}) collective-permute-start(f32[256,128]{1,0:T(8,128)S(1)} %get-tuple-element.16), channel_id=1, source_target_pairs={{0,16},{8,24},{16,0},{24,8},{1,17},{9,25},{17,1},{25,9},{2,18},{10... | collective-permute-start | bytes 393224 | tf_op jit(solution)/shard_map/ppermute | solution.py:220
  95.5 1.9 %collective-permute-start.1 = (f32[256,128]{1,0:T(8,128)S(1)}, f32[256,128]{1,0:T(8,128)S(1)}, u32[]{:S(2)}, u32[]{:S(2)}) collective-permute-start(f32[256,128]{1,0:T(8,128)S(1)} %get-tuple-element.14), channel_id=1, source_target_pairs={{0,8},{8,16},{16,24},{24,0},{1,9},{9,17},{17,25},{25,1},{2,10},{10... | collective-permute-start | bytes 393224 | tf_op jit(solution)/shard_map/ppermute | solution.py:220
  97.5 0.0 copy-done.1
  97.5 0.1 compare_bitcast_fusion
  97.5 0.0 collective-permute-done.3
  97.5 3.7 %collective-permute-done.2 = f32[256,128]{1,0:T(8,128)S(1)} collective-permute-done((f32[256,128]{1,0:T(8,128)S(1)}, f32[256,128]{1,0:T(8,128)S(1)}, u32[]{:S(2)}, u32[]{:S(2)}) %collective-permute-start.2) | collective-permute-done | bytes 131104 | tf_op jit(solution)/shard_map/ppermute | solution.py:220
  101.2 2.4 %collective-permute-done.1 = f32[256,128]{1,0:T(8,128)S(1)} collective-permute-done((f32[256,128]{1,0:T(8,128)S(1)}, f32[256,128]{1,0:T(8,128)S(1)}, u32[]{:S(2)}, u32[]{:S(2)}) %collective-permute-start.1) | collective-permute-done | bytes 131104 | tf_op jit(solution)/shard_map/ppermute | solution.py:220
  103.6 0.8 fusion.4
  104.4 0.0 all-to-all-done.3
  104.4 0.6 fusion.1
  (7 shorter events, 0.2 us)
Async XLA Ops:
  2.2 32.1 %all-to-all-start = ((bf16[16,32,128]{2,1,0:T(8,128)(2,1)}), bf16[16,32,128]{2,1,0:T(8,128)(2,1)S(1)}, u32[]{:S(2)}, u32[]{:S(2)}) async-start(bf16[16,32,128]{2,1,0:T(8,128)(2,1)} %get-tuple-element.7), calls=%async_computation | async-start | bytes 262144 | tf_op jit(solution)/shard_map/all_to_all | solution.py:188
  32.3 25.1 %copy-start = (bf16[2048,128]{1,0:T(8,128)(2,1)S(1)}, bf16[2048,128]{1,0:T(8,128)(2,1)}, u32[]{:S(2)}) copy-start(bf16[2048,128]{1,0:T(8,128)(2,1)} %all_gather.7.refs_3_) | copy-start | bytes 1572868
  34.3 23.0 %all-to-all-start.1 = ((f32[16,4,640]{2,1,0:T(4,128)}), f32[16,4,640]{2,1,0:T(4,128)S(1)}, u32[]{:S(2)}, u32[]{:S(2)}) async-start(f32[16,4,640]{2,1,0:T(4,128)} %bitcast.31), calls=%async_computation.1 | async-start | bytes 327680 | tf_op jit(solution)/shard_map/all_to_all | solution.py:188
  65.3 13.5 %all-to-all-start.2 = ((f16[4,520,128]{2,1,0:T(8,128)(2,1)}), f16[4,520,128]{2,1,0:T(8,128)(2,1)S(1)}, u32[]{:S(2)}, u32[]{:S(2)}) async-start(f16[4,520,128]{2,1,0:T(8,128)(2,1)} %convert_element_type.10), calls=%async_computation.2 | async-start | bytes 1064960 | tf_op jit(solution)/shard_map/all_to_all | solution.py:188
  69.4 18.8 %collective-permute-start = (f32[1024,128]{1,0:T(8,128)S(1)}, f32[1024,128]{1,0:T(8,128)S(1)}, u32[]{:S(2)}, u32[]{:S(2)}) collective-permute-start(f32[1024,128]{1,0:T(8,128)S(1)} %get-tuple-element.11), channel_id=1, source_target_pairs={{0,32},{32,0},{1,33},{33,1},{2,34},{34,2},{3,35},{35,3},{4,36},{36... | collective-permute-start | bytes 1572872 | tf_op jit(solution)/shard_map/ppermute | solution.py:215
  79.8 24.5 %all-to-all-start.3 = ((f16[16,40,128]{2,1,0:T(8,128)(2,1)}), f16[16,40,128]{2,1,0:T(8,128)(2,1)S(1)}, u32[]{:S(2)}, u32[]{:S(2)}) async-start(f16[16,40,128]{2,1,0:T(8,128)(2,1)} %pad_maximum_fusion), calls=%async_computation.3 | async-start | bytes 327680 | tf_op jit(solution)/shard_map/all_to_all | solution.py:188
  88.2 9.2 %copy-start.1 = (s32[2]{0:T(128)S(1)}, s32[2]{0:T(128)}, u32[]{:S(2)}) copy-start(s32[2]{0:T(128)} %lengths_ref.1) | copy-start | bytes 28
  88.3 9.2 %collective-permute-start.3 = (f32[256,128]{1,0:T(8,128)S(1)}, f32[256,128]{1,0:T(8,128)S(1)}, u32[]{:S(2)}, u32[]{:S(2)}) collective-permute-start(f32[256,128]{1,0:T(8,128)S(1)} %get-tuple-element.15), channel_id=1, source_target_pairs={{0,24},{8,0},{16,8},{24,16},{1,25},{9,1},{17,9},{25,17},{2,26},{10... | collective-permute-start | bytes 393224 | tf_op jit(solution)/shard_map/ppermute | solution.py:220
  92.7 8.5 %collective-permute-start.2 = (f32[256,128]{1,0:T(8,128)S(1)}, f32[256,128]{1,0:T(8,128)S(1)}, u32[]{:S(2)}, u32[]{:S(2)}) collective-permute-start(f32[256,128]{1,0:T(8,128)S(1)} %get-tuple-element.16), channel_id=1, source_target_pairs={{0,16},{8,24},{16,0},{24,8},{1,17},{9,25},{17,1},{25,9},{2,18},{10... | collective-permute-start | bytes 393224 | tf_op jit(solution)/shard_map/ppermute | solution.py:220
  95.5 8.1 %collective-permute-start.1 = (f32[256,128]{1,0:T(8,128)S(1)}, f32[256,128]{1,0:T(8,128)S(1)}, u32[]{:S(2)}, u32[]{:S(2)}) collective-permute-start(f32[256,128]{1,0:T(8,128)S(1)} %get-tuple-element.14), channel_id=1, source_target_pairs={{0,8},{8,16},{16,24},{24,0},{1,9},{9,17},{17,25},{25,1},{2,10},{10... | collective-permute-start | bytes 393224 | tf_op jit(solution)/shard_map/ppermute | solution.py:220

commit v10 on v9

--- a/solution.py
+++ b/solution.py
@@ -138,6 +138,12 @@
             p = jnp.concatenate([signal[i : i + 1, here] for i in which], axis=1)
             t = jnp.minimum(s[k * length : (k + 1) * length] * (SHARPNESS * LOG2E) - z, 0.0)
             w_ref[at + k * length : at + (k + 1) * length, :] = (jnp.exp2(t) * p).astype(bf16)
+        part = jnp.dot(w_ref[at : at + GROUP * length, :], q, preferred_element_type=f32)
+        own = mine_ref.shape[0]
+        if at < own:
+            mine_ref[at : at + GROUP * length, :] = part
+        else:
+            other_ref[at - own : at - own + GROUP * length, :] = part
     w = w_ref[...]
     qg = lax.dot_general(dr_ref[...], w, (((0,), (0,)), ((), ())), preferred_element_type=f32).T
     most = jnp.max(jnp.max(jnp.abs(qg).reshape(-1, 8, width), axis=0), keepdims=True)
@@ -149,9 +155,6 @@
                 at = (zh * nzl + j) * rows
                 sent_ref[x, at : at + rows, :] = qg[j, x, zh]
         sent_ref[x, nzh * nzl * rows :, :] = jnp.broadcast_to(top, (EXPONENT_ROWS, width))
-    own = mine_ref.shape[0]
-    mine_ref[...] = jnp.dot(w[:own], q, preferred_element_type=f32)
-    other_ref[...] = jnp.dot(w[own:], q, preferred_element_type=f32)
 
 
 def tile_gradients(q, d, n):

time: 106 us -> 105 us (level)
  no operation moved by 1% of the time
where the time goes in v10:
time: 105 us; the launch traced here: 104 us
  starting transfers between devices  48.6 us (46%)
  blocking collectives  28 us (27%)
  waiting for transfers between devices  13.6 us (13%)
  Pallas kernels  9.72 us (9%)
  other arithmetic  3.34 us (3%)
    all_to_all x4, starting transfers between devices, exchange(): return lax.all_to_all(x, axes, split_axis=0, concat_axis=0, tiled=True)  37.6 us
    all_gather x1, blocking collectives, per_device(): d = lax.all_gather(live_docs, ('y', 'c'), tiled=True)  14.9 us
    all_gather x1, blocking collectives, per_device(): q = lax.all_gather(q, 'x', tiled=True).reshape(nx, nzh, nzl, rows, width)  13.1 us
    ppermute x3, starting transfers between devices, per_device(): lax.ppermute(away, 'y', [(i, (i + k) % ny) for i in range(ny)])  9.09 us
    all_to_all x4, waiting for transfers between devices, exchange(): return lax.all_to_all(x, axes, split_axis=0, concat_axis=0, tiled=True)  7.54 us
    pallas_call x1, Pallas kernels, tile_gradients(): pl.pallas_call(tile_body, in_specs=[vmem] * 3, out_specs=[vmem] * 3, out_...  6.14 us
    ppermute x3, waiting for transfers between devices, per_device(): lax.ppermute(away, 'y', [(i, (i + k) % ny) for i in range(ny)])  6.06 us
  transfers between devices with their start and end apart: 8, of which 3 were waited for; matrix products, arithmetic and copies ran while one was open for 2% of the time, Pallas kernels for 2%

profile of v10, /device:TPU:32, one launch (start us, length us, event | category | flops | bytes accessed | tf_op | source)
XLA Modules:
  0.0 104.1 jit_solution(1392986240895276012)
XLA Ops:
  0.6 1.6 %first.1 = (bf16[16,32,128]{2,1,0:T(8,128)(2,1)}, bf16[256,128]{1,0:T(8,128)(2,1)}) custom-call(s32[2]{0:T(128)} %lengths_ref.1, bf16[32,128]{1,0:T(8,128)(2,1)} %queries_ref.1, bf16[256,128]{1,0:T(8,128)(2,1)} %docs_ref.1), custom_call_target="tpu_custom_call" | custom-call | tf_op jit(solution)/shard_map/first/pallas_call | solution.py:36
  2.2 15.2 %all-to-all-start = ((bf16[16,32,128]{2,1,0:T(8,128)(2,1)}), bf16[16,32,128]{2,1,0:T(8,128)(2,1)S(1)}, u32[]{:S(2)}, u32[]{:S(2)}) async-start(bf16[16,32,128]{2,1,0:T(8,128)(2,1)} %get-tuple-element.7), calls=%async_computation | async-start | bytes 262144 | tf_op jit(solution)/shard_map/all_to_all | solution.py:191
  17.4 14.9 %all_gather.7.refs_3_ = bf16[2048,128]{1,0:T(8,128)(2,1)} all-gather(bf16[256,128]{1,0:T(8,128)(2,1)} %get-tuple-element.8), channel_id=1, replica_groups=mesh['x'=4,'zh'=2,'c'=2,'y'=4,'zl'=8] {'y','c'}, dimensions={0}, use_global_device_ids=true | all-gather | bytes 589824 | tf_op jit(solution)/shard_map/all_gather | solution.py:211
  32.3 0.0 copy-start
  32.3 2.0 %pair_table.1 = f32[8,2,4,640]{3,2,1,0:T(4,128)} custom-call(s32[16]{0:T(128)} %refs_0_.1, f32[64,512]{1,0:T(8,128)} %refs_1_.1, f32[16,64]{1,0:T(8,128)} %refs_2_.1, bf16[2048,128]{1,0:T(8,128)(2,1)} %all_gather.7.refs_3_), custom_call_target="tpu_custom_call" | custom-call | tf_op jit(solution)/shard_map/pair_table/pallas_call | solution.py:97
  34.3 0.0 all-to-all-done
  34.3 9.9 %all-to-all-start.1 = ((f32[16,4,640]{2,1,0:T(4,128)}), f32[16,4,640]{2,1,0:T(4,128)S(1)}, u32[]{:S(2)}, u32[]{:S(2)}) async-start(f32[16,4,640]{2,1,0:T(4,128)} %bitcast.31), calls=%async_computation.1 | async-start | bytes 327680 | tf_op jit(solution)/shard_map/all_to_all | solution.py:191
  44.3 13.1 %all_gather.6 = bf16[2048,128]{1,0:T(8,128)(2,1)S(1)} all-gather(bf16[512,128]{1,0:T(8,128)(2,1)S(1)} %bitcast.32), channel_id=1, replica_groups=mesh['x'=4,'zh'=2,'c'=2,'y'=4,'zl'=8] {'x'}, dimensions={0}, use_global_device_ids=true | all-gather | bytes 655360 | tf_op jit(solution)/shard_map/all_gather | solution.py:209
  57.4 0.0 all-to-all-done.1
  57.4 0.0 copy-done
  57.4 6.1 %pair_tile.1 = (f32[4,520,128]{2,1,0:T(8,128)S(1)}, f32[1024,128]{1,0:T(8,128)S(1)}, f32[1024,128]{1,0:T(8,128)S(1)}) custom-call(bf16[4,2,8,32,128]{4,3,2,1,0:T(8,128)(2,1)S(1)} %bitcast.26, bf16[4,2,256,128]{3,2,1,0:T(8,128)(2,1)S(1)} %bitcast.25, f32[8,2,4,640]{3,2,1,0:T(4,128)S(1)} %bitcast.27), custom_call_target="tpu_custom_call" | custom-call | flops 3221225472 | bytes 2097152 | tf_op jit(solution)/shard_map/pair_tile/pallas_call | solution.py:166
  63.5 0.9 convert_element_type.10
  64.4 4.1 %all-to-all-start.2 = ((f16[4,520,128]{2,1,0:T(8,128)(2,1)}), f16[4,520,128]{2,1,0:T(8,128)(2,1)S(1)}, u32[]{:S(2)}, u32[]{:S(2)}) async-start(f16[4,520,128]{2,1,0:T(8,128)(2,1)} %convert_element_type.10), calls=%async_computation.2 | async-start | bytes 1064960 | tf_op jit(solution)/shard_map/all_to_all | solution.py:191
  68.5 1.9 %collective-permute-start = (f32[1024,128]{1,0:T(8,128)S(1)}, f32[1024,128]{1,0:T(8,128)S(1)}, u32[]{:S(2)}, u32[]{:S(2)}) collective-permute-start(f32[1024,128]{1,0:T(8,128)S(1)} %get-tuple-element.11), channel_id=1, source_target_pairs={{0,32},{32,0},{1,33},{33,1},{2,34},{34,2},{3,35},{35,3},{4,36},{36... | collective-permute-start | bytes 1572872 | tf_op jit(solution)/shard_map/ppermute | solution.py:218
  70.4 7.5 %all-to-all-done.2 = f16[4,520,128]{2,1,0:T(8,128)(2,1)S(1)} async-done(((f16[4,520,128]{2,1,0:T(8,128)(2,1)}), f16[4,520,128]{2,1,0:T(8,128)(2,1)S(1)}, u32[]{:S(2)}, u32[]{:S(2)}) %all-to-all-start.2) | async-done | bytes 532512 | tf_op jit(solution)/shard_map/all_to_all | solution.py:191
  77.9 0.1 convert_element_type.11
  78.0 0.1 fusion
  78.2 0.7 pad_maximum_fusion
  78.9 8.4 %all-to-all-start.3 = ((f16[16,40,128]{2,1,0:T(8,128)(2,1)}), f16[16,40,128]{2,1,0:T(8,128)(2,1)S(1)}, u32[]{:S(2)}, u32[]{:S(2)}) async-start(f16[16,40,128]{2,1,0:T(8,128)(2,1)} %pad_maximum_fusion), calls=%async_computation.3 | async-start | bytes 327680 | tf_op jit(solution)/shard_map/all_to_all | solution.py:191
  87.3 0.0 collective-permute-done
  87.3 0.0 copy-start.1
  87.3 0.1 add.51
  87.4 4.4 %collective-permute-start.3 = (f32[256,128]{1,0:T(8,128)S(1)}, f32[256,128]{1,0:T(8,128)S(1)}, u32[]{:S(2)}, u32[]{:S(2)}) collective-permute-start(f32[256,128]{1,0:T(8,128)S(1)} %get-tuple-element.15), channel_id=1, source_target_pairs={{0,24},{8,0},{16,8},{24,16},{1,25},{9,1},{17,9},{25,17},{2,26},{10... | collective-permute-start | bytes 393224 | tf_op jit(solution)/shard_map/ppermute | solution.py:223
  91.8 2.8 %collective-permute-start.2 = (f32[256,128]{1,0:T(8,128)S(1)}, f32[256,128]{1,0:T(8,128)S(1)}, u32[]{:S(2)}, u32[]{:S(2)}) collective-permute-start(f32[256,128]{1,0:T(8,128)S(1)} %get-tuple-element.16), channel_id=1, source_target_pairs={{0,16},{8,24},{16,0},{24,8},{1,17},{9,25},{17,1},{25,9},{2,18},{10... | collective-permute-start | bytes 393224 | tf_op jit(solution)/shard_map/ppermute | solution.py:223
  94.6 1.9 %collective-permute-start.1 = (f32[256,128]{1,0:T(8,128)S(1)}, f32[256,128]{1,0:T(8,128)S(1)}, u32[]{:S(2)}, u32[]{:S(2)}) collective-permute-start(f32[256,128]{1,0:T(8,128)S(1)} %get-tuple-element.14), channel_id=1, source_target_pairs={{0,8},{8,16},{16,24},{24,0},{1,9},{9,17},{17,25},{25,1},{2,10},{10... | collective-permute-start | bytes 393224 | tf_op jit(solution)/shard_map/ppermute | solution.py:223
  96.5 0.0 copy-done.1
  96.5 0.1 compare_bitcast_fusion
  96.6 0.0 collective-permute-done.3
  96.6 3.7 %collective-permute-done.2 = f32[256,128]{1,0:T(8,128)S(1)} collective-permute-done((f32[256,128]{1,0:T(8,128)S(1)}, f32[256,128]{1,0:T(8,128)S(1)}, u32[]{:S(2)}, u32[]{:S(2)}) %collective-permute-start.2) | collective-permute-done | bytes 131104 | tf_op jit(solution)/shard_map/ppermute | solution.py:223
  100.3 2.4 %collective-permute-done.1 = f32[256,128]{1,0:T(8,128)S(1)} collective-permute-done((f32[256,128]{1,0:T(8,128)S(1)}, f32[256,128]{1,0:T(8,128)S(1)}, u32[]{:S(2)}, u32[]{:S(2)}) %collective-permute-start.1) | collective-permute-done | bytes 131104 | tf_op jit(solution)/shard_map/ppermute | solution.py:223
  102.7 0.8 fusion.4
  103.4 0.0 all-to-all-done.3
  103.5 0.6 fusion.1
  (7 shorter events, 0.2 us)
Async XLA Ops:
  2.2 32.1 %all-to-all-start = ((bf16[16,32,128]{2,1,0:T(8,128)(2,1)}), bf16[16,32,128]{2,1,0:T(8,128)(2,1)S(1)}, u32[]{:S(2)}, u32[]{:S(2)}) async-start(bf16[16,32,128]{2,1,0:T(8,128)(2,1)} %get-tuple-element.7), calls=%async_computation | async-start | bytes 262144 | tf_op jit(solution)/shard_map/all_to_all | solution.py:191
  32.3 25.1 %copy-start = (bf16[2048,128]{1,0:T(8,128)(2,1)S(1)}, bf16[2048,128]{1,0:T(8,128)(2,1)}, u32[]{:S(2)}) copy-start(bf16[2048,128]{1,0:T(8,128)(2,1)} %all_gather.7.refs_3_) | copy-start | bytes 1572868
  34.3 23.0 %all-to-all-start.1 = ((f32[16,4,640]{2,1,0:T(4,128)}), f32[16,4,640]{2,1,0:T(4,128)S(1)}, u32[]{:S(2)}, u32[]{:S(2)}) async-start(f32[16,4,640]{2,1,0:T(4,128)} %bitcast.31), calls=%async_computation.1 | async-start | bytes 327680 | tf_op jit(solution)/shard_map/all_to_all | solution.py:191
  64.4 13.5 %all-to-all-start.2 = ((f16[4,520,128]{2,1,0:T(8,128)(2,1)}), f16[4,520,128]{2,1,0:T(8,128)(2,1)S(1)}, u32[]{:S(2)}, u32[]{:S(2)}) async-start(f16[4,520,128]{2,1,0:T(8,128)(2,1)} %convert_element_type.10), calls=%async_computation.2 | async-start | bytes 1064960 | tf_op jit(solution)/shard_map/all_to_all | solution.py:191
  68.5 18.8 %collective-permute-start = (f32[1024,128]{1,0:T(8,128)S(1)}, f32[1024,128]{1,0:T(8,128)S(1)}, u32[]{:S(2)}, u32[]{:S(2)}) collective-permute-start(f32[1024,128]{1,0:T(8,128)S(1)} %get-tuple-element.11), channel_id=1, source_target_pairs={{0,32},{32,0},{1,33},{33,1},{2,34},{34,2},{3,35},{35,3},{4,36},{36... | collective-permute-start | bytes 1572872 | tf_op jit(solution)/shard_map/ppermute | solution.py:218
  78.9 24.5 %all-to-all-start.3 = ((f16[16,40,128]{2,1,0:T(8,128)(2,1)}), f16[16,40,128]{2,1,0:T(8,128)(2,1)S(1)}, u32[]{:S(2)}, u32[]{:S(2)}) async-start(f16[16,40,128]{2,1,0:T(8,128)(2,1)} %pad_maximum_fusion), calls=%async_computation.3 | async-start | bytes 327680 | tf_op jit(solution)/shard_map/all_to_all | solution.py:191
  87.3 9.2 %copy-start.1 = (s32[2]{0:T(128)S(1)}, s32[2]{0:T(128)}, u32[]{:S(2)}) copy-start(s32[2]{0:T(128)} %lengths_ref.1) | copy-start | bytes 28
  87.4 9.2 %collective-permute-start.3 = (f32[256,128]{1,0:T(8,128)S(1)}, f32[256,128]{1,0:T(8,128)S(1)}, u32[]{:S(2)}, u32[]{:S(2)}) collective-permute-start(f32[256,128]{1,0:T(8,128)S(1)} %get-tuple-element.15), channel_id=1, source_target_pairs={{0,24},{8,0},{16,8},{24,16},{1,25},{9,1},{17,9},{25,17},{2,26},{10... | collective-permute-start | bytes 393224 | tf_op jit(solution)/shard_map/ppermute | solution.py:223
  91.8 8.5 %collective-permute-start.2 = (f32[256,128]{1,0:T(8,128)S(1)}, f32[256,128]{1,0:T(8,128)S(1)}, u32[]{:S(2)}, u32[]{:S(2)}) collective-permute-start(f32[256,128]{1,0:T(8,128)S(1)} %get-tuple-element.16), channel_id=1, source_target_pairs={{0,16},{8,24},{16,0},{24,8},{1,17},{9,25},{17,1},{25,9},{2,18},{10... | collective-permute-start | bytes 393224 | tf_op jit(solution)/shard_map/ppermute | solution.py:223
  94.6 8.1 %collective-permute-start.1 = (f32[256,128]{1,0:T(8,128)S(1)}, f32[256,128]{1,0:T(8,128)S(1)}, u32[]{:S(2)}, u32[]{:S(2)}) collective-permute-start(f32[256,128]{1,0:T(8,128)S(1)} %get-tuple-element.14), channel_id=1, source_target_pairs={{0,8},{8,16},{16,24},{24,0},{1,9},{9,17},{17,25},{25,1},{2,10},{10... | collective-permute-start | bytes 393224 | tf_op jit(solution)/shard_map/ppermute | solution.py:223
